TPU v7x, 512 devices: a whole 4x8x8 slice. The times are simulated.
512 devices in a mesh: gx: 4 (over x), gy: 8 (over y_lo, core), gz: 16 (over y_hi, z).
Axes of the slice: x: 4, y: 8 (y_hi: 2, y_lo: 4; y = y_hi * 4 + y_lo), z: 8, core: 2. Of those that a mesh axis runs over, the one named last changes fastest.
Arguments:
- coarse_state: float32 [4, 32, 64, 2048], P(None, 'gx', 'gy', 'gz'), may hold values from -6 to 6
- diffusion_number: float32 [32, 64, 2048], P('gx', 'gy', 'gz'), may hold values from 0.01 to 0.15
- route_cell: int32 [4, 8, 16, 16], P('gx', 'gy', 'gz'), may hold values from -1 to 127, as said below
- fine_state: float32 [4, 8, 16, 16, 4, 4096], P('gx', 'gy', 'gz'), may hold values from -6 to 6
- fine_diffusion: float32 [4, 8, 16, 16, 4096], P('gx', 'gy', 'gz'), may hold values from 0.01 to 0.15
Outputs:
- coarse_next: float32 [4, 32, 64, 2048], P(None, 'gx', 'gy', 'gz')
- fine_next: float32 [4, 8, 16, 16, 4, 4096], P('gx', 'gy', 'gz')
Inputs may be any that keep to these rules, and one draw needn't show every extreme that they name: `route_cell`: entry [a, b, s, h] is -1 where the source device (a, b, s) places no patch on host h of its gz line, else the index of the patch's block of 4^3 coarse cells among the source's (2) (2) (32) blocks, numbered with the third dimension fastest. The blocks named by one source are distinct.
All inputs are finite; a program needn't handle non-finite values.
Results may differ from a plain program's by a relative error of at most 0.000071.
Values sent between devices are 32-bit elements; how exact they have to be, the bound alone decides.
No kernel may reach another device: no remote copies, remote signals or barrier semaphores. Data moves between devices by JAX's collectives and lax.ppermute only.
A program may use at most 64 MiB of HBM per device.

v0:
```python
import functools
import math

import jax
import jax.numpy as jnp
import numpy as np
from jax import lax
from jax.experimental import pallas as pl
from jax.experimental.pallas import tpu as pltpu
from jax.sharding import PartitionSpec as P

PB = 4
RATIO = 4
EDGE = PB * RATIO
HOSTS = 16
SLOT_ROWS = 40
WIND_COARSE = (0.05, 0.03, 0.07)
WIND_FINE = tuple(RATIO * speed for speed in WIND_COARSE)
F32 = jnp.float32
BF16 = jnp.bfloat16


def interp_table(coarse_count, ratio):
    fine_total = coarse_count * ratio + 4
    weights_table = np.zeros((fine_total, coarse_count + 4), np.float32)
    for fine_index in range(fine_total):
        position = (fine_index - 1.5) / ratio + 2.0
        first_node = math.floor(position - 0.5) - 1
        for offset in range(4):
            weight = 1.0
            for other_node in range(4):
                if other_node != offset:
                    weight = (
                        weight
                        * (position - (first_node + other_node + 0.5))
                        / (offset - other_node)
                    )
            weights_table[fine_index, first_node + offset] = weight
    return weights_table


def high_low(table):
    high = np.asarray(table, np.float32).astype(jnp.bfloat16)
    low = (np.asarray(table, np.float64) - high.astype(np.float64)).astype(jnp.bfloat16)
    return high, low


def tables():
    interp = interp_table(PB, RATIO).astype(np.float64)
    span = EDGE + 4
    lap = np.zeros((span, span, EDGE * EDGE))
    adv = np.zeros((span, span, EDGE * EDGE))
    for y in range(EDGE):
        for z in range(EDGE):
            col = y * EDGE + z
            lap[y + 2, z + 2, col] = -6.0
            for dy, dz, wind in ((1, 0, WIND_FINE[1]), (0, 1, WIND_FINE[2])):
                for sign in (1, -1):
                    lap[y + 2 + sign * dy, z + 2 + sign * dz, col] += 1.0
                    adv[y + 2 + sign * dy, z + 2 + sign * dz, col] += sign * 8.0 * wind / 12.0
                    adv[y + 2 + sign * 2 * dy, z + 2 + sign * 2 * dz, col] -= sign * wind / 12.0
    inner = np.zeros((span, span), bool)
    inner[2:-2, 2:-2] = True
    inner = inner.reshape(-1)
    both = np.concatenate([lap.reshape(span * span, -1), adv.reshape(span * span, -1)], axis=1)
    plane_hi, plane_lo = high_low(both[inner])
    plane = np.concatenate([plane_hi, plane_hi], axis=0)
    plane_rest = plane_lo[:, EDGE * EDGE :]
    spread = np.kron(interp, interp)
    ghost_hi, ghost_lo = high_low(spread.T @ np.where(inner[:, None], 0.0, both))
    ghost = np.concatenate([ghost_hi, ghost_lo, ghost_hi, np.zeros_like(ghost_hi)], axis=0)
    face_hi, face_lo = high_low(spread[inner].T)
    face = np.concatenate([face_hi, face_lo, face_hi, np.zeros_like(face_hi)], axis=0)
    mean = np.zeros((PB, EDGE, EDGE, PB, 4, PB, PB), np.float32)
    for big_x in range(PB):
        for y in range(EDGE):
            for z in range(EDGE):
                mean[big_x, y, z, z // RATIO, :, big_x, y // RATIO] = 1.0 / RATIO**3
    mean = mean.reshape(PB * EDGE * EDGE, 256).astype(jnp.bfloat16)
    copy = np.zeros((4, 2, PB, 2, PB, 2, 4, PB, PB), np.float32)
    for q in range(4):
        for big_x in range(PB):
            for big_y in range(PB):
                copy[q, :, big_x, :, big_y, 0, q, big_x, big_y] = 1.0
    copy = copy.reshape(256, 128).astype(jnp.bfloat16)
    return plane, plane_rest, ghost, face, mean, copy


def dot(left, right):
    return lax.dot_general(
        left, right, (((1,), (0,)), ((), ())), preferred_element_type=F32
    )


def dot_t(left, right):
    return lax.dot_general(
        left, right, (((1,), (1,)), ((), ())), preferred_element_type=F32
    )


def split(values):
    high = values.astype(BF16)
    return high, (values - high.astype(F32)).astype(BF16)


def ring_field(coarse_ref, number_ref, left_ref, right_ref, q, x):
    if x < 8:
        return coarse_ref[q, x] if q < 4 else number_ref[x]
    return right_ref[q, x - 8] if x < 12 else left_ref[q, x - 12]


def y_kernel(coarse_ref, number_ref, left_ref, right_ref, low_ref, high_ref):
    top = lax.broadcasted_iota(jnp.int32, (8, 128), 0) < 4
    field = functools.partial(ring_field, coarse_ref, number_ref, left_ref, right_ref)
    for q in range(5):
        for pair in range(8):
            even, odd = field(q, 2 * pair), field(q, 2 * pair + 1)
            at = pl.ds((q * 8 + pair) * 8, 8)
            low_ref[at] = jnp.where(top, even, pltpu.roll(odd, 4, 0))
            high_ref[at] = jnp.where(top, pltpu.roll(even, 4, 0), odd)


def z_kernel(
    coarse_ref, number_ref, left_ref, right_ref, below_ref, above_ref, all_ref, low_ref, high_ref
):
    top = lax.broadcasted_iota(jnp.int32, (8, 128), 0) < 4
    field = functools.partial(ring_field, coarse_ref, number_ref, left_ref, right_ref)
    for q in range(5):
        for pair in range(8):
            at = pl.ds((q * 8 + pair) * 8, 8)
            below, above = below_ref[at], above_ref[at]
            row = (q * 16 + 2 * pair) * 16
            all_ref[pl.ds(row, 8)] = field(q, 2 * pair)
            all_ref[pl.ds(row + 8, 8)] = jnp.where(top, above, pltpu.roll(below, 4, 0))
            all_ref[pl.ds(row + 16, 8)] = field(q, 2 * pair + 1)
            all_ref[pl.ds(row + 24, 8)] = jnp.where(top, pltpu.roll(above, 4, 0), below)
    group = lax.broadcasted_iota(jnp.int32, (40, 128), 1) // 4
    low = jnp.zeros((40, 128), F32)
    high = jnp.zeros((40, 128), F32)
    for g in range(32):
        rows = all_ref[pl.ds(g * 40, 40)]
        low = jnp.where(group == g, pltpu.roll(rows, 4 * g, 1) if g else rows, low)
        shift = (4 * g + 4) % 128
        high = jnp.where(group == g, pltpu.roll(rows, shift, 1) if shift else rows, high)
    low_ref[...] = low
    high_ref[...] = high


def slot_lanes(route_ref, width, shape):
    lane = lax.broadcasted_iota(jnp.int32, shape, 1)
    group = (lane // width) % HOSTS
    values = jnp.zeros(shape, jnp.int32)
    for slot in range(HOSTS):
        values = jnp.where(group == slot, route_ref[slot], values)
    return values


def rate_parts(center, x_near, x_far, y_axis, wind):
    rows, lanes = center.shape
    y_up, y_down = pltpu.roll(center, rows - 1, y_axis), pltpu.roll(center, 1, y_axis)
    y_up2, y_down2 = pltpu.roll(center, rows - 2, y_axis), pltpu.roll(center, 2, y_axis)
    z_up, z_down = pltpu.roll(center, lanes - 1, 1), pltpu.roll(center, 1, 1)
    z_up2, z_down2 = pltpu.roll(center, lanes - 2, 1), pltpu.roll(center, 2, 1)
    laplace = (
        (x_near[0] + x_near[1]) + (y_up + y_down) + (z_up + z_down) - 6.0 * center
    )
    advect = (
        (wind[0] / 12.0) * (8.0 * (x_near[0] - x_near[1]) - (x_far[0] - x_far[1]))
        + (wind[1] / 12.0) * (8.0 * (y_up - y_down) - (y_up2 - y_down2))
        + (wind[2] / 12.0) * (8.0 * (z_up - z_down) - (z_up2 - z_down2))
    )
    return laplace, advect


HALF_PLACES = tuple(range(10)) + (14, 15)
WINDOW_PLACES = (14, 15) + tuple(range(10))


def half_kernel(all_ref, before_ref, after_ref, route_ref, pay_ref, half_ref, now_ref, cut_ref):
    lane40 = lax.broadcasted_iota(jnp.int32, (40, 128), 1)
    before, after = before_ref[...], after_ref[...]
    for g in range(32):
        ahead = pltpu.roll(after, (128 - 4 * g) % 128, 1) if g else after
        shift = (124 - 4 * g) % 128
        behind = pltpu.roll(before, shift, 1) if shift else before
        rows = pl.ds(g * 40, 40)
        now_ref[rows, pl.ds(0, 128)] = all_ref[rows]
        now_ref[rows, pl.ds(128, 128)] = jnp.where(
            lane40 < 4, ahead, jnp.where(lane40 >= 124, behind, 0.0)
        )

    def sheet(q, x):
        return now_ref[pl.ds((q * 16 + x) * 16, 16)]

    for x in HALF_PLACES:
        number = sheet(4, x)
        for q in range(4):
            center = sheet(q, x)
            near = (sheet(q, (x + 1) % 16), sheet(q, (x - 1) % 16))
            far = (sheet(q, (x + 2) % 16), sheet(q, (x - 2) % 16))
            laplace, advect = rate_parts(center, near, far, 0, WIND_COARSE)
            stepped = center + number * laplace - advect
            half_ref[pl.ds((q * 16 + x) * 16, 16)] = jnp.where(number > 0.0, stepped, 0.0)

    cells = slot_lanes(route_ref, 8, (8, 128))[0:1]
    lane = lax.broadcasted_iota(jnp.int32, (1, 128), 1)
    wanted = (4 * (cells & 31) - 2 + (lane & 7)) & 255
    place = lax.broadcasted_iota(jnp.int32, (256, 128), 0)
    pick = jnp.where((place == wanted) & (cells >= 0), 1.0, 0.0).astype(BF16)
    far_x = jnp.broadcast_to(((cells >> 6) & 1) == 1, (16, 128))
    far_y = jnp.broadcast_to(((cells >> 5) & 1) == 1, (8, 128))
    for t, field_ref in enumerate((now_ref, half_ref)):
        for q in range(4):
            cut = []
            for first, count in ((14, 2), (0, 10)):
                high, low = split(field_ref[pl.ds((q * 16 + first) * 16, count * 16)])
                cut.append(dot(high, pick) + dot(low, pick))
            cut = jnp.concatenate(cut, axis=0)
            for i in range(8):
                rows = jnp.where(
                    far_x, cut[(i + 4) * 16 : (i + 5) * 16], cut[i * 16 : (i + 1) * 16]
                )
                near_rows = pltpu.roll(rows, 2, 0)[:8]
                far_rows = pltpu.roll(rows, 14, 0)[:8]
                cut_ref[pl.ds(((t * 4 + q) * 8 + i) * 8, 8)] = jnp.where(
                    far_y, far_rows, near_rows
                )
    group = lax.broadcasted_iota(jnp.int32, (32, 128), 1) // 8
    pieces = [
        cut_ref[pl.ds(t * 256 + y, 32, stride=8)] for t in range(2) for y in range(8)
    ]
    for step in (8, 4, 2, 1):
        swap = (group & step) != 0
        for i in range(16):
            if not i & step:
                a, b = pieces[i], pieces[i + step]
                pieces[i] = jnp.where(swap, pltpu.roll(b, 8 * step, 1), a)
                pieces[i + step] = jnp.where(swap, b, pltpu.roll(a, 128 - 8 * step, 1))
    for slot in range(HOSTS):
        pay_ref[pl.ds(slot * SLOT_ROWS, 32)] = pieces[slot]
        placed = jnp.where(route_ref[slot] >= 0, 1.0, 0.0)
        pay_ref[pl.ds(slot * SLOT_ROWS + 32, 8)] = jnp.full((8, 128), placed, F32)


def full_kernel(coarse_ref, number_ref, half_ref, route_ref, full_ref):
    lane = lax.broadcasted_iota(jnp.int32, (8, 128), 1)
    top = lax.broadcasted_iota(jnp.int32, (8, 128), 0) < 4
    covered = [jnp.zeros((8, 128), jnp.int32) for _ in range(4)]
    for slot in range(HOSTS):
        cell = route_ref[slot]
        hit = (lane // 4) == (cell & 31)
        for corner in range(4):
            chosen = jnp.where((cell >> 5) == corner, 1, 0)
            covered[corner] = jnp.where(hit, jnp.maximum(covered[corner], chosen), covered[corner])

    def sheet(q, x):
        return half_ref[pl.ds((q * 16 + x % 16) * 16, 16)]

    for x in range(8):
        keep = jnp.where(top, covered[(x // 4) * 2], covered[(x // 4) * 2 + 1]) == 0
        number = number_ref[x]
        for q in range(4):
            center = sheet(q, x)
            laplace, advect = rate_parts(
                center,
                (sheet(q, x + 1), sheet(q, x - 1)),
                (sheet(q, x + 2), sheet(q, x - 2)),
                0,
                WIND_COARSE,
            )
            done = 0.5 * (
                coarse_ref[q, x]
                + center[:8, :128]
                + number * laplace[:8, :128]
                - advect[:8, :128]
            )
            full_ref[q, x] = jnp.where(keep, done, 0.0)


def put_kernel(back_ref, full_ref, route_ref, copy_ref, next_ref):
    even = back_ref[pl.ds(0, 16, stride=2)]
    odd = back_ref[pl.ds(1, 16, stride=2)]
    values = jnp.concatenate(
        [even, pltpu.roll(even, 64, 1), odd, pltpu.roll(odd, 64, 1)], axis=0
    )
    high = values.astype(BF16)
    rest = values - high.astype(F32)
    low, lowest = split(rest)
    parts = jnp.concatenate([high, low, lowest, jnp.zeros_like(high)], axis=0)
    spread = dot_t(copy_ref[...], parts)
    cells = slot_lanes(route_ref, 1, (8, 256))[0:1]
    row = lax.broadcasted_iota(jnp.int32, (256, 1), 0)
    corner = ((row >> 5) & 1) * 2 + ((row >> 2) & 1)
    spread = jnp.where((cells >> 5) == corner, spread, 0.0).astype(BF16)
    z = lax.broadcasted_iota(jnp.int32, (128, 256), 0)
    lane = lax.broadcasted_iota(jnp.int32, (128, 256), 1)
    here = ((z >> 2) == (cells & 31)) & ((z & 3) == ((lane >> 4) & 3)) & (cells >= 0)
    added = dot_t(spread, jnp.where(here, 1.0, 0.0).astype(BF16))
    for q in range(4):
        for x in range(8):
            at = (q * 8 + x) * 8
            next_ref[q, x] = full_ref[q, x] + added[at : at + 8]


def plane_parts(field, plane_ref, rest_ref):
    high, low = split(field)
    both = dot(high, plane_ref[pl.ds(0, 256)]) + dot(low, plane_ref[pl.ds(256, 256)])
    return both[:, :256], both[:, 256:] + dot(high, rest_ref[...])


def x_parts(padded):
    laplace, advect = [], []
    for x in range(2, 18):
        laplace.append(padded[x + 1] + padded[x - 1])
        advect.append(
            (WIND_FINE[0] / 12.0)
            * (8.0 * (padded[x + 1] - padded[x - 1]) - (padded[x + 2] - padded[x - 2]))
        )
    return jnp.concatenate(laplace, axis=0), jnp.concatenate(advect, axis=0)


def load_numbers(number_ref):
    return jnp.concatenate(
        [number_ref[:, pl.ds(x * 256, 256)] for x in range(EDGE)], axis=0
    )


def early_kernel(fine_ref, number_ref, plane_ref, rest_ref, step_ref, field_ref):
    zero = jnp.zeros((HOSTS, 256), F32)
    numbers = load_numbers(number_ref)
    for q in range(4):
        planes = []
        for x in range(EDGE):
            sides = [
                fine_ref[pl.ds((2 * x + side) * 4 + q, HOSTS, stride=128)] for side in range(2)
            ]
            planes.append(jnp.concatenate(sides, axis=1))
        field = jnp.concatenate(planes, axis=0)
        laplace, advect = plane_parts(field, plane_ref, rest_ref)
        x_laplace, x_advect = x_parts([zero, zero] + planes + [zero, zero])
        at = pl.ds(q * 256, 256)
        field_ref[at] = field
        step_ref[at] = field + numbers * (laplace + x_laplace) - (advect + x_advect)


def late_kernel(
    block_ref,
    step_ref,
    field_ref,
    number_ref,
    plane_ref,
    rest_ref,
    ghost_ref,
    face_ref,
    mean_ref,
    fine_ref,
    back_ref,
):
    interp = interp_table(PB, RATIO)
    zero = jnp.zeros((HOSTS, 256), F32)
    numbers = load_numbers(number_ref)
    first_half = lax.broadcasted_iota(jnp.int32, (HOSTS, 128), 1) < 64
    placed = block_ref[pl.ds(32, HOSTS, stride=SLOT_ROWS)] > 0.5
    lane_q = (lax.broadcasted_iota(jnp.int32, (HOSTS, 256), 1) >> 4) & 3
    back = zero

    def ghosts(q, t):
        coarse = []
        for x in range(8):
            rows = block_ref[pl.ds(q * 8 + x, HOSTS, stride=SLOT_ROWS)]
            turned = pltpu.roll(rows, 64, 1)
            coarse.append(
                jnp.where(first_half, rows, turned) if t == 0 else jnp.where(first_half, turned, rows)
            )
        inner, outer = [], []
        for i in range(EDGE + 4):
            total = None
            for j in range(8):
                if interp[i, j] != 0.0:
                    term = float(interp[i, j]) * coarse[j]
                    total = term if total is None else total + term
            (inner if 2 <= i < EDGE + 2 else outer).append(total)
        inner = jnp.concatenate(inner, axis=0)
        outer = jnp.concatenate(outer, axis=0)
        sides = dot(jnp.concatenate(split(inner), axis=1), ghost_ref[...])
        faces = dot(jnp.concatenate(split(outer), axis=1), face_ref[...])
        return sides[:, :256], sides[:, 256:], [faces[i * 16 : (i + 1) * 16] for i in range(4)]

    for q in range(4):
        at = pl.ds(q * 256, 256)
        side_laplace, side_advect, faces = ghosts(q, 0)
        x_laplace, x_advect = x_parts(faces[:2] + [zero] * EDGE + faces[2:])
        half = step_ref[at] + numbers * (side_laplace + x_laplace) - (side_advect + x_advect)
        side_laplace, side_advect, faces = ghosts(q, 1)
        planes = [half[x * 16 : (x + 1) * 16] for x in range(EDGE)]
        x_laplace, x_advect = x_parts(faces[:2] + planes + faces[2:])
        laplace, advect = plane_parts(half, plane_ref, rest_ref)
        field = field_ref[at]
        done = 0.5 * (
            field
            + half
            + numbers * (laplace + side_laplace + x_laplace)
            - (advect + side_advect + x_advect)
        )
        sums = []
        for x in range(EDGE):
            rows = slice(x * 16, (x + 1) * 16)
            for side in range(2):
                lanes = slice(side * 128, side * 128 + 128)
                fine_ref[pl.ds((2 * x + side) * 4 + q, HOSTS, stride=128)] = jnp.where(
                    placed, done[rows, lanes], field[rows, lanes]
                )
        total = zero
        for big_x in range(PB):
            group = [done[(big_x * 4 + i) * 16 : (big_x * 4 + i + 1) * 16] for i in range(4)]
            sums.append((group[0] + group[1]) + (group[2] + group[3]))
        for big_x in range(PB):
            high, low = split(sums[big_x])
            weights = mean_ref[pl.ds(big_x * 256, 256)]
            total = total + dot(high, weights) + dot(low, weights)
        back = jnp.where(lane_q == q, total, back)
    back_ref[pl.ds(0, HOSTS, stride=2)] = back[:, :128]
    back_ref[pl.ds(1, HOSTS, stride=2)] = back[:, 128:]


def call(kernel, operands, outs, smem=(), scratch=(), flops=1000000, name=None):
    vmem = pl.BlockSpec(memory_space=pltpu.VMEM)
    scalar = pl.BlockSpec(memory_space=pltpu.SMEM)
    moved = sum(int(np.prod(o.shape)) * o.dtype.itemsize for o in operands)
    return pl.pallas_call(
        kernel,
        out_shape=tuple(jax.ShapeDtypeStruct(shape, F32) for shape in outs),
        in_specs=[scalar if i in smem else vmem for i in range(len(operands))],
        out_specs=tuple(vmem for _ in outs),
        scratch_shapes=[pltpu.VMEM(shape, F32) for shape in scratch],
        compiler_params=pltpu.CompilerParams(vmem_limit_bytes=40 * 1024 * 1024),
        cost_estimate=pl.CostEstimate(flops=flops, bytes_accessed=moved, transcendentals=0),
        name=name,
    )(*operands)


def shards(coarse_state, diffusion_number, route_cell, fine_state, fine_diffusion):
    plane, plane_rest, ghost, face, mean, copy = (jnp.asarray(table) for table in tables())
    route = route_cell.reshape(HOSTS)

    def exchange(low, high, axis):
        count = lax.axis_size(axis)
        up = [(i, i + 1) for i in range(count - 1)]
        down = [(i + 1, i) for i in range(count - 1)]
        return lax.ppermute(high, axis, up), lax.ppermute(low, axis, down)

    fields = jnp.concatenate([coarse_state, diffusion_number[None]], axis=0)
    left, right = exchange(fields[:, :4], fields[:, 4:], "gx")
    own = (coarse_state, diffusion_number, left, right)
    low, high = call(y_kernel, own, [(320, 128), (320, 128)], name="y_messages")
    below, above = exchange(low, high, "gy")
    everything, low, high = call(
        z_kernel, own + (below, above), [(1280, 128), (40, 128), (40, 128)], name="z_messages"
    )
    before, after = exchange(low, high, "gz")
    pay, half = call(
        half_kernel,
        (everything, before, after, route),
        [(HOSTS * SLOT_ROWS, 128), (1024, 256)],
        smem=(3,),
        scratch=[(1280, 256), (512, 128)],
        name="half_step",
    )
    fine_rows = fine_state.reshape(HOSTS, 4, 32, 128).transpose(0, 2, 1, 3).reshape(2048, 128)
    fine_numbers = fine_diffusion.reshape(HOSTS, EDGE**3)
    step, field = call(
        early_kernel,
        (fine_rows, fine_numbers, plane, plane_rest),
        [(1024, 256), (1024, 256)],
        flops=10**9,
        name="fine_early",
    )
    blocks = lax.all_to_all(
        pay.reshape(HOSTS, SLOT_ROWS, 128), "gz", split_axis=0, concat_axis=0, tiled=True
    ).reshape(HOSTS * SLOT_ROWS, 128)
    (full,) = call(
        full_kernel,
        (coarse_state, diffusion_number, half, route),
        [(4, 8, 8, 128)],
        smem=(3,),
        name="coarse_full",
    )
    fine_done, back = call(
        late_kernel,
        (blocks, step, field, fine_numbers, plane, plane_rest, ghost, face, mean),
        [(2048, 128), (32, 128)],
        flops=10**9,
        name="fine_late",
    )
    returned = lax.all_to_all(
        back.reshape(HOSTS, 2, 128), "gz", split_axis=0, concat_axis=0, tiled=True
    ).reshape(32, 128)
    (coarse_next,) = call(
        put_kernel,
        (returned, full, route, copy),
        [(4, 8, 8, 128)],
        smem=(2,),
        name="put_means",
    )
    fine_next = (
        fine_done.reshape(HOSTS, 32, 4, 128).transpose(0, 2, 1, 3).reshape(fine_state.shape)
    )
    return coarse_next, fine_next


def solution(mesh):
    return jax.shard_map(
        shards,
        mesh=mesh,
        in_specs=(
            P(None, "gx", "gy", "gz"),
            P("gx", "gy", "gz"),
            P("gx", "gy", "gz", None),
            P("gx", "gy", "gz", None, None, None),
            P("gx", "gy", "gz", None, None),
        ),
        out_specs=(P(None, "gx", "gy", "gz"), P("gx", "gy", "gz", None, None, None)),
        check_vma=False,
    )
```

profile of v0, /device:TPU:22, one launch (start us, length us, event | category | flops | bytes accessed | tf_op | source)
XLA Modules:
  0.0 91.4 jit_solution(6975010703687894184)
XLA Ops:
  0.6 0.0 copy-start
  0.6 0.0 copy-start.3
  0.6 1.0 %pad_maximum_fusion = (f32[5,4,8,128]{3,2,1,0:T(8,128)S(1)}, f32[5,4,8,128]{3,2,1,0:T(8,128)S(1)}) fusion(f32[1,8,8,128]{3,2,1,0:T(8,128)} %bitcast.18, f32[4,8,8,128]{3,2,1,0:T(8,128)} %coarse_ref.5), kind=kLoop, calls=%fused_computation.3 | loop fusion | flops 40960 | bytes 327680 | tf_op jit(solution)/shard_map/concatenate | solution.py:452
  1.6 2.7 %collective-permute-start.1 = (f32[5,4,8,128]{3,2,1,0:T(8,128)S(1)}, f32[5,4,8,128]{3,2,1,0:T(8,128)S(1)}, u32[]{:S(2)}, u32[]{:S(2)}) collective-permute-start(f32[5,4,8,128]{3,2,1,0:T(8,128)S(1)} %get-tuple-element.24), channel_id=1, source_target_pairs={{128,0},{256,128},{384,256},{129,1},{257,129},{385,257},{130,2},{2... | collective-permute-start | bytes 245768 | tf_op jit(solution)/shard_map/ppermute | solution.py:450
  4.4 1.3 %collective-permute-start = (f32[5,4,8,128]{3,2,1,0:T(8,128)S(1)}, f32[5,4,8,128]{3,2,1,0:T(8,128)S(1)}, u32[]{:S(2)}, u32[]{:S(2)}) collective-permute-start(f32[5,4,8,128]{3,2,1,0:T(8,128)S(1)} %get-tuple-element.25), channel_id=1, source_target_pairs={{0,128},{128,256},{256,384},{1,129},{129,257},{257,385},{2,130},{1... | collective-permute-start | bytes 245768 | tf_op jit(solution)/shard_map/ppermute | solution.py:450
  5.7 0.7 collective-permute-done.1.right_ref
  6.4 4.3 %collective-permute-done.left_ref = f32[5,4,8,128]{3,2,1,0:T(8,128)S(1)} collective-permute-done((f32[5,4,8,128]{3,2,1,0:T(8,128)S(1)}, f32[5,4,8,128]{3,2,1,0:T(8,128)S(1)}, u32[]{:S(2)}, u32[]{:S(2)}) %collective-permute-start) | collective-permute-done | bytes 81952 | tf_op jit(solution)/shard_map/ppermute | solution.py:450
  10.7 0.0 copy-done
  10.7 0.0 copy-done.3
  10.7 1.9 %collective-permute-start.2 = (f32[320,128]{1,0:T(8,128)S(1)}, f32[320,128]{1,0:T(8,128)S(1)}, u32[]{:S(2)}, u32[]{:S(2)}) collective-permute-start(f32[320,128]{1,0:T(8,128)S(1)} %get-tuple-element.13), channel_id=1, source_target_pairs={{0,16},{16,32},{32,48},{48,64},{64,80},{80,96},{96,112},{1,17},{17... | collective-permute-start | bytes 491528 | tf_op jit(solution)/shard_map/ppermute | solution.py:450
  12.7 3.6 %collective-permute-start.3 = (f32[320,128]{1,0:T(8,128)S(1)}, f32[320,128]{1,0:T(8,128)S(1)}, u32[]{:S(2)}, u32[]{:S(2)}) collective-permute-start(f32[320,128]{1,0:T(8,128)S(1)} %get-tuple-element.14), channel_id=1, source_target_pairs={{16,0},{32,16},{48,32},{64,48},{80,64},{96,80},{112,96},{17,1},{33... | collective-permute-start | bytes 491528 | tf_op jit(solution)/shard_map/ppermute | solution.py:450
  16.3 1.1 %collective-permute-done.2.below_ref = f32[320,128]{1,0:T(8,128)S(1)} collective-permute-done((f32[320,128]{1,0:T(8,128)S(1)}, f32[320,128]{1,0:T(8,128)S(1)}, u32[]{:S(2)}, u32[]{:S(2)}) %collective-permute-start.2) | collective-permute-done | bytes 163872 | tf_op jit(solution)/shard_map/ppermute | solution.py:450
  17.4 1.8 %collective-permute-done.3.above_ref = f32[320,128]{1,0:T(8,128)S(1)} collective-permute-done((f32[320,128]{1,0:T(8,128)S(1)}, f32[320,128]{1,0:T(8,128)S(1)}, u32[]{:S(2)}, u32[]{:S(2)}) %collective-permute-start.3) | collective-permute-done | bytes 163872 | tf_op jit(solution)/shard_map/ppermute | solution.py:450
  19.1 0.4 z_messages.1
  19.5 4.3 %collective-permute-start.4 = (f32[40,128]{1,0:T(8,128)S(1)}, f32[40,128]{1,0:T(8,128)S(1)}, u32[]{:S(2)}, u32[]{:S(2)}) collective-permute-start(f32[40,128]{1,0:T(8,128)S(1)} %get-tuple-element.16), channel_id=1, source_target_pairs={{0,1},{1,2},{2,3},{3,4},{4,5},{5,6},{6,7},{7,8},{8,9},{9,10},{10,1... | collective-permute-start | bytes 61448 | tf_op jit(solution)/shard_map/ppermute | solution.py:450
  23.8 1.3 %collective-permute-start.5 = (f32[40,128]{1,0:T(8,128)S(1)}, f32[40,128]{1,0:T(8,128)S(1)}, u32[]{:S(2)}, u32[]{:S(2)}) collective-permute-start(f32[40,128]{1,0:T(8,128)S(1)} %get-tuple-element.17), channel_id=1, source_target_pairs={{1,0},{2,1},{3,2},{4,3},{5,4},{6,5},{7,6},{8,7},{9,8},{10,9},{11,1... | collective-permute-start | bytes 61448 | tf_op jit(solution)/shard_map/ppermute | solution.py:450
  25.1 0.2 collective-permute-done.4.before_ref
  25.3 4.6 %collective-permute-done.5.after_ref = f32[40,128]{1,0:T(8,128)S(1)} collective-permute-done((f32[40,128]{1,0:T(8,128)S(1)}, f32[40,128]{1,0:T(8,128)S(1)}, u32[]{:S(2)}, u32[]{:S(2)}) %collective-permute-start.5) | collective-permute-done | bytes 20512 | tf_op jit(solution)/shard_map/ppermute | solution.py:450
  29.8 0.0 copy-start.11
  29.8 0.7 copy-done.11
  30.5 0.0 copy-start.4
  30.5 3.5 %half_step.1 = (f32[640,128]{1,0:T(8,128)}, f32[1024,256]{1,0:T(8,128)S(1)}) custom-call(f32[1280,128]{1,0:T(8,128)S(1)} %get-tuple-element.15.all_ref, f32[40,128]{1,0:T(8,128)S(1)} %collective-permute-done.4.before_ref, f32[40,128]{1,0:T(8,128)S(1)} %collective-permute-done.5.after_ref, s32[16]{0:T(128)S(1)} %bitcast.22), custom_call_target="tpu_custom_call" | custom-call | flops 1000000 | bytes 696384 | tf_op jit(solution)/shard_map/half_step/pallas_call | solution.py:430
  34.0 0.0 copy-start.6
  34.0 0.0 copy-start.8
  34.0 13.8 %all-to-all-start = ((f32[16,40,128]{2,1,0:T(8,128)}), f32[16,40,128]{2,1,0:T(8,128)S(1)}, u32[]{:S(2)}, u32[]{:S(2)}) async-start(f32[16,40,128]{2,1,0:T(8,128)} %bitcast.2), calls=%async_computation | async-start | bytes 655360 | tf_op jit(solution)/shard_map/all_to_all | solution.py:478
  47.9 0.0 copy-done.4
  47.9 0.0 copy-done.6
  47.9 0.0 copy-done.8
  47.9 0.0 copy-start.12
  47.9 1.2 %copy-done.12 = f32[1,1,1,16,4,4096]{5,4,3,2,1,0:T(4,128)S(1)} copy-done((f32[1,1,1,16,4,4096]{5,4,3,2,1,0:T(4,128)S(1)}, f32[1,1,1,16,4,4096]{5,4,3,2,1,0:T(4,128)}, u32[]{:S(2)}) %copy-start.12) | copy-done | bytes 1048600
  49.1 1.6 %fine_early.1 = (f32[1024,256]{1,0:T(8,128)S(1)}, f32[1024,256]{1,0:T(8,128)S(1)}) custom-call(f32[2048,128]{1,0:T(8,128)S(1)} %bitcast.25, f32[16,4096]{1,0:T(8,128)S(1)} %bitcast.19, bf16[512,512]{1,0:T(8,128)(2,1)S(1)} %copy-done.4, bf16[256,256]{1,0:T(8,128)(2,1)S(1)} %copy-done.8), custom_call_target="tpu_custom_call" | custom-call | flops 1000000000 | bytes 1966080 | tf_op jit(solution)/shard_map/fine_early/pallas_call | solution.py:430
  50.7 0.0 copy-start.1
  50.7 1.0 %copy-done.1 = f32[1024,256]{1,0:T(8,128)} copy-done((f32[1024,256]{1,0:T(8,128)}, f32[1024,256]{1,0:T(8,128)S(1)}, u32[]{:S(2)}) %copy-start.1) | copy-done | bytes 1048600
  51.7 12.1 %all-to-all-done = f32[16,40,128]{2,1,0:T(8,128)S(1)} async-done(((f32[16,40,128]{2,1,0:T(8,128)}), f32[16,40,128]{2,1,0:T(8,128)S(1)}, u32[]{:S(2)}, u32[]{:S(2)}) %all-to-all-start) | async-done | bytes 327712 | tf_op jit(solution)/shard_map/all_to_all | solution.py:478
  63.8 0.0 copy-start.2
  63.8 1.2 %copy-done.2 = f32[1024,256]{1,0:T(8,128)S(1)} copy-done((f32[1024,256]{1,0:T(8,128)S(1)}, f32[1024,256]{1,0:T(8,128)}, u32[]{:S(2)}) %copy-start.2) | copy-done | bytes 1048600
  65.0 0.0 copy-start.5
  65.0 1.0 %copy-done.5 = bf16[1024,256]{1,0:T(8,128)(2,1)S(1)} copy-done((bf16[1024,256]{1,0:T(8,128)(2,1)S(1)}, bf16[1024,256]{1,0:T(8,128)(2,1)}, u32[]{:S(2)}) %copy-start.5) | copy-done | bytes 524312
  66.1 0.0 copy-start.7
  66.1 0.9 %copy-done.7 = bf16[256,512]{1,0:T(8,128)(2,1)S(1)} copy-done((bf16[256,512]{1,0:T(8,128)(2,1)S(1)}, bf16[256,512]{1,0:T(8,128)(2,1)}, u32[]{:S(2)}) %copy-start.7) | copy-done | bytes 262168
  67.0 0.9 copy-done.9
  67.9 4.4 %fine_late.1 = (f32[2048,128]{1,0:T(8,128)}, f32[32,128]{1,0:T(8,128)}) custom-call(f32[640,128]{1,0:T(8,128)S(1)} %bitcast.17, f32[1024,256]{1,0:T(8,128)S(1)} %get-tuple-element.19.step_ref, f32[1024,256]{1,0:T(8,128)S(1)} %copy-done.2, f32[16,4096]{1,0:T(8,128)S(1)} %bitcast.20, bf16[512,512]{1,0:T(8,128)(2,1)S(1)} %copy-done.4, ...), custom_call_target="tpu_custom_call" | custom-call | flops 1000000000 | bytes 4259840 | tf_op jit(solution)/shard_map/fine_late/pallas_call | solution.py:430
  72.3 5.1 %all-to-all-start.1 = ((f32[16,2,128]{2,1,0:T(2,128)}), f32[16,2,128]{2,1,0:T(2,128)S(1)}, u32[]{:S(2)}, u32[]{:S(2)}) async-start(f32[16,2,128]{2,1,0:T(2,128)} %bitcast.8), calls=%async_computation.1 | async-start | bytes 32768 | tf_op jit(solution)/shard_map/all_to_all | solution.py:495
  77.4 0.0 copy-start.10
  77.4 0.9 coarse_full.1.full_ref
  78.3 11.5 %all-to-all-done.1 = f32[16,2,128]{2,1,0:T(2,128)S(1)} async-done(((f32[16,2,128]{2,1,0:T(2,128)}), f32[16,2,128]{2,1,0:T(2,128)S(1)}, u32[]{:S(2)}, u32[]{:S(2)}) %all-to-all-start.1) | async-done | bytes 16416 | tf_op jit(solution)/shard_map/all_to_all | solution.py:495
  89.8 0.0 copy-done.10
  89.8 1.6 %put_means.1 = f32[4,8,8,128]{3,2,1,0:T(8,128)} custom-call(f32[32,128]{1,0:T(8,128)S(1)} %bitcast.21, f32[4,8,8,128]{3,2,1,0:T(8,128)S(1)} %coarse_full.1.full_ref, s32[16]{0:T(128)S(1)} %bitcast.24, bf16[256,128]{1,0:T(8,128)(2,1)S(1)} %copy-done.10), custom_call_target="tpu_custom_call" | custom-call | flops 1000000 | bytes 213056 | tf_op jit(solution)/shard_map/put_means/pallas_call | solution.py:430
  (2 shorter events, 0.0 us)
Async XLA Ops:
  0.6 10.1 %copy-start = (f32[4,8,8,128]{3,2,1,0:T(8,128)S(1)}, f32[4,8,8,128]{3,2,1,0:T(8,128)}, u32[]{:S(2)}) copy-start(f32[4,8,8,128]{3,2,1,0:T(8,128)} %coarse_ref.5) | copy-start | bytes 393220
  0.6 10.1 %copy-start.3 = (f32[8,8,128]{2,1,0:T(8,128)S(1)}, f32[8,8,128]{2,1,0:T(8,128)}, u32[]{:S(2)}) copy-start(f32[8,8,128]{2,1,0:T(8,128)} %number_ref.5) | copy-start | bytes 98308
  1.6 4.8 %collective-permute-start.1 = (f32[5,4,8,128]{3,2,1,0:T(8,128)S(1)}, f32[5,4,8,128]{3,2,1,0:T(8,128)S(1)}, u32[]{:S(2)}, u32[]{:S(2)}) collective-permute-start(f32[5,4,8,128]{3,2,1,0:T(8,128)S(1)} %get-tuple-element.24), channel_id=1, source_target_pairs={{128,0},{256,128},{384,256},{129,1},{257,129},{385,257},{130,2},{2... | collective-permute-start | bytes 245768 | tf_op jit(solution)/shard_map/ppermute | solution.py:450
  4.4 6.3 %collective-permute-start = (f32[5,4,8,128]{3,2,1,0:T(8,128)S(1)}, f32[5,4,8,128]{3,2,1,0:T(8,128)S(1)}, u32[]{:S(2)}, u32[]{:S(2)}) collective-permute-start(f32[5,4,8,128]{3,2,1,0:T(8,128)S(1)} %get-tuple-element.25), channel_id=1, source_target_pairs={{0,128},{128,256},{256,384},{1,129},{129,257},{257,385},{2,130},{1... | collective-permute-start | bytes 245768 | tf_op jit(solution)/shard_map/ppermute | solution.py:450
  10.7 6.6 %collective-permute-start.2 = (f32[320,128]{1,0:T(8,128)S(1)}, f32[320,128]{1,0:T(8,128)S(1)}, u32[]{:S(2)}, u32[]{:S(2)}) collective-permute-start(f32[320,128]{1,0:T(8,128)S(1)} %get-tuple-element.13), channel_id=1, source_target_pairs={{0,16},{16,32},{32,48},{48,64},{64,80},{80,96},{96,112},{1,17},{17... | collective-permute-start | bytes 491528 | tf_op jit(solution)/shard_map/ppermute | solution.py:450
  12.7 6.5 %collective-permute-start.3 = (f32[320,128]{1,0:T(8,128)S(1)}, f32[320,128]{1,0:T(8,128)S(1)}, u32[]{:S(2)}, u32[]{:S(2)}) collective-permute-start(f32[320,128]{1,0:T(8,128)S(1)} %get-tuple-element.14), channel_id=1, source_target_pairs={{16,0},{32,16},{48,32},{64,48},{80,64},{96,80},{112,96},{17,1},{33... | collective-permute-start | bytes 491528 | tf_op jit(solution)/shard_map/ppermute | solution.py:450
  19.5 5.7 %collective-permute-start.4 = (f32[40,128]{1,0:T(8,128)S(1)}, f32[40,128]{1,0:T(8,128)S(1)}, u32[]{:S(2)}, u32[]{:S(2)}) collective-permute-start(f32[40,128]{1,0:T(8,128)S(1)} %get-tuple-element.16), channel_id=1, source_target_pairs={{0,1},{1,2},{2,3},{3,4},{4,5},{5,6},{6,7},{7,8},{8,9},{9,10},{10,1... | collective-permute-start | bytes 61448 | tf_op jit(solution)/shard_map/ppermute | solution.py:450
  23.8 6.0 %collective-permute-start.5 = (f32[40,128]{1,0:T(8,128)S(1)}, f32[40,128]{1,0:T(8,128)S(1)}, u32[]{:S(2)}, u32[]{:S(2)}) collective-permute-start(f32[40,128]{1,0:T(8,128)S(1)} %get-tuple-element.17), channel_id=1, source_target_pairs={{1,0},{2,1},{3,2},{4,3},{5,4},{6,5},{7,6},{8,7},{9,8},{10,9},{11,1... | collective-permute-start | bytes 61448 | tf_op jit(solution)/shard_map/ppermute | solution.py:450
  29.8 0.7 copy-start.11
  30.5 17.4 %copy-start.4 = (bf16[512,512]{1,0:T(8,128)(2,1)S(1)}, bf16[512,512]{1,0:T(8,128)(2,1)}, u32[]{:S(2)}) copy-start(bf16[512,512]{1,0:T(8,128)(2,1)} %constant.12.clone.plane_ref) | copy-start | bytes 1572868
  34.0 13.9 %copy-start.6 = (f32[1,1,1,16,4096]{4,3,2,1,0:T(8,128)S(1)}, f32[1,1,1,16,4096]{4,3,2,1,0:T(8,128)}, u32[]{:S(2)}) copy-start(f32[1,1,1,16,4096]{4,3,2,1,0:T(8,128)} %param.15) | copy-start | bytes 786436
  34.0 13.9 %copy-start.8 = (bf16[256,256]{1,0:T(8,128)(2,1)S(1)}, bf16[256,256]{1,0:T(8,128)(2,1)}, u32[]{:S(2)}) copy-start(bf16[256,256]{1,0:T(8,128)(2,1)} %constant.13.clone.rest_ref) | copy-start | bytes 393220
  34.0 29.8 %all-to-all-start = ((f32[16,40,128]{2,1,0:T(8,128)}), f32[16,40,128]{2,1,0:T(8,128)S(1)}, u32[]{:S(2)}, u32[]{:S(2)}) async-start(f32[16,40,128]{2,1,0:T(8,128)} %bitcast.2), calls=%async_computation | async-start | bytes 655360 | tf_op jit(solution)/shard_map/all_to_all | solution.py:478
  47.9 1.2 %copy-start.12 = (f32[1,1,1,16,4,4096]{5,4,3,2,1,0:T(4,128)S(1)}, f32[1,1,1,16,4,4096]{5,4,3,2,1,0:T(4,128)}, u32[]{:S(2)}) copy-start(f32[1,1,1,16,4,4096]{5,4,3,2,1,0:T(4,128)} %param.14) | copy-start | bytes 3145732
  50.7 1.0 %copy-start.1 = (f32[1024,256]{1,0:T(8,128)}, f32[1024,256]{1,0:T(8,128)S(1)}, u32[]{:S(2)}) copy-start(f32[1024,256]{1,0:T(8,128)S(1)} %get-tuple-element.20.field_ref) | copy-start | bytes 3145732
  63.8 1.2 %copy-start.2 = (f32[1024,256]{1,0:T(8,128)S(1)}, f32[1024,256]{1,0:T(8,128)}, u32[]{:S(2)}) copy-start(f32[1024,256]{1,0:T(8,128)} %copy-done.1) | copy-start | bytes 3145732
  65.0 1.0 %copy-start.5 = (bf16[1024,256]{1,0:T(8,128)(2,1)S(1)}, bf16[1024,256]{1,0:T(8,128)(2,1)}, u32[]{:S(2)}) copy-start(bf16[1024,256]{1,0:T(8,128)(2,1)} %constant.16.clone.mean_ref) | copy-start | bytes 1572868
  66.1 0.9 %copy-start.7 = (bf16[256,512]{1,0:T(8,128)(2,1)S(1)}, bf16[256,512]{1,0:T(8,128)(2,1)}, u32[]{:S(2)}) copy-start(bf16[256,512]{1,0:T(8,128)(2,1)} %constant.14.clone.ghost_ref) | copy-start | bytes 786436
  67.0 0.9 copy-start.9
  72.3 17.5 %all-to-all-start.1 = ((f32[16,2,128]{2,1,0:T(2,128)}), f32[16,2,128]{2,1,0:T(2,128)S(1)}, u32[]{:S(2)}, u32[]{:S(2)}) async-start(f32[16,2,128]{2,1,0:T(2,128)} %bitcast.8), calls=%async_computation.1 | async-start | bytes 32768 | tf_op jit(solution)/shard_map/all_to_all | solution.py:495
  77.4 12.4 %copy-start.10 = (bf16[256,128]{1,0:T(8,128)(2,1)S(1)}, bf16[256,128]{1,0:T(8,128)(2,1)}, u32[]{:S(2)}) copy-start(bf16[256,128]{1,0:T(8,128)(2,1)} %constant.17.clone.copy_ref) | copy-start | bytes 196612
where the time goes:
time: 92 us; the launch traced here: 91.4 us
  waiting for transfers between devices  36.2 us (39%)
  starting transfers between devices  34.1 us (37%)
  Pallas kernels  12.4 us (13%)
  local copies, waits for them, and re-layouts  6.99 us (8%)
  other arithmetic  0.95 us (1%)
    ppermute x6, starting transfers between devices, exchange(): return (lax.ppermute(high, axis, up), lax.ppermute(low, axis, down))  15.2 us
    all_to_all x1, starting transfers between devices, shards(): lax.all_to_all(pay.reshape(HOSTS, SLOT_ROWS, 128), 'gz', split_axis=0, co...  13.8 us
    ppermute x6, waiting for transfers between devices, exchange(): return (lax.ppermute(high, axis, up), lax.ppermute(low, axis, down))  12.6 us
    pallas_call x7, Pallas kernels, call(): pl.pallas_call(kernel, out_shape=tuple((jax.ShapeDtypeStruct(shape, F32)...  12.4 us
    all_to_all x1, waiting for transfers between devices, shards(): lax.all_to_all(pay.reshape(HOSTS, SLOT_ROWS, 128), 'gz', split_axis=0, co...  12.1 us
    all_to_all x1, waiting for transfers between devices, shards(): lax.all_to_all(back.reshape(HOSTS, 2, 128), 'gz', split_axis=0, concat_ax...  11.5 us
    unnamed x26, local copies, waits for them, and re-layouts  6.99 us
    all_to_all x1, starting transfers between devices, shards(): lax.all_to_all(back.reshape(HOSTS, 2, 128), 'gz', split_axis=0, concat_ax...  5.1 us
  transfers between devices with their start and end apart: 8, of which 8 were waited for; matrix products, arithmetic and copies ran while one was open for 0% of the time, Pallas kernels for 3%

commit v1 on v0

--- a/solution.py
+++ b/solution.py
@@ -13,7 +13,11 @@
 RATIO = 4
 EDGE = PB * RATIO
 HOSTS = 16
-SLOT_ROWS = 40
+LIMIT = 16
+NUMBER_ROW = 32
+MEAN_ROW = 64
+FLAG_ROW = 66
+SLOT_ROWS = 67
 WIND_COARSE = (0.05, 0.03, 0.07)
 WIND_FINE = tuple(RATIO * speed for speed in WIND_COARSE)
 F32 = jnp.float32
@@ -146,15 +150,6 @@
     high_ref[...] = high
 
 
-def slot_lanes(route_ref, width, shape):
-    lane = lax.broadcasted_iota(jnp.int32, shape, 1)
-    group = (lane // width) % HOSTS
-    values = jnp.zeros(shape, jnp.int32)
-    for slot in range(HOSTS):
-        values = jnp.where(group == slot, route_ref[slot], values)
-    return values
-
-
 def rate_parts(center, x_near, x_far, y_axis, wind):
     rows, lanes = center.shape
     y_up, y_down = pltpu.roll(center, rows - 1, y_axis), pltpu.roll(center, 1, y_axis)
@@ -176,7 +171,9 @@
 WINDOW_PLACES = (14, 15) + tuple(range(10))
 
 
-def half_kernel(all_ref, before_ref, after_ref, route_ref, pay_ref, half_ref, now_ref, cut_ref):
+def half_kernel(
+    all_ref, before_ref, after_ref, cells_ref, number_ref, mean_ref, pay_ref, half_ref, now_ref, cut_ref
+):
     lane40 = lax.broadcasted_iota(jnp.int32, (40, 128), 1)
     before, after = before_ref[...], after_ref[...]
     for g in range(32):
@@ -202,7 +199,7 @@
             stepped = center + number * laplace - advect
             half_ref[pl.ds((q * 16 + x) * 16, 16)] = jnp.where(number > 0.0, stepped, 0.0)
 
-    cells = slot_lanes(route_ref, 8, (8, 128))[0:1]
+    cells = cells_ref[pl.ds(0, 1), pl.ds(0, 128)]
     lane = lax.broadcasted_iota(jnp.int32, (1, 128), 1)
     wanted = (4 * (cells & 31) - 2 + (lane & 7)) & 255
     place = lax.broadcasted_iota(jnp.int32, (256, 128), 0)
@@ -238,20 +235,27 @@
                 pieces[i + step] = jnp.where(swap, b, pltpu.roll(a, 128 - 8 * step, 1))
     for slot in range(HOSTS):
         pay_ref[pl.ds(slot * SLOT_ROWS, 32)] = pieces[slot]
-        placed = jnp.where(route_ref[slot] >= 0, 1.0, 0.0)
-        pay_ref[pl.ds(slot * SLOT_ROWS + 32, 8)] = jnp.full((8, 128), placed, F32)
-
-
-def full_kernel(coarse_ref, number_ref, half_ref, route_ref, full_ref):
-    lane = lax.broadcasted_iota(jnp.int32, (8, 128), 1)
+    for column in range(32):
+        pay_ref[pl.ds(NUMBER_ROW + column, HOSTS, stride=SLOT_ROWS)] = number_ref[
+            :, pl.ds(column * 128, 128)
+        ]
+    for side in range(2):
+        pay_ref[pl.ds(MEAN_ROW + side, HOSTS, stride=SLOT_ROWS)] = mean_ref[
+            :, pl.ds(side * 128, 128)
+        ]
+    placed = cells_ref[pl.ds(16, HOSTS), pl.ds(0, 128)] >= 0
+    pay_ref[pl.ds(FLAG_ROW, HOSTS, stride=SLOT_ROWS)] = jnp.where(placed, 1.0, 0.0)
+
+
+def full_kernel(coarse_ref, number_ref, half_ref, cells_ref, full_ref):
+    lane = lax.broadcasted_iota(jnp.int32, (HOSTS, 128), 1)
     top = lax.broadcasted_iota(jnp.int32, (8, 128), 0) < 4
-    covered = [jnp.zeros((8, 128), jnp.int32) for _ in range(4)]
-    for slot in range(HOSTS):
-        cell = route_ref[slot]
-        hit = (lane // 4) == (cell & 31)
-        for corner in range(4):
-            chosen = jnp.where((cell >> 5) == corner, 1, 0)
-            covered[corner] = jnp.where(hit, jnp.maximum(covered[corner], chosen), covered[corner])
+    cells = cells_ref[pl.ds(16, HOSTS), pl.ds(0, 128)]
+    hit = (lane >> 2) == (cells & 31)
+    covered = [
+        jnp.max(jnp.where(hit & ((cells >> 5) == corner), 1, 0), axis=0, keepdims=True)
+        for corner in range(4)
+    ]
 
     def sheet(q, x):
         return half_ref[pl.ds((q * 16 + x % 16) * 16, 16)]
@@ -277,18 +281,16 @@
             full_ref[q, x] = jnp.where(keep, done, 0.0)
 
 
-def put_kernel(back_ref, full_ref, route_ref, copy_ref, next_ref):
-    even = back_ref[pl.ds(0, 16, stride=2)]
-    odd = back_ref[pl.ds(1, 16, stride=2)]
+def put_means(back, full_ref, cells_ref, copy_ref, next_ref):
+    even, odd = back[:, :128], back[:, 128:]
     values = jnp.concatenate(
         [even, pltpu.roll(even, 64, 1), odd, pltpu.roll(odd, 64, 1)], axis=0
     )
     high = values.astype(BF16)
-    rest = values - high.astype(F32)
-    low, lowest = split(rest)
+    low, lowest = split(values - high.astype(F32))
     parts = jnp.concatenate([high, low, lowest, jnp.zeros_like(high)], axis=0)
     spread = dot_t(copy_ref[...], parts)
-    cells = slot_lanes(route_ref, 1, (8, 256))[0:1]
+    cells = cells_ref[pl.ds(8, 1)]
     row = lax.broadcasted_iota(jnp.int32, (256, 1), 0)
     corner = ((row >> 5) & 1) * 2 + ((row >> 2) & 1)
     spread = jnp.where((cells >> 5) == corner, spread, 0.0).astype(BF16)
@@ -308,26 +310,60 @@
     return both[:, :256], both[:, 256:] + dot(high, rest_ref[...])
 
 
+def plus(left, right):
+    if left is None or right is None:
+        return right if left is None else left
+    return left + right
+
+
+def minus(left, right):
+    if right is None:
+        return left
+    return -right if left is None else left - right
+
+
 def x_parts(padded):
     laplace, advect = [], []
     for x in range(2, 18):
-        laplace.append(padded[x + 1] + padded[x - 1])
-        advect.append(
-            (WIND_FINE[0] / 12.0)
-            * (8.0 * (padded[x + 1] - padded[x - 1]) - (padded[x + 2] - padded[x - 2]))
-        )
-    return jnp.concatenate(laplace, axis=0), jnp.concatenate(advect, axis=0)
-
-
-def load_numbers(number_ref):
-    return jnp.concatenate(
-        [number_ref[:, pl.ds(x * 256, 256)] for x in range(EDGE)], axis=0
-    )
-
-
-def early_kernel(fine_ref, number_ref, plane_ref, rest_ref, step_ref, field_ref):
-    zero = jnp.zeros((HOSTS, 256), F32)
-    numbers = load_numbers(number_ref)
+        near = minus(padded[x + 1], padded[x - 1])
+        far = minus(padded[x + 2], padded[x - 2])
+        laplace.append(plus(padded[x + 1], padded[x - 1]))
+        near = None if near is None else (8.0 * WIND_FINE[0] / 12.0) * near
+        far = None if far is None else (WIND_FINE[0] / 12.0) * far
+        advect.append(minus(near, far))
+    return laplace, advect
+
+
+def plane(values, x):
+    return values[x * HOSTS : (x + 1) * HOSTS]
+
+
+def rate_of(numbers, padded, laplace, advect):
+    x_laplace, x_advect = x_parts(padded)
+    return [
+        numbers[x] * plus(x_laplace[x], plane(laplace, x)) - plus(x_advect[x], plane(advect, x))
+        for x in range(EDGE)
+    ]
+
+
+def means(planes, mean_ref):
+    total = None
+    for big_x in range(PB):
+        group = planes[big_x * 4 : big_x * 4 + 4]
+        high, low = split((group[0] + group[1]) + (group[2] + group[3]))
+        weights = mean_ref[pl.ds(big_x * 256, 256)]
+        total = plus(total, dot(high, weights) + dot(low, weights))
+    return total
+
+
+def lane_of_q():
+    return (lax.broadcasted_iota(jnp.int32, (HOSTS, 256), 1) >> 4) & 3
+
+
+def early_kernel(fine_ref, number_ref, plane_ref, rest_ref, mean_ref, route_ref, step_ref, back_ref, cells_ref):
+    numbers = [number_ref[:, pl.ds(x * 256, 256)] for x in range(EDGE)]
+    nothing = [None, None]
+    back = jnp.zeros((HOSTS, 256), F32)
     for q in range(4):
         planes = []
         for x in range(EDGE):
@@ -335,92 +371,103 @@
                 fine_ref[pl.ds((2 * x + side) * 4 + q, HOSTS, stride=128)] for side in range(2)
             ]
             planes.append(jnp.concatenate(sides, axis=1))
-        field = jnp.concatenate(planes, axis=0)
-        laplace, advect = plane_parts(field, plane_ref, rest_ref)
-        x_laplace, x_advect = x_parts([zero, zero] + planes + [zero, zero])
-        at = pl.ds(q * 256, 256)
-        field_ref[at] = field
-        step_ref[at] = field + numbers * (laplace + x_laplace) - (advect + x_advect)
+        parts = plane_parts(jnp.concatenate(planes, axis=0), plane_ref, rest_ref)
+        rate = rate_of(numbers, nothing + planes + nothing, *parts)
+        half = [planes[x] + rate[x] for x in range(EDGE)]
+        parts = plane_parts(jnp.concatenate(half, axis=0), plane_ref, rest_ref)
+        rate = rate_of(numbers, nothing + half + nothing, *parts)
+        done = [0.5 * (planes[x] + half[x] + rate[x]) for x in range(EDGE)]
+        for x in range(EDGE):
+            step_ref[pl.ds((q * EDGE + x) * HOSTS, HOSTS)] = done[x]
+        back = jnp.where(lane_of_q() == q, means(done, mean_ref), back)
+    back_ref[...] = back
+    lane = lax.broadcasted_iota(jnp.int32, (8, 256), 1)
+    row = lax.broadcasted_iota(jnp.int32, (HOSTS, 256), 0)
+    by_eight = jnp.zeros((8, 256), jnp.int32)
+    by_one = jnp.zeros((8, 256), jnp.int32)
+    by_row = jnp.zeros((HOSTS, 256), jnp.int32)
+    for slot in range(HOSTS):
+        cell = route_ref[slot]
+        by_eight = jnp.where(((lane >> 3) & 15) == slot, cell, by_eight)
+        by_one = jnp.where((lane & 15) == slot, cell, by_one)
+        by_row = jnp.where(row == slot, cell, by_row)
+    cells_ref[pl.ds(0, 8)] = by_eight
+    cells_ref[pl.ds(8, 8)] = by_one
+    cells_ref[pl.ds(16, HOSTS)] = by_row
+
+
+def ghosts(block_ref, q, t, ghost_ref, face_ref):
+    interp = interp_table(PB, RATIO)
+    first_half = lax.broadcasted_iota(jnp.int32, (HOSTS, 128), 1) < 64
+    coarse = []
+    for x in range(8):
+        rows = block_ref[pl.ds(q * 8 + x, HOSTS, stride=SLOT_ROWS)]
+        turned = pltpu.roll(rows, 64, 1)
+        coarse.append(
+            jnp.where(first_half, rows, turned) if t == 0 else jnp.where(first_half, turned, rows)
+        )
+    inner, outer = [], []
+    for i in range(EDGE + 4):
+        total = None
+        for j in range(8):
+            if interp[i, j] != 0.0:
+                total = plus(total, float(interp[i, j]) * coarse[j])
+        (inner if 2 <= i < EDGE + 2 else outer).append(total)
+    sides = dot(jnp.concatenate(split(jnp.concatenate(inner, axis=0)), axis=1), ghost_ref[...])
+    faces = dot(jnp.concatenate(split(jnp.concatenate(outer, axis=0)), axis=1), face_ref[...])
+    return sides[:, :256], sides[:, 256:], [plane(faces, i) for i in range(4)]
+
+
+def ghost_part(block_ref, numbers, q, plane_ref, rest_ref, ghost_ref, face_ref):
+    laplace, advect, faces = ghosts(block_ref, q, 0, ghost_ref, face_ref)
+    half = rate_of(numbers, faces[:2] + [None] * EDGE + faces[2:], laplace, advect)
+    laplace, advect, faces = ghosts(block_ref, q, 1, ghost_ref, face_ref)
+    parts = plane_parts(jnp.concatenate(half, axis=0), plane_ref, rest_ref)
+    rate = rate_of(
+        numbers, faces[:2] + half + faces[2:], parts[0] + laplace, parts[1] + advect
+    )
+    return [0.5 * (half[x] + rate[x]) for x in range(EDGE)]
 
 
 def late_kernel(
-    block_ref,
-    step_ref,
-    field_ref,
-    number_ref,
+    block_ref, step_ref, old_ref, number_ref, plane_ref, rest_ref, ghost_ref, face_ref, fine_ref
+):
+    numbers = [number_ref[:, pl.ds(x * 256, 256)] for x in range(EDGE)]
+    placed = block_ref[pl.ds(FLAG_ROW, HOSTS, stride=SLOT_ROWS)] > 0.5
+    for q in range(4):
+        added = ghost_part(block_ref, numbers, q, plane_ref, rest_ref, ghost_ref, face_ref)
+        for x in range(EDGE):
+            done = step_ref[pl.ds((q * EDGE + x) * HOSTS, HOSTS)] + added[x]
+            for side in range(2):
+                at = pl.ds((2 * x + side) * 4 + q, HOSTS, stride=128)
+                fine_ref[at] = jnp.where(
+                    placed, done[:, side * 128 : side * 128 + 128], old_ref[at]
+                )
+
+
+def back_kernel(
+    sent_ref,
+    got_ref,
+    full_ref,
+    cells_ref,
+    copy_ref,
     plane_ref,
     rest_ref,
     ghost_ref,
     face_ref,
     mean_ref,
-    fine_ref,
-    back_ref,
+    next_ref,
 ):
-    interp = interp_table(PB, RATIO)
-    zero = jnp.zeros((HOSTS, 256), F32)
-    numbers = load_numbers(number_ref)
-    first_half = lax.broadcasted_iota(jnp.int32, (HOSTS, 128), 1) < 64
-    placed = block_ref[pl.ds(32, HOSTS, stride=SLOT_ROWS)] > 0.5
-    lane_q = (lax.broadcasted_iota(jnp.int32, (HOSTS, 256), 1) >> 4) & 3
-    back = zero
-
-    def ghosts(q, t):
-        coarse = []
-        for x in range(8):
-            rows = block_ref[pl.ds(q * 8 + x, HOSTS, stride=SLOT_ROWS)]
-            turned = pltpu.roll(rows, 64, 1)
-            coarse.append(
-                jnp.where(first_half, rows, turned) if t == 0 else jnp.where(first_half, turned, rows)
-            )
-        inner, outer = [], []
-        for i in range(EDGE + 4):
-            total = None
-            for j in range(8):
-                if interp[i, j] != 0.0:
-                    term = float(interp[i, j]) * coarse[j]
-                    total = term if total is None else total + term
-            (inner if 2 <= i < EDGE + 2 else outer).append(total)
-        inner = jnp.concatenate(inner, axis=0)
-        outer = jnp.concatenate(outer, axis=0)
-        sides = dot(jnp.concatenate(split(inner), axis=1), ghost_ref[...])
-        faces = dot(jnp.concatenate(split(outer), axis=1), face_ref[...])
-        return sides[:, :256], sides[:, 256:], [faces[i * 16 : (i + 1) * 16] for i in range(4)]
-
+    def got(row):
+        sides = [got_ref[pl.ds(row + side, HOSTS, stride=SLOT_ROWS)] for side in range(2)]
+        return jnp.concatenate(sides, axis=1)
+
+    numbers = [got(NUMBER_ROW + 2 * x) for x in range(EDGE)]
+    back = jnp.zeros((HOSTS, 256), F32)
     for q in range(4):
-        at = pl.ds(q * 256, 256)
-        side_laplace, side_advect, faces = ghosts(q, 0)
-        x_laplace, x_advect = x_parts(faces[:2] + [zero] * EDGE + faces[2:])
-        half = step_ref[at] + numbers * (side_laplace + x_laplace) - (side_advect + x_advect)
-        side_laplace, side_advect, faces = ghosts(q, 1)
-        planes = [half[x * 16 : (x + 1) * 16] for x in range(EDGE)]
-        x_laplace, x_advect = x_parts(faces[:2] + planes + faces[2:])
-        laplace, advect = plane_parts(half, plane_ref, rest_ref)
-        field = field_ref[at]
-        done = 0.5 * (
-            field
-            + half
-            + numbers * (laplace + side_laplace + x_laplace)
-            - (advect + side_advect + x_advect)
-        )
-        sums = []
-        for x in range(EDGE):
-            rows = slice(x * 16, (x + 1) * 16)
-            for side in range(2):
-                lanes = slice(side * 128, side * 128 + 128)
-                fine_ref[pl.ds((2 * x + side) * 4 + q, HOSTS, stride=128)] = jnp.where(
-                    placed, done[rows, lanes], field[rows, lanes]
-                )
-        total = zero
-        for big_x in range(PB):
-            group = [done[(big_x * 4 + i) * 16 : (big_x * 4 + i + 1) * 16] for i in range(4)]
-            sums.append((group[0] + group[1]) + (group[2] + group[3]))
-        for big_x in range(PB):
-            high, low = split(sums[big_x])
-            weights = mean_ref[pl.ds(big_x * 256, 256)]
-            total = total + dot(high, weights) + dot(low, weights)
-        back = jnp.where(lane_q == q, total, back)
-    back_ref[pl.ds(0, HOSTS, stride=2)] = back[:, :128]
-    back_ref[pl.ds(1, HOSTS, stride=2)] = back[:, 128:]
+        added = ghost_part(sent_ref, numbers, q, plane_ref, rest_ref, ghost_ref, face_ref)
+        back = jnp.where(lane_of_q() == q, means(added, mean_ref), back)
+    put_means(back + got(MEAN_ROW), full_ref, cells_ref, copy_ref, next_ref)
 
 
 def call(kernel, operands, outs, smem=(), scratch=(), flops=1000000, name=None):
@@ -429,78 +476,80 @@
     moved = sum(int(np.prod(o.shape)) * o.dtype.itemsize for o in operands)
     return pl.pallas_call(
         kernel,
-        out_shape=tuple(jax.ShapeDtypeStruct(shape, F32) for shape in outs),
+        out_shape=tuple(jax.ShapeDtypeStruct(shape, dtype) for shape, dtype in outs),
         in_specs=[scalar if i in smem else vmem for i in range(len(operands))],
         out_specs=tuple(vmem for _ in outs),
         scratch_shapes=[pltpu.VMEM(shape, F32) for shape in scratch],
-        compiler_params=pltpu.CompilerParams(vmem_limit_bytes=40 * 1024 * 1024),
+        compiler_params=pltpu.CompilerParams(vmem_limit_bytes=LIMIT * 1024 * 1024),
         cost_estimate=pl.CostEstimate(flops=flops, bytes_accessed=moved, transcendentals=0),
         name=name,
     )(*operands)
 
 
 def shards(coarse_state, diffusion_number, route_cell, fine_state, fine_diffusion):
-    plane, plane_rest, ghost, face, mean, copy = (jnp.asarray(table) for table in tables())
-    route = route_cell.reshape(HOSTS)
-
-    def exchange(low, high, axis):
+    flat, rest, ghost, face, mean, copy = (jnp.asarray(table) for table in tables())
+    fine_rows = fine_state.reshape(HOSTS, 4, 32, 128).transpose(0, 2, 1, 3).reshape(2048, 128)
+    fine_numbers = fine_diffusion.reshape(HOSTS, EDGE**3)
+
+    def exchange(low, high, axis, up_first):
         count = lax.axis_size(axis)
         up = [(i, i + 1) for i in range(count - 1)]
         down = [(i + 1, i) for i in range(count - 1)]
-        return lax.ppermute(high, axis, up), lax.ppermute(low, axis, down)
+        if up_first:
+            from_below = lax.ppermute(high, axis, up)
+            return from_below, lax.ppermute(low, axis, down)
+        from_above = lax.ppermute(low, axis, down)
+        return lax.ppermute(high, axis, up), from_above
 
     fields = jnp.concatenate([coarse_state, diffusion_number[None]], axis=0)
-    left, right = exchange(fields[:, :4], fields[:, 4:], "gx")
+    left, right = exchange(fields[:, :4], fields[:, 4:], "gx", True)
     own = (coarse_state, diffusion_number, left, right)
-    low, high = call(y_kernel, own, [(320, 128), (320, 128)], name="y_messages")
-    below, above = exchange(low, high, "gy")
+    low, high = call(y_kernel, own, [((320, 128), F32)] * 2, name="y_messages")
+    below, above = exchange(low, high, "gy", True)
     everything, low, high = call(
-        z_kernel, own + (below, above), [(1280, 128), (40, 128), (40, 128)], name="z_messages"
-    )
-    before, after = exchange(low, high, "gz")
-    pay, half = call(
+        z_kernel,
+        own + (below, above),
+        [((1280, 128), F32), ((40, 128), F32), ((40, 128), F32)],
+        name="z_messages",
+    )
+    before, after = exchange(low, high, "gz", False)
+    step, early_means, cells = call(
+        early_kernel,
+        (fine_rows, fine_numbers, flat, rest, mean, route_cell.reshape(HOSTS)),
+        [((1024, 256), F32), ((HOSTS, 256), F32), ((32, 256), jnp.int32)],
+        smem=(5,),
+        flops=10**9,
+        name="fine_early",
+    )
+    sent, half = call(
         half_kernel,
-        (everything, before, after, route),
-        [(HOSTS * SLOT_ROWS, 128), (1024, 256)],
-        smem=(3,),
+        (everything, before, after, cells, fine_numbers, early_means),
+        [((HOSTS * SLOT_ROWS, 128), F32), ((1024, 256), F32)],
         scratch=[(1280, 256), (512, 128)],
         name="half_step",
     )
-    fine_rows = fine_state.reshape(HOSTS, 4, 32, 128).transpose(0, 2, 1, 3).reshape(2048, 128)
-    fine_numbers = fine_diffusion.reshape(HOSTS, EDGE**3)
-    step, field = call(
-        early_kernel,
-        (fine_rows, fine_numbers, plane, plane_rest),
-        [(1024, 256), (1024, 256)],
-        flops=10**9,
-        name="fine_early",
-    )
-    blocks = lax.all_to_all(
-        pay.reshape(HOSTS, SLOT_ROWS, 128), "gz", split_axis=0, concat_axis=0, tiled=True
+    got = lax.all_to_all(
+        sent.reshape(HOSTS, SLOT_ROWS, 1, 128), "gz", split_axis=0, concat_axis=0, tiled=True
     ).reshape(HOSTS * SLOT_ROWS, 128)
     (full,) = call(
         full_kernel,
-        (coarse_state, diffusion_number, half, route),
-        [(4, 8, 8, 128)],
-        smem=(3,),
+        (coarse_state, diffusion_number, half, cells),
+        [((4, 8, 8, 128), F32)],
         name="coarse_full",
     )
-    fine_done, back = call(
+    (coarse_next,) = call(
+        back_kernel,
+        (sent, got, full, cells, copy, flat, rest, ghost, face, mean),
+        [((4, 8, 8, 128), F32)],
+        flops=10**9,
+        name="coarse_next",
+    )
+    (fine_done,) = call(
         late_kernel,
-        (blocks, step, field, fine_numbers, plane, plane_rest, ghost, face, mean),
-        [(2048, 128), (32, 128)],
+        (got, step, fine_rows, fine_numbers, flat, rest, ghost, face),
+        [((2048, 128), F32)],
         flops=10**9,
-        name="fine_late",
-    )
-    returned = lax.all_to_all(
-        back.reshape(HOSTS, 2, 128), "gz", split_axis=0, concat_axis=0, tiled=True
-    ).reshape(32, 128)
-    (coarse_next,) = call(
-        put_kernel,
-        (returned, full, route, copy),
-        [(4, 8, 8, 128)],
-        smem=(2,),
-        name="put_means",
+        name="fine_next",
     )
     fine_next = (
         fine_done.reshape(HOSTS, 32, 4, 128).transpose(0, 2, 1, 3).reshape(fine_state.shape)

time: 92 us -> 87.3 us (0.949)
  waiting for transfers between devices: 36.2 us -> 27.3 us
  local copies, waits for them, and re-layouts: 6.99 us -> 10.8 us
  Pallas kernels: 12.4 us -> 15.9 us
  starting transfers between devices: 34.1 us -> 30.6 us
    ppermute x6, waiting for transfers between devices: 12.6 us -> 7.86 us  [the longest x2 5.36 us: exchange(): from_below = lax.ppermute(high, axis, up)]
    all_to_all x2 -> x1, waiting for transfers between devices: 23.6 us -> 19.4 us  [shards(): lax.all_to_all(sent.reshape(HOSTS, SLOT_ROWS, 1, 128), 'gz', split_axis=0...]
    unnamed x26 -> x48, local copies, waits for them, and re-layouts: 6.99 us -> 10.8 us
    pallas_call x7, Pallas kernels: 12.4 us -> 15.9 us  [call(): pl.pallas_call(kernel, out_shape=tuple((jax.ShapeDtypeStruct(shape, dtype...]
    all_to_all x2 -> x1, starting transfers between devices: 19 us -> 15.5 us  [shards(): lax.all_to_all(sent.reshape(HOSTS, SLOT_ROWS, 1, 128), 'gz', split_axis=0...]
  transfers between devices with their start and end apart: 8 -> 7, of which waited for: 8 -> 5; matrix products, arithmetic and copies ran while one was open for 0% -> 0% of each run, Pallas kernels for 3% -> 6%
where the time goes in v1:
time: 87.3 us; the launch traced here: 86.5 us
  starting transfers between devices  30.6 us (35%)
  waiting for transfers between devices  27.3 us (31%)
  Pallas kernels  15.9 us (18%)
  local copies, waits for them, and re-layouts  10.8 us (12%)
  other arithmetic  1.02 us (1%)
    all_to_all x1, waiting for transfers between devices, shards(): lax.all_to_all(sent.reshape(HOSTS, SLOT_ROWS, 1, 128), 'gz', split_axis=0...  19.4 us
    pallas_call x7, Pallas kernels, call(): pl.pallas_call(kernel, out_shape=tuple((jax.ShapeDtypeStruct(shape, dtype...  15.9 us
    all_to_all x1, starting transfers between devices, shards(): lax.all_to_all(sent.reshape(HOSTS, SLOT_ROWS, 1, 128), 'gz', split_axis=0...  15.5 us
    unnamed x48, local copies, waits for them, and re-layouts  10.8 us
    ppermute x2, starting transfers between devices, exchange(): return (from_below, lax.ppermute(low, axis, down))  6.38 us
    ppermute x2, waiting for transfers between devices, exchange(): from_below = lax.ppermute(high, axis, up)  5.36 us
    ppermute x1, starting transfers between devices, exchange(): return (lax.ppermute(high, axis, up), from_above)  4.28 us
    ppermute x2, starting transfers between devices, exchange(): from_below = lax.ppermute(high, axis, up)  3.21 us
  transfers between devices with their start and end apart: 7, of which 5 were waited for; matrix products, arithmetic and copies ran while one was open for 0% of the time, Pallas kernels for 6%

profile of v1, /device:TPU:22, one launch (start us, length us, event | category | flops | bytes accessed | tf_op | source)
XLA Modules:
  0.0 86.5 jit_solution(6000360641982211497)
XLA Ops:
  0.6 0.0 copy-start
  0.6 0.0 copy-start.1
  0.6 1.0 %pad_maximum_fusion = (f32[5,4,8,128]{3,2,1,0:T(8,128)S(1)}, f32[5,4,8,128]{3,2,1,0:T(8,128)S(1)}) fusion(f32[1,8,8,128]{3,2,1,0:T(8,128)} %bitcast.23, f32[4,8,8,128]{3,2,1,0:T(8,128)} %coarse_ref.5), kind=kLoop, calls=%fused_computation.3 | loop fusion | flops 40960 | bytes 327680 | tf_op jit(solution)/shard_map/concatenate | solution.py:504
  1.7 2.7 %collective-permute-start.1 = (f32[5,4,8,128]{3,2,1,0:T(8,128)S(1)}, f32[5,4,8,128]{3,2,1,0:T(8,128)S(1)}, u32[]{:S(2)}, u32[]{:S(2)}) collective-permute-start(f32[5,4,8,128]{3,2,1,0:T(8,128)S(1)} %get-tuple-element.22), channel_id=1, source_target_pairs={{128,0},{256,128},{384,256},{129,1},{257,129},{385,257},{130,2},{2... | collective-permute-start | bytes 245768 | tf_op jit(solution)/shard_map/ppermute | solution.py:500
  4.4 1.3 %collective-permute-start = (f32[5,4,8,128]{3,2,1,0:T(8,128)S(1)}, f32[5,4,8,128]{3,2,1,0:T(8,128)S(1)}, u32[]{:S(2)}, u32[]{:S(2)}) collective-permute-start(f32[5,4,8,128]{3,2,1,0:T(8,128)S(1)} %get-tuple-element.23), channel_id=1, source_target_pairs={{0,128},{128,256},{256,384},{1,129},{129,257},{257,385},{2,130},{1... | collective-permute-start | bytes 245768 | tf_op jit(solution)/shard_map/ppermute | solution.py:499
  5.7 0.7 collective-permute-done.1.right_ref
  6.5 4.3 %collective-permute-done.left_ref = f32[5,4,8,128]{3,2,1,0:T(8,128)S(1)} collective-permute-done((f32[5,4,8,128]{3,2,1,0:T(8,128)S(1)}, f32[5,4,8,128]{3,2,1,0:T(8,128)S(1)}, u32[]{:S(2)}, u32[]{:S(2)}) %collective-permute-start) | collective-permute-done | bytes 81952 | tf_op jit(solution)/shard_map/ppermute | solution.py:499
  10.7 0.0 copy-done
  10.8 0.8 copy-done.11
  11.5 1.9 %collective-permute-start.2 = (f32[320,128]{1,0:T(8,128)S(1)}, f32[320,128]{1,0:T(8,128)S(1)}, u32[]{:S(2)}, u32[]{:S(2)}) collective-permute-start(f32[320,128]{1,0:T(8,128)S(1)} %get-tuple-element.12), channel_id=1, source_target_pairs={{0,16},{16,32},{32,48},{48,64},{64,80},{80,96},{96,112},{1,17},{17... | collective-permute-start | bytes 491528 | tf_op jit(solution)/shard_map/ppermute | solution.py:499
  13.5 3.6 %collective-permute-start.3 = (f32[320,128]{1,0:T(8,128)S(1)}, f32[320,128]{1,0:T(8,128)S(1)}, u32[]{:S(2)}, u32[]{:S(2)}) collective-permute-start(f32[320,128]{1,0:T(8,128)S(1)} %get-tuple-element.13), channel_id=1, source_target_pairs={{16,0},{32,16},{48,32},{64,48},{80,64},{96,80},{112,96},{17,1},{33... | collective-permute-start | bytes 491528 | tf_op jit(solution)/shard_map/ppermute | solution.py:500
  17.1 1.1 %collective-permute-done.2.below_ref = f32[320,128]{1,0:T(8,128)S(1)} collective-permute-done((f32[320,128]{1,0:T(8,128)S(1)}, f32[320,128]{1,0:T(8,128)S(1)}, u32[]{:S(2)}, u32[]{:S(2)}) %collective-permute-start.2) | collective-permute-done | bytes 163872 | tf_op jit(solution)/shard_map/ppermute | solution.py:499
  18.2 1.8 %collective-permute-done.3.above_ref = f32[320,128]{1,0:T(8,128)S(1)} collective-permute-done((f32[320,128]{1,0:T(8,128)S(1)}, f32[320,128]{1,0:T(8,128)S(1)}, u32[]{:S(2)}, u32[]{:S(2)}) %collective-permute-start.3) | collective-permute-done | bytes 163872 | tf_op jit(solution)/shard_map/ppermute | solution.py:500
  19.9 0.8 copy-done.12
  20.7 0.4 z_messages.1
  21.1 4.3 %collective-permute-start.4 = (f32[40,128]{1,0:T(8,128)S(1)}, f32[40,128]{1,0:T(8,128)S(1)}, u32[]{:S(2)}, u32[]{:S(2)}) collective-permute-start(f32[40,128]{1,0:T(8,128)S(1)} %get-tuple-element.15), channel_id=1, source_target_pairs={{0,1},{1,2},{2,3},{3,4},{4,5},{5,6},{6,7},{7,8},{8,9},{9,10},{10,1... | collective-permute-start | bytes 61448 | tf_op jit(solution)/shard_map/ppermute | solution.py:502
  25.4 1.3 %collective-permute-start.5 = (f32[40,128]{1,0:T(8,128)S(1)}, f32[40,128]{1,0:T(8,128)S(1)}, u32[]{:S(2)}, u32[]{:S(2)}) collective-permute-start(f32[40,128]{1,0:T(8,128)S(1)} %get-tuple-element.16), channel_id=1, source_target_pairs={{1,0},{2,1},{3,2},{4,3},{5,4},{6,5},{7,6},{8,7},{9,8},{10,9},{11,1... | collective-permute-start | bytes 61448 | tf_op jit(solution)/shard_map/ppermute | solution.py:501
  26.7 0.0 copy-start.20
  26.7 0.0 copy-done.1
  26.7 0.0 copy-done.15
  26.7 0.6 copy-done.20
  27.3 0.9 %copy-done.4 = f32[1,1,1,16,4096]{4,3,2,1,0:T(8,128)S(1)} copy-done((f32[1,1,1,16,4096]{4,3,2,1,0:T(8,128)S(1)}, f32[1,1,1,16,4096]{4,3,2,1,0:T(8,128)}, u32[]{:S(2)}) %copy-start.4) | copy-done | bytes 262168
  28.3 1.0 %copy-done.8 = bf16[512,512]{1,0:T(8,128)(2,1)S(1)} copy-done((bf16[512,512]{1,0:T(8,128)(2,1)S(1)}, bf16[512,512]{1,0:T(8,128)(2,1)}, u32[]{:S(2)}) %copy-start.8) | copy-done | bytes 524312
  29.3 1.0 %copy-done.21 = bf16[1024,256]{1,0:T(8,128)(2,1)S(1)} copy-done((bf16[1024,256]{1,0:T(8,128)(2,1)S(1)}, bf16[1024,256]{1,0:T(8,128)(2,1)}, u32[]{:S(2)}) %copy-start.21) | copy-done | bytes 524312
  30.4 4.8 %fine_early.1 = (f32[1024,256]{1,0:T(8,128)S(1)}, f32[16,256]{1,0:T(8,128)S(1)}, s32[32,256]{1,0:T(8,128)S(1)}) custom-call(f32[2048,128]{1,0:T(8,128)S(1)} %bitcast.17, f32[16,4096]{1,0:T(8,128)S(1)} %bitcast.19, bf16[512,512]{1,0:T(8,128)(2,1)S(1)} %copy-done.8, bf16[256,256]{1,0:T(8,128)(2,1)S(1)} %copy-done.15, bf16[1024,256]{1,0:T(8,128)(2,1)S(1)} %copy-done.21, ...), custom_call_target="tpu_custom_call" | custom-call | flops 1000000000 | bytes 2490432 | tf_op jit(solution)/shard_map/fine_early/pallas_call | solution.py:477
  35.2 0.0 collective-permute-done.4.before_ref
  35.2 0.0 collective-permute-done.5.after_ref
  35.2 0.0 copy-done.5
  35.2 2.2 %half_step.1 = (f32[1072,128]{1,0:T(8,128)S(1)}, f32[1024,256]{1,0:T(8,128)S(1)}) custom-call(f32[1280,128]{1,0:T(8,128)S(1)} %get-tuple-element.14.all_ref, f32[40,128]{1,0:T(8,128)S(1)} %collective-permute-done.4.before_ref, f32[40,128]{1,0:T(8,128)S(1)} %collective-permute-done.5.after_ref, s32[32,256]{1,0:T(8,128)S(1)} %get-tuple-element.17.cells_ref, ...), custom_call_target="tpu_custom_call" | custom-call | flops 1000000 | bytes 1007616 | tf_op jit(solution)/shard_map/half_step/pallas_call | solution.py:477
  37.4 0.0 copy-start.2
  37.4 1.0 %copy-done.2 = f32[1024,256]{1,0:T(8,128)} copy-done((f32[1024,256]{1,0:T(8,128)}, f32[1024,256]{1,0:T(8,128)S(1)}, u32[]{:S(2)}) %copy-start.2) | copy-done | bytes 1048600
  38.4 0.8 copy-done.6
  39.2 15.5 %all-to-all-start = ((f32[16,67,1,128]{3,2,1,0:T(1,128)}), f32[16,67,1,128]{3,2,1,0:T(1,128)S(1)}, u32[]{:S(2)}, u32[]{:S(2)}) async-start(f32[16,67,1,128]{3,2,1,0:T(1,128)} %bitcast.22), calls=%async_computation | async-start | bytes 1097728 | tf_op jit(solution)/shard_map/all_to_all | solution.py:531
  54.7 0.0 copy-done.13
  54.7 0.0 copy-start.3
  54.7 1.2 %copy-done.3 = f32[1024,256]{1,0:T(8,128)S(1)} copy-done((f32[1024,256]{1,0:T(8,128)S(1)}, f32[1024,256]{1,0:T(8,128)}, u32[]{:S(2)}) %copy-start.3) | copy-done | bytes 1048600
  55.9 0.3 coarse_full.1.full_ref
  56.3 0.0 copy-start.18
  56.3 0.6 copy-done.18
  56.9 19.4 %all-to-all-done = f32[16,67,1,128]{3,2,1,0:T(1,128)S(1)} async-done(((f32[16,67,1,128]{3,2,1,0:T(1,128)}), f32[16,67,1,128]{3,2,1,0:T(1,128)S(1)}, u32[]{:S(2)}, u32[]{:S(2)}) %all-to-all-start) | async-done | bytes 548896 | tf_op jit(solution)/shard_map/all_to_all | solution.py:531
  76.4 0.0 copy-done.14
  76.4 1.0 %copy-done.9 = bf16[512,512]{1,0:T(8,128)(2,1)S(1)} copy-done((bf16[512,512]{1,0:T(8,128)(2,1)S(1)}, bf16[512,512]{1,0:T(8,128)(2,1)}, u32[]{:S(2)}) %copy-start.9) | copy-done | bytes 524312
  77.4 0.9 %copy-done.16 = bf16[256,256]{1,0:T(8,128)(2,1)S(1)} copy-done((bf16[256,256]{1,0:T(8,128)(2,1)S(1)}, bf16[256,256]{1,0:T(8,128)(2,1)}, u32[]{:S(2)}) %copy-start.16) | copy-done | bytes 131096
  78.3 0.0 copy-start.22
  78.3 0.0 copy-start.23
  78.4 3.9 %fine_next.1 = f32[2048,128]{1,0:T(8,128)} custom-call(f32[1072,128]{1,0:T(8,128)S(1)} %bitcast.15, f32[1024,256]{1,0:T(8,128)S(1)} %get-tuple-element.21.step_ref, f32[2048,128]{1,0:T(8,128)S(1)} %bitcast.18, f32[16,4096]{1,0:T(8,128)S(1)} %bitcast.21, bf16[512,512]{1,0:T(8,128)(2,1)S(1)} %copy-done.9, bf16[256,256]{1,0:T(8,128)(2,1)S(1)} %copy-done.15, ...), custom_call_target="tpu_custom_call" | custom-call | flops 1000000000 | bytes 3956736 | tf_op jit(solution)/shard_map/fine_next/pallas_call | solution.py:477
  82.3 0.0 copy-done.10
  82.3 4.1 %coarse_next.1 = f32[4,8,8,128]{3,2,1,0:T(8,128)} custom-call(f32[1072,128]{1,0:T(8,128)S(1)} %copy-done.7, f32[1072,128]{1,0:T(8,128)S(1)} %bitcast.16, f32[4,8,8,128]{3,2,1,0:T(8,128)S(1)} %copy-done.19, s32[32,256]{1,0:T(8,128)S(1)} %get-tuple-element.17.cells_ref, bf16[256,128]{1,0:T(8,128)(2,1)S(1)} %copy-done.23, bf16[512,512]{1,0:T(8,128)(2,1)S(1)} %copy-done.10, ...), custom_call_target="tpu_custom_call" | custom-call | flops 1000000000 | bytes 2899968 | tf_op jit(solution)/shard_map/coarse_next/pallas_call | solution.py:477
  (22 shorter events, 0.1 us)
Async XLA Ops:
  0.6 10.1 %copy-start = (f32[4,8,8,128]{3,2,1,0:T(8,128)S(1)}, f32[4,8,8,128]{3,2,1,0:T(8,128)}, u32[]{:S(2)}) copy-start(f32[4,8,8,128]{3,2,1,0:T(8,128)} %coarse_ref.5) | copy-start | bytes 393220
  0.6 26.1 %copy-start.1 = (f32[1,1,1,16,4,4096]{5,4,3,2,1,0:T(4,128)S(1)}, f32[1,1,1,16,4,4096]{5,4,3,2,1,0:T(4,128)}, u32[]{:S(2)}) copy-start(f32[1,1,1,16,4,4096]{5,4,3,2,1,0:T(4,128)} %param.14) | copy-start | bytes 3145732
  1.7 4.8 %collective-permute-start.1 = (f32[5,4,8,128]{3,2,1,0:T(8,128)S(1)}, f32[5,4,8,128]{3,2,1,0:T(8,128)S(1)}, u32[]{:S(2)}, u32[]{:S(2)}) collective-permute-start(f32[5,4,8,128]{3,2,1,0:T(8,128)S(1)} %get-tuple-element.22), channel_id=1, source_target_pairs={{128,0},{256,128},{384,256},{129,1},{257,129},{385,257},{130,2},{2... | collective-permute-start | bytes 245768 | tf_op jit(solution)/shard_map/ppermute | solution.py:500
  4.4 6.3 %collective-permute-start = (f32[5,4,8,128]{3,2,1,0:T(8,128)S(1)}, f32[5,4,8,128]{3,2,1,0:T(8,128)S(1)}, u32[]{:S(2)}, u32[]{:S(2)}) collective-permute-start(f32[5,4,8,128]{3,2,1,0:T(8,128)S(1)} %get-tuple-element.23), channel_id=1, source_target_pairs={{0,128},{128,256},{256,384},{1,129},{129,257},{257,385},{2,130},{1... | collective-permute-start | bytes 245768 | tf_op jit(solution)/shard_map/ppermute | solution.py:499
  10.8 0.8 copy-start.11
  11.5 6.6 %collective-permute-start.2 = (f32[320,128]{1,0:T(8,128)S(1)}, f32[320,128]{1,0:T(8,128)S(1)}, u32[]{:S(2)}, u32[]{:S(2)}) collective-permute-start(f32[320,128]{1,0:T(8,128)S(1)} %get-tuple-element.12), channel_id=1, source_target_pairs={{0,16},{16,32},{32,48},{48,64},{64,80},{80,96},{96,112},{1,17},{17... | collective-permute-start | bytes 491528 | tf_op jit(solution)/shard_map/ppermute | solution.py:499
  13.5 6.5 %collective-permute-start.3 = (f32[320,128]{1,0:T(8,128)S(1)}, f32[320,128]{1,0:T(8,128)S(1)}, u32[]{:S(2)}, u32[]{:S(2)}) collective-permute-start(f32[320,128]{1,0:T(8,128)S(1)} %get-tuple-element.13), channel_id=1, source_target_pairs={{16,0},{32,16},{48,32},{64,48},{80,64},{96,80},{112,96},{17,1},{33... | collective-permute-start | bytes 491528 | tf_op jit(solution)/shard_map/ppermute | solution.py:500
  19.9 0.8 copy-start.12
  20.7 6.0 %copy-start.15 = (bf16[256,256]{1,0:T(8,128)(2,1)S(1)}, bf16[256,256]{1,0:T(8,128)(2,1)}, u32[]{:S(2)}) copy-start(bf16[256,256]{1,0:T(8,128)(2,1)} %constant.13.clone.rest_ref) | copy-start | bytes 393220
  21.1 14.1 %collective-permute-start.4 = (f32[40,128]{1,0:T(8,128)S(1)}, f32[40,128]{1,0:T(8,128)S(1)}, u32[]{:S(2)}, u32[]{:S(2)}) collective-permute-start(f32[40,128]{1,0:T(8,128)S(1)} %get-tuple-element.15), channel_id=1, source_target_pairs={{0,1},{1,2},{2,3},{3,4},{4,5},{5,6},{6,7},{7,8},{8,9},{9,10},{10,1... | collective-permute-start | bytes 61448 | tf_op jit(solution)/shard_map/ppermute | solution.py:502
  25.4 9.8 %collective-permute-start.5 = (f32[40,128]{1,0:T(8,128)S(1)}, f32[40,128]{1,0:T(8,128)S(1)}, u32[]{:S(2)}, u32[]{:S(2)}) collective-permute-start(f32[40,128]{1,0:T(8,128)S(1)} %get-tuple-element.16), channel_id=1, source_target_pairs={{1,0},{2,1},{3,2},{4,3},{5,4},{6,5},{7,6},{8,7},{9,8},{10,9},{11,1... | collective-permute-start | bytes 61448 | tf_op jit(solution)/shard_map/ppermute | solution.py:501
  26.7 0.7 copy-start.20
  27.3 0.9 %copy-start.4 = (f32[1,1,1,16,4096]{4,3,2,1,0:T(8,128)S(1)}, f32[1,1,1,16,4096]{4,3,2,1,0:T(8,128)}, u32[]{:S(2)}) copy-start(f32[1,1,1,16,4096]{4,3,2,1,0:T(8,128)} %param.15) | copy-start | bytes 786436
  28.3 1.0 %copy-start.8 = (bf16[512,512]{1,0:T(8,128)(2,1)S(1)}, bf16[512,512]{1,0:T(8,128)(2,1)}, u32[]{:S(2)}) copy-start(bf16[512,512]{1,0:T(8,128)(2,1)} %constant.12.clone.plane_ref) | copy-start | bytes 1572868
  29.3 1.0 %copy-start.21 = (bf16[1024,256]{1,0:T(8,128)(2,1)S(1)}, bf16[1024,256]{1,0:T(8,128)(2,1)}, u32[]{:S(2)}) copy-start(bf16[1024,256]{1,0:T(8,128)(2,1)} %constant.16.clone.mean_ref) | copy-start | bytes 1572868
  30.4 4.8 %copy-start.5 = (f32[1,1,1,16,4096]{4,3,2,1,0:T(8,128)S(1)}, f32[1,1,1,16,4096]{4,3,2,1,0:T(8,128)}, u32[]{:S(2)}) copy-start(f32[1,1,1,16,4096]{4,3,2,1,0:T(8,128)} %param.15) | copy-start | bytes 786436
  37.4 1.0 %copy-start.2 = (f32[1024,256]{1,0:T(8,128)}, f32[1024,256]{1,0:T(8,128)S(1)}, u32[]{:S(2)}) copy-start(f32[1024,256]{1,0:T(8,128)S(1)} %get-tuple-element.20.half_ref) | copy-start | bytes 3145732
  38.4 0.8 copy-start.6
  39.2 15.5 %copy-start.13 = (f32[8,8,128]{2,1,0:T(8,128)S(1)}, f32[8,8,128]{2,1,0:T(8,128)}, u32[]{:S(2)}) copy-start(f32[8,8,128]{2,1,0:T(8,128)} %number_ref.5) | copy-start | bytes 98308
  39.2 37.2 %all-to-all-start = ((f32[16,67,1,128]{3,2,1,0:T(1,128)}), f32[16,67,1,128]{3,2,1,0:T(1,128)S(1)}, u32[]{:S(2)}, u32[]{:S(2)}) async-start(f32[16,67,1,128]{3,2,1,0:T(1,128)} %bitcast.22), calls=%async_computation | async-start | bytes 1097728 | tf_op jit(solution)/shard_map/all_to_all | solution.py:531
  54.7 1.2 %copy-start.3 = (f32[1024,256]{1,0:T(8,128)S(1)}, f32[1024,256]{1,0:T(8,128)}, u32[]{:S(2)}) copy-start(f32[1024,256]{1,0:T(8,128)} %copy-done.2) | copy-start | bytes 3145732
  55.9 20.4 %copy-start.14 = (bf16[256,512]{1,0:T(8,128)(2,1)S(1)}, bf16[256,512]{1,0:T(8,128)(2,1)}, u32[]{:S(2)}) copy-start(bf16[256,512]{1,0:T(8,128)(2,1)} %constant.14.clone.ghost_ref) | copy-start | bytes 786436
  56.3 0.7 copy-start.18
  76.4 1.0 %copy-start.9 = (bf16[512,512]{1,0:T(8,128)(2,1)S(1)}, bf16[512,512]{1,0:T(8,128)(2,1)}, u32[]{:S(2)}) copy-start(bf16[512,512]{1,0:T(8,128)(2,1)} %constant.12.clone.plane_ref) | copy-start | bytes 1572868
  77.4 0.9 %copy-start.16 = (bf16[256,256]{1,0:T(8,128)(2,1)S(1)}, bf16[256,256]{1,0:T(8,128)(2,1)}, u32[]{:S(2)}) copy-start(bf16[256,256]{1,0:T(8,128)(2,1)} %constant.15.clone.face_ref) | copy-start | bytes 393220
  78.3 4.0 %copy-start.7 = (f32[1072,128]{1,0:T(8,128)S(1)}, f32[1072,128]{1,0:T(8,128)}, u32[]{:S(2)}) copy-start(f32[1072,128]{1,0:T(8,128)} %copy-done.6) | copy-start | bytes 1646596
  78.3 4.0 %copy-start.10 = (bf16[512,512]{1,0:T(8,128)(2,1)S(1)}, bf16[512,512]{1,0:T(8,128)(2,1)}, u32[]{:S(2)}) copy-start(bf16[512,512]{1,0:T(8,128)(2,1)} %constant.12.clone.plane_ref) | copy-start | bytes 1572868
  78.3 4.0 %copy-start.17 = (bf16[256,256]{1,0:T(8,128)(2,1)S(1)}, bf16[256,256]{1,0:T(8,128)(2,1)}, u32[]{:S(2)}) copy-start(bf16[256,256]{1,0:T(8,128)(2,1)} %constant.15.clone.face_ref) | copy-start | bytes 393220
  78.3 4.0 %copy-start.19 = (f32[4,8,8,128]{3,2,1,0:T(8,128)S(1)}, f32[4,8,8,128]{3,2,1,0:T(8,128)}, u32[]{:S(2)}) copy-start(f32[4,8,8,128]{3,2,1,0:T(8,128)} %copy-done.18) | copy-start | bytes 393220
  78.3 4.0 %copy-start.22 = (bf16[1024,256]{1,0:T(8,128)(2,1)S(1)}, bf16[1024,256]{1,0:T(8,128)(2,1)}, u32[]{:S(2)}) copy-start(bf16[1024,256]{1,0:T(8,128)(2,1)} %constant.16.clone.mean_ref) | copy-start | bytes 1572868
  78.3 4.0 %copy-start.23 = (bf16[256,128]{1,0:T(8,128)(2,1)S(1)}, bf16[256,128]{1,0:T(8,128)(2,1)}, u32[]{:S(2)}) copy-start(bf16[256,128]{1,0:T(8,128)(2,1)} %constant.17.clone.copy_ref) | copy-start | bytes 196612

commit v2 on v1

--- a/solution.py
+++ b/solution.py
@@ -68,26 +68,34 @@
     inner = inner.reshape(-1)
     both = np.concatenate([lap.reshape(span * span, -1), adv.reshape(span * span, -1)], axis=1)
     plane_hi, plane_lo = high_low(both[inner])
-    plane = np.concatenate([plane_hi, plane_hi], axis=0)
-    plane_rest = plane_lo[:, EDGE * EDGE :]
     spread = np.kron(interp, interp)
     ghost_hi, ghost_lo = high_low(spread.T @ np.where(inner[:, None], 0.0, both))
-    ghost = np.concatenate([ghost_hi, ghost_lo, ghost_hi, np.zeros_like(ghost_hi)], axis=0)
     face_hi, face_lo = high_low(spread[inner].T)
-    face = np.concatenate([face_hi, face_lo, face_hi, np.zeros_like(face_hi)], axis=0)
-    mean = np.zeros((PB, EDGE, EDGE, PB, 4, PB, PB), np.float32)
-    for big_x in range(PB):
-        for y in range(EDGE):
-            for z in range(EDGE):
-                mean[big_x, y, z, z // RATIO, :, big_x, y // RATIO] = 1.0 / RATIO**3
-    mean = mean.reshape(PB * EDGE * EDGE, 256).astype(jnp.bfloat16)
+    mean = np.zeros((EDGE, EDGE, PB, 4, PB, PB), np.float32)
+    for y in range(EDGE):
+        for z in range(EDGE):
+            mean[y, z, z // RATIO, :, :, y // RATIO] = 1.0 / RATIO**3
     copy = np.zeros((4, 2, PB, 2, PB, 2, 4, PB, PB), np.float32)
     for q in range(4):
         for big_x in range(PB):
             for big_y in range(PB):
                 copy[q, :, big_x, :, big_y, 0, q, big_x, big_y] = 1.0
-    copy = copy.reshape(256, 128).astype(jnp.bfloat16)
-    return plane, plane_rest, ghost, face, mean, copy
+    table = np.zeros((4, 256, 512), jnp.bfloat16)
+    table[0] = plane_hi
+    table[1] = np.concatenate([ghost_hi, ghost_lo, ghost_hi, np.zeros_like(ghost_hi)], axis=0)
+    table[2, :, :256] = plane_lo[:, 256:]
+    table[2, :, 256:] = np.concatenate([face_hi, face_lo, face_hi, np.zeros_like(face_hi)], axis=0)
+    table[3, :, :256] = mean.reshape(256, 256)
+    table[3, :, 256:384] = copy.reshape(256, 128)
+    return table.reshape(1024, 512)
+
+
+PLANE = (pl.ds(0, 256), pl.ds(0, 512))
+GHOST = (pl.ds(256, 256), pl.ds(0, 512))
+REST = (pl.ds(512, 256), pl.ds(0, 256))
+FACE = (pl.ds(512, 256), pl.ds(256, 256))
+MEAN = (pl.ds(768, 256), pl.ds(0, 256))
+COPY = (pl.ds(768, 256), pl.ds(256, 128))
 
 
 def dot(left, right):
@@ -107,15 +115,13 @@
     return high, (values - high.astype(F32)).astype(BF16)
 
 
-def ring_field(coarse_ref, number_ref, left_ref, right_ref, q, x):
-    if x < 8:
-        return coarse_ref[q, x] if q < 4 else number_ref[x]
-    return right_ref[q, x - 8] if x < 12 else left_ref[q, x - 12]
-
-
-def y_kernel(coarse_ref, number_ref, left_ref, right_ref, low_ref, high_ref):
+def ring_field(first_ref, last_ref, left_ref, right_ref, q, x):
+    return (first_ref, last_ref, right_ref, left_ref)[x // 4][q, x % 4]
+
+
+def y_kernel(first_ref, last_ref, left_ref, right_ref, low_ref, high_ref):
     top = lax.broadcasted_iota(jnp.int32, (8, 128), 0) < 4
-    field = functools.partial(ring_field, coarse_ref, number_ref, left_ref, right_ref)
+    field = functools.partial(ring_field, first_ref, last_ref, left_ref, right_ref)
     for q in range(5):
         for pair in range(8):
             even, odd = field(q, 2 * pair), field(q, 2 * pair + 1)
@@ -125,10 +131,10 @@
 
 
 def z_kernel(
-    coarse_ref, number_ref, left_ref, right_ref, below_ref, above_ref, all_ref, low_ref, high_ref
+    first_ref, last_ref, left_ref, right_ref, below_ref, above_ref, all_ref, low_ref, high_ref
 ):
     top = lax.broadcasted_iota(jnp.int32, (8, 128), 0) < 4
-    field = functools.partial(ring_field, coarse_ref, number_ref, left_ref, right_ref)
+    field = functools.partial(ring_field, first_ref, last_ref, left_ref, right_ref)
     for q in range(5):
         for pair in range(8):
             at = pl.ds((q * 8 + pair) * 8, 8)
@@ -172,7 +178,19 @@
 
 
 def half_kernel(
-    all_ref, before_ref, after_ref, cells_ref, number_ref, mean_ref, pay_ref, half_ref, now_ref, cut_ref
+    all_ref,
+    before_ref,
+    after_ref,
+    cells_ref,
+    number_ref,
+    mean_ref,
+    sent_ref,
+    full_ref,
+    now_ref,
+    half_ref,
+    cut_ref,
+    pay_ref,
+    sem,
 ):
     lane40 = lax.broadcasted_iota(jnp.int32, (40, 128), 1)
     before, after = before_ref[...], after_ref[...]
@@ -245,9 +263,13 @@
         ]
     placed = cells_ref[pl.ds(16, HOSTS), pl.ds(0, 128)] >= 0
     pay_ref[pl.ds(FLAG_ROW, HOSTS, stride=SLOT_ROWS)] = jnp.where(placed, 1.0, 0.0)
-
-
-def full_kernel(coarse_ref, number_ref, half_ref, cells_ref, full_ref):
+    copy = pltpu.make_async_copy(pay_ref, sent_ref, sem)
+    copy.start()
+    full_step(now_ref, half_ref, cells_ref, full_ref)
+    copy.wait()
+
+
+def full_step(now_ref, half_ref, cells_ref, full_ref):
     lane = lax.broadcasted_iota(jnp.int32, (HOSTS, 128), 1)
     top = lax.broadcasted_iota(jnp.int32, (8, 128), 0) < 4
     cells = cells_ref[pl.ds(16, HOSTS), pl.ds(0, 128)]
@@ -262,7 +284,7 @@
 
     for x in range(8):
         keep = jnp.where(top, covered[(x // 4) * 2], covered[(x // 4) * 2 + 1]) == 0
-        number = number_ref[x]
+        number = now_ref[pl.ds((64 + x) * 16, 8), pl.ds(0, 128)]
         for q in range(4):
             center = sheet(q, x)
             laplace, advect = rate_parts(
@@ -273,7 +295,7 @@
                 WIND_COARSE,
             )
             done = 0.5 * (
-                coarse_ref[q, x]
+                now_ref[pl.ds((q * 16 + x) * 16, 8), pl.ds(0, 128)]
                 + center[:8, :128]
                 + number * laplace[:8, :128]
                 - advect[:8, :128]
@@ -281,7 +303,7 @@
             full_ref[q, x] = jnp.where(keep, done, 0.0)
 
 
-def put_means(back, full_ref, cells_ref, copy_ref, next_ref):
+def put_means(back, full_ref, cells_ref, table_ref, next_ref):
     even, odd = back[:, :128], back[:, 128:]
     values = jnp.concatenate(
         [even, pltpu.roll(even, 64, 1), odd, pltpu.roll(odd, 64, 1)], axis=0
@@ -289,7 +311,7 @@
     high = values.astype(BF16)
     low, lowest = split(values - high.astype(F32))
     parts = jnp.concatenate([high, low, lowest, jnp.zeros_like(high)], axis=0)
-    spread = dot_t(copy_ref[...], parts)
+    spread = dot_t(table_ref[COPY], parts)
     cells = cells_ref[pl.ds(8, 1)]
     row = lax.broadcasted_iota(jnp.int32, (256, 1), 0)
     corner = ((row >> 5) & 1) * 2 + ((row >> 2) & 1)
@@ -304,10 +326,10 @@
             next_ref[q, x] = full_ref[q, x] + added[at : at + 8]
 
 
-def plane_parts(field, plane_ref, rest_ref):
+def plane_parts(field, table_ref):
     high, low = split(field)
-    both = dot(high, plane_ref[pl.ds(0, 256)]) + dot(low, plane_ref[pl.ds(256, 256)])
-    return both[:, :256], both[:, 256:] + dot(high, rest_ref[...])
+    both = dot(high, table_ref[PLANE]) + dot(low, table_ref[PLANE])
+    return both[:, :256], both[:, 256:] + dot(high, table_ref[REST])
 
 
 def plus(left, right):
@@ -346,13 +368,17 @@
     ]
 
 
-def means(planes, mean_ref):
-    total = None
+def means(planes, table_ref):
+    sums = []
     for big_x in range(PB):
         group = planes[big_x * 4 : big_x * 4 + 4]
-        high, low = split((group[0] + group[1]) + (group[2] + group[3]))
-        weights = mean_ref[pl.ds(big_x * 256, 256)]
-        total = plus(total, dot(high, weights) + dot(low, weights))
+        sums.append((group[0] + group[1]) + (group[2] + group[3]))
+    high, low = split(jnp.concatenate(sums, axis=0))
+    every = dot(high, table_ref[MEAN]) + dot(low, table_ref[MEAN])
+    lane_x = (lax.broadcasted_iota(jnp.int32, (HOSTS, 256), 1) >> 2) & 3
+    total = plane(every, 0)
+    for big_x in range(1, PB):
+        total = jnp.where(lane_x == big_x, plane(every, big_x), total)
     return total
 
 
@@ -360,7 +386,7 @@
     return (lax.broadcasted_iota(jnp.int32, (HOSTS, 256), 1) >> 4) & 3
 
 
-def early_kernel(fine_ref, number_ref, plane_ref, rest_ref, mean_ref, route_ref, step_ref, back_ref, cells_ref):
+def early_kernel(fine_ref, number_ref, table_ref, route_ref, step_ref, back_ref, cells_ref):
     numbers = [number_ref[:, pl.ds(x * 256, 256)] for x in range(EDGE)]
     nothing = [None, None]
     back = jnp.zeros((HOSTS, 256), F32)
@@ -371,15 +397,15 @@
                 fine_ref[pl.ds((2 * x + side) * 4 + q, HOSTS, stride=128)] for side in range(2)
             ]
             planes.append(jnp.concatenate(sides, axis=1))
-        parts = plane_parts(jnp.concatenate(planes, axis=0), plane_ref, rest_ref)
+        parts = plane_parts(jnp.concatenate(planes, axis=0), table_ref)
         rate = rate_of(numbers, nothing + planes + nothing, *parts)
         half = [planes[x] + rate[x] for x in range(EDGE)]
-        parts = plane_parts(jnp.concatenate(half, axis=0), plane_ref, rest_ref)
+        parts = plane_parts(jnp.concatenate(half, axis=0), table_ref)
         rate = rate_of(numbers, nothing + half + nothing, *parts)
         done = [0.5 * (planes[x] + half[x] + rate[x]) for x in range(EDGE)]
         for x in range(EDGE):
             step_ref[pl.ds((q * EDGE + x) * HOSTS, HOSTS)] = done[x]
-        back = jnp.where(lane_of_q() == q, means(done, mean_ref), back)
+        back = jnp.where(lane_of_q() == q, means(done, table_ref), back)
     back_ref[...] = back
     lane = lax.broadcasted_iota(jnp.int32, (8, 256), 1)
     row = lax.broadcasted_iota(jnp.int32, (HOSTS, 256), 0)
@@ -396,7 +422,7 @@
     cells_ref[pl.ds(16, HOSTS)] = by_row
 
 
-def ghosts(block_ref, q, t, ghost_ref, face_ref):
+def ghosts(block_ref, q, t, table_ref):
     interp = interp_table(PB, RATIO)
     first_half = lax.broadcasted_iota(jnp.int32, (HOSTS, 128), 1) < 64
     coarse = []
@@ -413,29 +439,66 @@
             if interp[i, j] != 0.0:
                 total = plus(total, float(interp[i, j]) * coarse[j])
         (inner if 2 <= i < EDGE + 2 else outer).append(total)
-    sides = dot(jnp.concatenate(split(jnp.concatenate(inner, axis=0)), axis=1), ghost_ref[...])
-    faces = dot(jnp.concatenate(split(jnp.concatenate(outer, axis=0)), axis=1), face_ref[...])
+    sides = dot(jnp.concatenate(split(jnp.concatenate(inner, axis=0)), axis=1), table_ref[GHOST])
+    faces = dot(jnp.concatenate(split(jnp.concatenate(outer, axis=0)), axis=1), table_ref[FACE])
     return sides[:, :256], sides[:, 256:], [plane(faces, i) for i in range(4)]
 
 
-def ghost_part(block_ref, numbers, q, plane_ref, rest_ref, ghost_ref, face_ref):
-    laplace, advect, faces = ghosts(block_ref, q, 0, ghost_ref, face_ref)
+def ghost_part(block_ref, numbers, q, table_ref):
+    laplace, advect, faces = ghosts(block_ref, q, 0, table_ref)
     half = rate_of(numbers, faces[:2] + [None] * EDGE + faces[2:], laplace, advect)
-    laplace, advect, faces = ghosts(block_ref, q, 1, ghost_ref, face_ref)
-    parts = plane_parts(jnp.concatenate(half, axis=0), plane_ref, rest_ref)
+    laplace, advect, faces = ghosts(block_ref, q, 1, table_ref)
+    parts = plane_parts(jnp.concatenate(half, axis=0), table_ref)
     rate = rate_of(
         numbers, faces[:2] + half + faces[2:], parts[0] + laplace, parts[1] + advect
     )
     return [0.5 * (half[x] + rate[x]) for x in range(EDGE)]
 
 
-def late_kernel(
-    block_ref, step_ref, old_ref, number_ref, plane_ref, rest_ref, ghost_ref, face_ref, fine_ref
+def last_kernel(
+    got_ref,
+    sent_hbm,
+    step_hbm,
+    old_hbm,
+    number_hbm,
+    full_ref,
+    cells_ref,
+    table_ref,
+    fine_hbm,
+    next_ref,
+    sent_ref,
+    step_ref,
+    old_ref,
+    number_ref,
+    fine_ref,
+    sems,
 ):
+    copies = [
+        pltpu.make_async_copy(src, dst, sems.at[i])
+        for i, (src, dst) in enumerate(
+            (
+                (number_hbm, number_ref),
+                (step_hbm, step_ref),
+                (old_hbm, old_ref),
+                (sent_hbm, sent_ref),
+            )
+        )
+    ]
+    for copy in copies:
+        copy.start()
+
+    def got(row):
+        sides = [got_ref[pl.ds(row + side, HOSTS, stride=SLOT_ROWS)] for side in range(2)]
+        return jnp.concatenate(sides, axis=1)
+
+    placed = got_ref[pl.ds(FLAG_ROW, HOSTS, stride=SLOT_ROWS)] > 0.5
+    copies[0].wait()
     numbers = [number_ref[:, pl.ds(x * 256, 256)] for x in range(EDGE)]
-    placed = block_ref[pl.ds(FLAG_ROW, HOSTS, stride=SLOT_ROWS)] > 0.5
     for q in range(4):
-        added = ghost_part(block_ref, numbers, q, plane_ref, rest_ref, ghost_ref, face_ref)
+        added = ghost_part(got_ref, numbers, q, table_ref)
+        if q == 0:
+            copies[1].wait()
+            copies[2].wait()
         for x in range(EDGE):
             done = step_ref[pl.ds((q * EDGE + x) * HOSTS, HOSTS)] + added[x]
             for side in range(2):
@@ -443,43 +506,31 @@
                 fine_ref[at] = jnp.where(
                     placed, done[:, side * 128 : side * 128 + 128], old_ref[at]
                 )
-
-
-def back_kernel(
-    sent_ref,
-    got_ref,
-    full_ref,
-    cells_ref,
-    copy_ref,
-    plane_ref,
-    rest_ref,
-    ghost_ref,
-    face_ref,
-    mean_ref,
-    next_ref,
-):
-    def got(row):
-        sides = [got_ref[pl.ds(row + side, HOSTS, stride=SLOT_ROWS)] for side in range(2)]
-        return jnp.concatenate(sides, axis=1)
-
+    out = pltpu.make_async_copy(fine_ref, fine_hbm, sems.at[4])
+    out.start()
+    copies[3].wait()
     numbers = [got(NUMBER_ROW + 2 * x) for x in range(EDGE)]
     back = jnp.zeros((HOSTS, 256), F32)
     for q in range(4):
-        added = ghost_part(sent_ref, numbers, q, plane_ref, rest_ref, ghost_ref, face_ref)
-        back = jnp.where(lane_of_q() == q, means(added, mean_ref), back)
-    put_means(back + got(MEAN_ROW), full_ref, cells_ref, copy_ref, next_ref)
-
-
-def call(kernel, operands, outs, smem=(), scratch=(), flops=1000000, name=None):
+        added = ghost_part(sent_ref, numbers, q, table_ref)
+        back = jnp.where(lane_of_q() == q, means(added, table_ref), back)
+    put_means(back + got(MEAN_ROW), full_ref, cells_ref, table_ref, next_ref)
+    out.wait()
+
+
+def call(kernel, operands, outs, smem=(), hbm=(), hbm_outs=(), scratch=(), flops=10**6, name=None):
     vmem = pl.BlockSpec(memory_space=pltpu.VMEM)
     scalar = pl.BlockSpec(memory_space=pltpu.SMEM)
+    far = pl.BlockSpec(memory_space=pltpu.HBM)
     moved = sum(int(np.prod(o.shape)) * o.dtype.itemsize for o in operands)
     return pl.pallas_call(
         kernel,
         out_shape=tuple(jax.ShapeDtypeStruct(shape, dtype) for shape, dtype in outs),
-        in_specs=[scalar if i in smem else vmem for i in range(len(operands))],
-        out_specs=tuple(vmem for _ in outs),
-        scratch_shapes=[pltpu.VMEM(shape, F32) for shape in scratch],
+        in_specs=[
+            scalar if i in smem else far if i in hbm else vmem for i in range(len(operands))
+        ],
+        out_specs=tuple(far if i in hbm_outs else vmem for i in range(len(outs))),
+        scratch_shapes=list(scratch),
         compiler_params=pltpu.CompilerParams(vmem_limit_bytes=LIMIT * 1024 * 1024),
         cost_estimate=pl.CostEstimate(flops=flops, bytes_accessed=moved, transcendentals=0),
         name=name,
@@ -487,7 +538,7 @@
 
 
 def shards(coarse_state, diffusion_number, route_cell, fine_state, fine_diffusion):
-    flat, rest, ghost, face, mean, copy = (jnp.asarray(table) for table in tables())
+    table = jnp.asarray(tables())
     fine_rows = fine_state.reshape(HOSTS, 4, 32, 128).transpose(0, 2, 1, 3).reshape(2048, 128)
     fine_numbers = fine_diffusion.reshape(HOSTS, EDGE**3)
 
@@ -502,8 +553,8 @@
         return lax.ppermute(high, axis, up), from_above
 
     fields = jnp.concatenate([coarse_state, diffusion_number[None]], axis=0)
-    left, right = exchange(fields[:, :4], fields[:, 4:], "gx", True)
-    own = (coarse_state, diffusion_number, left, right)
+    first, last = fields[:, :4], fields[:, 4:]
+    own = (first, last) + exchange(first, last, "gx", True)
     low, high = call(y_kernel, own, [((320, 128), F32)] * 2, name="y_messages")
     below, above = exchange(low, high, "gy", True)
     everything, low, high = call(
@@ -515,41 +566,46 @@
     before, after = exchange(low, high, "gz", False)
     step, early_means, cells = call(
         early_kernel,
-        (fine_rows, fine_numbers, flat, rest, mean, route_cell.reshape(HOSTS)),
+        (fine_rows, fine_numbers, table, route_cell.reshape(HOSTS)),
         [((1024, 256), F32), ((HOSTS, 256), F32), ((32, 256), jnp.int32)],
-        smem=(5,),
+        smem=(3,),
         flops=10**9,
         name="fine_early",
     )
-    sent, half = call(
+    payload = (HOSTS * SLOT_ROWS, 128)
+    sent, full = call(
         half_kernel,
         (everything, before, after, cells, fine_numbers, early_means),
-        [((HOSTS * SLOT_ROWS, 128), F32), ((1024, 256), F32)],
-        scratch=[(1280, 256), (512, 128)],
+        [(payload, F32), ((4, 8, 8, 128), F32)],
+        hbm_outs=(0,),
+        scratch=[
+            pltpu.VMEM((1280, 256), F32),
+            pltpu.VMEM((1024, 256), F32),
+            pltpu.VMEM((512, 128), F32),
+            pltpu.VMEM(payload, F32),
+            pltpu.SemaphoreType.DMA,
+        ],
         name="half_step",
     )
     got = lax.all_to_all(
         sent.reshape(HOSTS, SLOT_ROWS, 1, 128), "gz", split_axis=0, concat_axis=0, tiled=True
-    ).reshape(HOSTS * SLOT_ROWS, 128)
-    (full,) = call(
-        full_kernel,
-        (coarse_state, diffusion_number, half, cells),
-        [((4, 8, 8, 128), F32)],
-        name="coarse_full",
-    )
-    (coarse_next,) = call(
-        back_kernel,
-        (sent, got, full, cells, copy, flat, rest, ghost, face, mean),
-        [((4, 8, 8, 128), F32)],
+    ).reshape(payload)
+    fine_done, coarse_next = call(
+        last_kernel,
+        (got, sent, step, fine_rows, fine_numbers, full, cells, table),
+        [((2048, 128), F32), ((4, 8, 8, 128), F32)],
+        hbm=(1, 2, 3, 4),
+        hbm_outs=(0,),
+        scratch=[
+            pltpu.VMEM(payload, F32),
+            pltpu.VMEM((1024, 256), F32),
+            pltpu.VMEM((2048, 128), F32),
+            pltpu.VMEM((HOSTS, 4096), F32),
+            pltpu.VMEM((2048, 128), F32),
+            pltpu.SemaphoreType.DMA((5,)),
+        ],
         flops=10**9,
-        name="coarse_next",
-    )
-    (fine_done,) = call(
-        late_kernel,
-        (got, step, fine_rows, fine_numbers, flat, rest, ghost, face),
-        [((2048, 128), F32)],
-        flops=10**9,
-        name="fine_next",
+        name="last_step",
     )
     fine_next = (
         fine_done.reshape(HOSTS, 32, 4, 128).transpose(0, 2, 1, 3).reshape(fine_state.shape)

time: 87.3 us -> 81.1 us (0.929)
  the two profiles are of different devices: /device:TPU:22 before, /device:TPU:16 now
where the time goes in v2:
time: 81.1 us; the launch traced here: 80.7 us
  blocking collectives  38.3 us (47%)
  starting transfers between devices  16 us (20%)
  Pallas kernels  14.8 us (18%)
  waiting for transfers between devices  7.85 us (10%)
  local copies, waits for them, and re-layouts  1.87 us (2%)
  other arithmetic  1.01 us (1%)
  between operations  0.94 us (1%)
    all_to_all x1, blocking collectives, shards(): lax.all_to_all(sent.reshape(HOSTS, SLOT_ROWS, 1, 128), 'gz', split_axis=0...  38.3 us
    pallas_call x5, Pallas kernels, call(): pl.pallas_call(kernel, out_shape=tuple((jax.ShapeDtypeStruct(shape, dtype...  14.8 us
    ppermute x2, waiting for transfers between devices, exchange(): return (from_below, lax.ppermute(low, axis, down))  6.2 us
    ppermute x2, starting transfers between devices, exchange(): from_below = lax.ppermute(high, axis, up)  5.32 us
    ppermute x2, starting transfers between devices, exchange(): return (from_below, lax.ppermute(low, axis, down))  5.07 us
    ppermute x1, starting transfers between devices, exchange(): return (lax.ppermute(high, axis, up), from_above)  4.28 us
    unnamed x10, local copies, waits for them, and re-layouts  1.87 us
    ppermute x2, waiting for transfers between devices, exchange(): from_below = lax.ppermute(high, axis, up)  1.65 us
  transfers between devices with their start and end apart: 6, of which 4 were waited for; matrix products, arithmetic and copies ran while one was open for 0% of the time, Pallas kernels for 6%

profile of v2, /device:TPU:16, one launch (start us, length us, event | category | flops | bytes accessed | tf_op | source)
XLA Modules:
  0.0 80.7 jit_solution(15325525981118938553)
XLA Ops:
  0.6 0.0 copy-start.1
  0.6 1.0 %pad_maximum_fusion = (f32[5,4,8,128]{3,2,1,0:T(8,128)S(1)}, f32[5,4,8,128]{3,2,1,0:T(8,128)S(1)}) fusion(f32[1,8,8,128]{3,2,1,0:T(8,128)} %bitcast.23, f32[4,8,8,128]{3,2,1,0:T(8,128)} %param.6), kind=kLoop, calls=%fused_computation.3 | loop fusion | flops 40960 | bytes 327680 | tf_op jit(solution)/shard_map/concatenate | solution.py:555
  1.6 3.4 %collective-permute-start = (f32[5,4,8,128]{3,2,1,0:T(8,128)S(1)}, f32[5,4,8,128]{3,2,1,0:T(8,128)S(1)}, u32[]{:S(2)}, u32[]{:S(2)}) collective-permute-start(f32[5,4,8,128]{3,2,1,0:T(8,128)S(1)} %get-tuple-element.26.last_ref), channel_id=1, source_target_pairs={{0,128},{128,256},{256,384},{1,129},{129,257},{257,385},{2,130},{1... | collective-permute-start | bytes 245768 | tf_op jit(solution)/shard_map/ppermute | solution.py:550
  5.1 1.3 %collective-permute-start.1 = (f32[5,4,8,128]{3,2,1,0:T(8,128)S(1)}, f32[5,4,8,128]{3,2,1,0:T(8,128)S(1)}, u32[]{:S(2)}, u32[]{:S(2)}) collective-permute-start(f32[5,4,8,128]{3,2,1,0:T(8,128)S(1)} %get-tuple-element.27.first_ref), channel_id=1, source_target_pairs={{128,0},{256,128},{384,256},{129,1},{257,129},{385,257},{130,2},{2... | collective-permute-start | bytes 245768 | tf_op jit(solution)/shard_map/ppermute | solution.py:551
  6.4 0.7 collective-permute-done.left_ref
  7.1 4.3 %collective-permute-done.1.right_ref = f32[5,4,8,128]{3,2,1,0:T(8,128)S(1)} collective-permute-done((f32[5,4,8,128]{3,2,1,0:T(8,128)S(1)}, f32[5,4,8,128]{3,2,1,0:T(8,128)S(1)}, u32[]{:S(2)}, u32[]{:S(2)}) %collective-permute-start.1) | collective-permute-done | bytes 81952 | tf_op jit(solution)/shard_map/ppermute | solution.py:551
  11.4 1.9 %collective-permute-start.2 = (f32[320,128]{1,0:T(8,128)S(1)}, f32[320,128]{1,0:T(8,128)S(1)}, u32[]{:S(2)}, u32[]{:S(2)}) collective-permute-start(f32[320,128]{1,0:T(8,128)S(1)} %get-tuple-element.14), channel_id=1, source_target_pairs={{0,16},{16,32},{32,48},{48,64},{64,80},{80,96},{96,112},{1,17},{17... | collective-permute-start | bytes 491528 | tf_op jit(solution)/shard_map/ppermute | solution.py:550
  13.4 0.0 copy-start
  13.4 3.8 %collective-permute-start.3 = (f32[320,128]{1,0:T(8,128)S(1)}, f32[320,128]{1,0:T(8,128)S(1)}, u32[]{:S(2)}, u32[]{:S(2)}) collective-permute-start(f32[320,128]{1,0:T(8,128)S(1)} %get-tuple-element.15), channel_id=1, source_target_pairs={{16,0},{32,16},{48,32},{64,48},{80,64},{96,80},{112,96},{17,1},{33... | collective-permute-start | bytes 491528 | tf_op jit(solution)/shard_map/ppermute | solution.py:551
  17.1 0.9 %collective-permute-done.2.below_ref = f32[320,128]{1,0:T(8,128)S(1)} collective-permute-done((f32[320,128]{1,0:T(8,128)S(1)}, f32[320,128]{1,0:T(8,128)S(1)}, u32[]{:S(2)}, u32[]{:S(2)}) %collective-permute-start.2) | collective-permute-done | bytes 163872 | tf_op jit(solution)/shard_map/ppermute | solution.py:550
  18.1 1.9 %collective-permute-done.3.above_ref = f32[320,128]{1,0:T(8,128)S(1)} collective-permute-done((f32[320,128]{1,0:T(8,128)S(1)}, f32[320,128]{1,0:T(8,128)S(1)}, u32[]{:S(2)}, u32[]{:S(2)}) %collective-permute-start.3) | collective-permute-done | bytes 163872 | tf_op jit(solution)/shard_map/ppermute | solution.py:551
  20.0 0.4 z_messages.1
  20.4 4.3 %collective-permute-start.4 = (f32[40,128]{1,0:T(8,128)S(1)}, f32[40,128]{1,0:T(8,128)S(1)}, u32[]{:S(2)}, u32[]{:S(2)}) collective-permute-start(f32[40,128]{1,0:T(8,128)S(1)} %get-tuple-element.17), channel_id=1, source_target_pairs={{0,1},{1,2},{2,3},{3,4},{4,5},{5,6},{6,7},{7,8},{8,9},{9,10},{10,1... | collective-permute-start | bytes 61448 | tf_op jit(solution)/shard_map/ppermute | solution.py:553
  24.6 1.3 %collective-permute-start.5 = (f32[40,128]{1,0:T(8,128)S(1)}, f32[40,128]{1,0:T(8,128)S(1)}, u32[]{:S(2)}, u32[]{:S(2)}) collective-permute-start(f32[40,128]{1,0:T(8,128)S(1)} %get-tuple-element.18), channel_id=1, source_target_pairs={{1,0},{2,1},{3,2},{4,3},{5,4},{6,5},{7,6},{8,7},{9,8},{10,9},{11,1... | collective-permute-start | bytes 61448 | tf_op jit(solution)/shard_map/ppermute | solution.py:552
  25.9 0.0 copy-start.4
  26.0 0.0 copy-done.1
  26.0 0.0 copy-done
  26.0 0.6 copy-done.4
  26.6 0.0 copy-start.2
  26.6 1.2 %copy-done.2 = bf16[1024,512]{1,0:T(8,128)(2,1)S(1)} copy-done((bf16[1024,512]{1,0:T(8,128)(2,1)S(1)}, bf16[1024,512]{1,0:T(8,128)(2,1)}, u32[]{:S(2)}) %copy-start.2) | copy-done | bytes 1048600
  27.8 4.5 %fine_early.1 = (f32[1024,256]{1,0:T(8,128)S(1)}, f32[16,256]{1,0:T(8,128)S(1)}, s32[32,256]{1,0:T(8,128)S(1)}) custom-call(f32[2048,128]{1,0:T(8,128)S(1)} %bitcast.20, f32[16,4096]{1,0:T(8,128)S(1)} %bitcast.17, bf16[1024,512]{1,0:T(8,128)(2,1)S(1)} %copy-done.2, s32[16]{0:T(128)S(1)} %bitcast.22), custom_call_target="tpu_custom_call" | custom-call | flops 1000000000 | bytes 2359360 | tf_op jit(solution)/shard_map/fine_early/pallas_call | solution.py:526
  32.4 0.0 collective-permute-done.4.before_ref
  32.4 0.0 collective-permute-done.5.after_ref
  32.4 0.0 copy-start.3
  32.4 2.6 %half_step.1 = (f32[1072,128]{1,0:T(8,128)S(1)}, f32[4,8,8,128]{3,2,1,0:T(8,128)S(1)}) custom-call(f32[1280,128]{1,0:T(8,128)S(1)} %get-tuple-element.16.all_ref, f32[40,128]{1,0:T(8,128)S(1)} %collective-permute-done.4.before_ref, f32[40,128]{1,0:T(8,128)S(1)} %collective-permute-done.5.after_ref, s32[32,256]{1,0:T(8,128)S(1)} %get-tuple-element.19.cells_ref, ...), custom_call_target="tpu_custom_call" | custom-call | flops 1000000 | bytes 1007616 | tf_op jit(solution)/shard_map/half_step/pallas_call | solution.py:526
  35.1 38.3 %all_to_all.5 = f32[16,67,1,128]{3,2,1,0:T(1,128)S(1)} all-to-all(f32[16,67,1,128]{3,2,1,0:T(1,128)S(1)} %bitcast.15), channel_id=1, replica_groups=mesh['gx'=4,'gy'=8,'gz'=16] {'gz'}, dimensions={0} | all-to-all | bytes 1097728 | tf_op jit(solution)/shard_map/all_to_all | solution.py:590
  73.4 0.0 copy-done.3
  73.4 7.2 %last_step.1 = (f32[2048,128]{1,0:T(8,128)}, f32[4,8,8,128]{3,2,1,0:T(8,128)}) custom-call(f32[1072,128]{1,0:T(8,128)S(1)} %bitcast.16, f32[1072,128]{1,0:T(8,128)S(1)} %get-tuple-element.21.sent_hbm, f32[1024,256]{1,0:T(8,128)S(1)} %get-tuple-element.22.step_hbm, f32[2048,128]{1,0:T(8,128)S(1)} %bitcast.21, f32[16,4096]{1,0:T(8,128)S(1)} %bitcast.19, ...), custom_call_target="tpu_custom_call" | custom-call | flops 1000000000 | bytes 4669440 | tf_op jit(solution)/shard_map/last_step/pallas_call | solution.py:526
  (1 shorter events, 0.0 us)
Async XLA Ops:
  0.6 25.3 %copy-start.1 = (f32[1,1,1,16,4,4096]{5,4,3,2,1,0:T(4,128)S(1)}, f32[1,1,1,16,4,4096]{5,4,3,2,1,0:T(4,128)}, u32[]{:S(2)}) copy-start(f32[1,1,1,16,4,4096]{5,4,3,2,1,0:T(4,128)} %param.9) | copy-start | bytes 3145732
  1.6 5.4 %collective-permute-start = (f32[5,4,8,128]{3,2,1,0:T(8,128)S(1)}, f32[5,4,8,128]{3,2,1,0:T(8,128)S(1)}, u32[]{:S(2)}, u32[]{:S(2)}) collective-permute-start(f32[5,4,8,128]{3,2,1,0:T(8,128)S(1)} %get-tuple-element.26.last_ref), channel_id=1, source_target_pairs={{0,128},{128,256},{256,384},{1,129},{129,257},{257,385},{2,130},{1... | collective-permute-start | bytes 245768 | tf_op jit(solution)/shard_map/ppermute | solution.py:550
  5.1 6.3 %collective-permute-start.1 = (f32[5,4,8,128]{3,2,1,0:T(8,128)S(1)}, f32[5,4,8,128]{3,2,1,0:T(8,128)S(1)}, u32[]{:S(2)}, u32[]{:S(2)}) collective-permute-start(f32[5,4,8,128]{3,2,1,0:T(8,128)S(1)} %get-tuple-element.27.first_ref), channel_id=1, source_target_pairs={{128,0},{256,128},{384,256},{129,1},{257,129},{385,257},{130,2},{2... | collective-permute-start | bytes 245768 | tf_op jit(solution)/shard_map/ppermute | solution.py:551
  11.4 6.6 %collective-permute-start.2 = (f32[320,128]{1,0:T(8,128)S(1)}, f32[320,128]{1,0:T(8,128)S(1)}, u32[]{:S(2)}, u32[]{:S(2)}) collective-permute-start(f32[320,128]{1,0:T(8,128)S(1)} %get-tuple-element.14), channel_id=1, source_target_pairs={{0,16},{16,32},{32,48},{48,64},{64,80},{80,96},{96,112},{1,17},{17... | collective-permute-start | bytes 491528 | tf_op jit(solution)/shard_map/ppermute | solution.py:550
  13.4 12.6 %copy-start = (f32[1,1,1,16,4096]{4,3,2,1,0:T(8,128)S(1)}, f32[1,1,1,16,4096]{4,3,2,1,0:T(8,128)}, u32[]{:S(2)}) copy-start(f32[1,1,1,16,4096]{4,3,2,1,0:T(8,128)} %param.10) | copy-start | bytes 786436
  13.4 6.6 %collective-permute-start.3 = (f32[320,128]{1,0:T(8,128)S(1)}, f32[320,128]{1,0:T(8,128)S(1)}, u32[]{:S(2)}, u32[]{:S(2)}) collective-permute-start(f32[320,128]{1,0:T(8,128)S(1)} %get-tuple-element.15), channel_id=1, source_target_pairs={{16,0},{32,16},{48,32},{64,48},{80,64},{96,80},{112,96},{17,1},{33... | collective-permute-start | bytes 491528 | tf_op jit(solution)/shard_map/ppermute | solution.py:551
  20.4 12.0 %collective-permute-start.4 = (f32[40,128]{1,0:T(8,128)S(1)}, f32[40,128]{1,0:T(8,128)S(1)}, u32[]{:S(2)}, u32[]{:S(2)}) collective-permute-start(f32[40,128]{1,0:T(8,128)S(1)} %get-tuple-element.17), channel_id=1, source_target_pairs={{0,1},{1,2},{2,3},{3,4},{4,5},{5,6},{6,7},{7,8},{8,9},{9,10},{10,1... | collective-permute-start | bytes 61448 | tf_op jit(solution)/shard_map/ppermute | solution.py:553
  24.6 7.8 %collective-permute-start.5 = (f32[40,128]{1,0:T(8,128)S(1)}, f32[40,128]{1,0:T(8,128)S(1)}, u32[]{:S(2)}, u32[]{:S(2)}) collective-permute-start(f32[40,128]{1,0:T(8,128)S(1)} %get-tuple-element.18), channel_id=1, source_target_pairs={{1,0},{2,1},{3,2},{4,3},{5,4},{6,5},{7,6},{8,7},{9,8},{10,9},{11,1... | collective-permute-start | bytes 61448 | tf_op jit(solution)/shard_map/ppermute | solution.py:552
  25.9 0.7 copy-start.4
  26.6 1.2 %copy-start.2 = (bf16[1024,512]{1,0:T(8,128)(2,1)S(1)}, bf16[1024,512]{1,0:T(8,128)(2,1)}, u32[]{:S(2)}) copy-start(bf16[1024,512]{1,0:T(8,128)(2,1)} %constant.2.clone.table_ref) | copy-start | bytes 3145732
  32.4 41.0 %copy-start.3 = (bf16[1024,512]{1,0:T(8,128)(2,1)S(1)}, bf16[1024,512]{1,0:T(8,128)(2,1)}, u32[]{:S(2)}) copy-start(bf16[1024,512]{1,0:T(8,128)(2,1)} %constant.2.clone.table_ref) | copy-start | bytes 3145732

commit v3 on v2

--- a/solution.py
+++ b/solution.py
@@ -19,7 +19,8 @@
 FLAG_ROW = 66
 SLOT_ROWS = 67
 WIND_COARSE = (0.05, 0.03, 0.07)
-WIND_FINE = tuple(RATIO * speed for speed in WIND_COARSE)
+WIND_PARTS = (5.0, 3.0, 7.0)
+ADVECT_UNIT = RATIO * 0.01 / 12.0
 F32 = jnp.float32
 BF16 = jnp.bfloat16
 
@@ -58,16 +59,15 @@
         for z in range(EDGE):
             col = y * EDGE + z
             lap[y + 2, z + 2, col] = -6.0
-            for dy, dz, wind in ((1, 0, WIND_FINE[1]), (0, 1, WIND_FINE[2])):
+            for dy, dz, wind in ((1, 0, WIND_PARTS[1]), (0, 1, WIND_PARTS[2])):
                 for sign in (1, -1):
                     lap[y + 2 + sign * dy, z + 2 + sign * dz, col] += 1.0
-                    adv[y + 2 + sign * dy, z + 2 + sign * dz, col] += sign * 8.0 * wind / 12.0
-                    adv[y + 2 + sign * 2 * dy, z + 2 + sign * 2 * dz, col] -= sign * wind / 12.0
+                    adv[y + 2 + sign * dy, z + 2 + sign * dz, col] += sign * 8.0 * wind
+                    adv[y + 2 + sign * 2 * dy, z + 2 + sign * 2 * dz, col] -= sign * wind
     inner = np.zeros((span, span), bool)
     inner[2:-2, 2:-2] = True
     inner = inner.reshape(-1)
     both = np.concatenate([lap.reshape(span * span, -1), adv.reshape(span * span, -1)], axis=1)
-    plane_hi, plane_lo = high_low(both[inner])
     spread = np.kron(interp, interp)
     ghost_hi, ghost_lo = high_low(spread.T @ np.where(inner[:, None], 0.0, both))
     face_hi, face_lo = high_low(spread[inner].T)
@@ -80,22 +80,21 @@
         for big_x in range(PB):
             for big_y in range(PB):
                 copy[q, :, big_x, :, big_y, 0, q, big_x, big_y] = 1.0
-    table = np.zeros((4, 256, 512), jnp.bfloat16)
-    table[0] = plane_hi
-    table[1] = np.concatenate([ghost_hi, ghost_lo, ghost_hi, np.zeros_like(ghost_hi)], axis=0)
-    table[2, :, :256] = plane_lo[:, 256:]
-    table[2, :, 256:] = np.concatenate([face_hi, face_lo, face_hi, np.zeros_like(face_hi)], axis=0)
+    table = np.zeros((5, 256, 512), jnp.bfloat16)
+    table[0] = table[1] = both[inner]
+    table[2] = np.concatenate([ghost_hi, ghost_lo, ghost_hi, np.zeros_like(ghost_hi)], axis=0)
     table[3, :, :256] = mean.reshape(256, 256)
-    table[3, :, 256:384] = copy.reshape(256, 128)
-    return table.reshape(1024, 512)
-
-
-PLANE = (pl.ds(0, 256), pl.ds(0, 512))
-GHOST = (pl.ds(256, 256), pl.ds(0, 512))
-REST = (pl.ds(512, 256), pl.ds(0, 256))
-FACE = (pl.ds(512, 256), pl.ds(256, 256))
+    table[3, :, 256:] = np.concatenate([face_hi, face_lo, face_hi, np.zeros_like(face_hi)], axis=0)
+    table[4, :, :128] = copy.reshape(256, 128)
+    return table.reshape(1280, 512)
+
+
+PLANES = (pl.ds(0, 512), pl.ds(0, 512))
+GHOST = (pl.ds(512, 256), pl.ds(0, 512))
+PLANES_AND_GHOST = (pl.ds(0, 768), pl.ds(0, 512))
 MEAN = (pl.ds(768, 256), pl.ds(0, 256))
-COPY = (pl.ds(768, 256), pl.ds(256, 128))
+FACE = (pl.ds(768, 256), pl.ds(256, 256))
+COPY = (pl.ds(1024, 256), pl.ds(0, 128))
 
 
 def dot(left, right):
@@ -115,30 +114,66 @@
     return high, (values - high.astype(F32)).astype(BF16)
 
 
-def ring_field(first_ref, last_ref, left_ref, right_ref, q, x):
-    return (first_ref, last_ref, right_ref, left_ref)[x // 4][q, x % 4]
-
-
-def y_kernel(first_ref, last_ref, left_ref, right_ref, low_ref, high_ref):
+def is_even(axis):
+    return lax.axis_index(axis) % 2 == 0
+
+
+def x_kernel(coarse_hbm, number_hbm, inner_ref, outer_ref, sems):
+    place = jnp.where(is_even("gx"), 4, 0)
+    copies = []
+    for i, ref in enumerate((outer_ref, inner_ref)):
+        at = pl.ds(place if i == 0 else 4 - place, 4)
+        copies.append(
+            pltpu.make_async_copy(coarse_hbm.at[:, at], ref.at[pl.ds(0, 4)], sems.at[2 * i])
+        )
+        copies.append(pltpu.make_async_copy(number_hbm.at[at], ref.at[4], sems.at[2 * i + 1]))
+    for copy in copies:
+        copy.start()
+    for copy in copies:
+        copy.wait()
+
+
+def ring_field(inner_ref, outer_ref, far_inner_ref, far_outer_ref, q, x):
+    refs = (inner_ref, outer_ref, far_outer_ref, far_inner_ref)
+    turned = (outer_ref, inner_ref, far_inner_ref, far_outer_ref)
+    even = jnp.broadcast_to(is_even("gx"), (8, 128))
+    return jnp.where(even, refs[x // 4][q, x % 4], turned[x // 4][q, x % 4])
+
+
+def y_kernel(inner_ref, outer_ref, far_inner_ref, far_outer_ref, done_hbm, low_ref, high_ref):
     top = lax.broadcasted_iota(jnp.int32, (8, 128), 0) < 4
-    field = functools.partial(ring_field, first_ref, last_ref, left_ref, right_ref)
+    even_y = jnp.broadcast_to(is_even("gy"), (8, 128))
+    field = functools.partial(ring_field, inner_ref, outer_ref, far_inner_ref, far_outer_ref)
     for q in range(5):
         for pair in range(8):
             even, odd = field(q, 2 * pair), field(q, 2 * pair + 1)
             at = pl.ds((q * 8 + pair) * 8, 8)
-            low_ref[at] = jnp.where(top, even, pltpu.roll(odd, 4, 0))
-            high_ref[at] = jnp.where(top, pltpu.roll(even, 4, 0), odd)
+            low = jnp.where(top, even, pltpu.roll(odd, 4, 0))
+            high = jnp.where(top, pltpu.roll(even, 4, 0), odd)
+            low_ref[at] = jnp.where(even_y, low, high)
+            high_ref[at] = jnp.where(even_y, high, low)
 
 
 def z_kernel(
-    first_ref, last_ref, left_ref, right_ref, below_ref, above_ref, all_ref, low_ref, high_ref
+    inner_ref,
+    outer_ref,
+    far_inner_ref,
+    far_outer_ref,
+    far_low_ref,
+    far_high_ref,
+    done_hbm,
+    all_ref,
+    low_ref,
+    high_ref,
 ):
     top = lax.broadcasted_iota(jnp.int32, (8, 128), 0) < 4
-    field = functools.partial(ring_field, first_ref, last_ref, left_ref, right_ref)
+    even_y = jnp.broadcast_to(is_even("gy"), (8, 128))
+    field = functools.partial(ring_field, inner_ref, outer_ref, far_inner_ref, far_outer_ref)
     for q in range(5):
         for pair in range(8):
             at = pl.ds((q * 8 + pair) * 8, 8)
-            below, above = below_ref[at], above_ref[at]
+            below = jnp.where(even_y, far_low_ref[at], far_high_ref[at])
+            above = jnp.where(even_y, far_high_ref[at], far_low_ref[at])
             row = (q * 16 + 2 * pair) * 16
             all_ref[pl.ds(row, 8)] = field(q, 2 * pair)
             all_ref[pl.ds(row + 8, 8)] = jnp.where(top, above, pltpu.roll(below, 4, 0))
@@ -152,8 +187,9 @@
         low = jnp.where(group == g, pltpu.roll(rows, 4 * g, 1) if g else rows, low)
         shift = (4 * g + 4) % 128
         high = jnp.where(group == g, pltpu.roll(rows, shift, 1) if shift else rows, high)
-    low_ref[...] = low
-    high_ref[...] = high
+    even_z = jnp.broadcast_to(is_even("gz"), (40, 128))
+    low_ref[...] = jnp.where(even_z, low, high)
+    high_ref[...] = jnp.where(even_z, high, low)
 
 
 def rate_parts(center, x_near, x_far, y_axis, wind):
@@ -179,11 +215,12 @@
 
 def half_kernel(
     all_ref,
-    before_ref,
-    after_ref,
+    far_low_ref,
+    far_high_ref,
     cells_ref,
     number_ref,
     mean_ref,
+    more_ref,
     sent_ref,
     full_ref,
     now_ref,
@@ -193,7 +230,9 @@
     sem,
 ):
     lane40 = lax.broadcasted_iota(jnp.int32, (40, 128), 1)
-    before, after = before_ref[...], after_ref[...]
+    even_z = jnp.broadcast_to(is_even("gz"), (40, 128))
+    before = jnp.where(even_z, far_low_ref[...], far_high_ref[...])
+    after = jnp.where(even_z, far_high_ref[...], far_low_ref[...])
     for g in range(32):
         ahead = pltpu.roll(after, (128 - 4 * g) % 128, 1) if g else after
         shift = (124 - 4 * g) % 128
@@ -258,9 +297,9 @@
             :, pl.ds(column * 128, 128)
         ]
     for side in range(2):
-        pay_ref[pl.ds(MEAN_ROW + side, HOSTS, stride=SLOT_ROWS)] = mean_ref[
-            :, pl.ds(side * 128, 128)
-        ]
+        pay_ref[pl.ds(MEAN_ROW + side, HOSTS, stride=SLOT_ROWS)] = (
+            mean_ref[:, pl.ds(side * 128, 128)] + more_ref[:, pl.ds(side * 128, 128)]
+        )
     placed = cells_ref[pl.ds(16, HOSTS), pl.ds(0, 128)] >= 0
     pay_ref[pl.ds(FLAG_ROW, HOSTS, stride=SLOT_ROWS)] = jnp.where(placed, 1.0, 0.0)
     copy = pltpu.make_async_copy(pay_ref, sent_ref, sem)
@@ -327,9 +366,8 @@
 
 
 def plane_parts(field, table_ref):
-    high, low = split(field)
-    both = dot(high, table_ref[PLANE]) + dot(low, table_ref[PLANE])
-    return both[:, :256], both[:, 256:] + dot(high, table_ref[REST])
+    both = dot(jnp.concatenate(split(field), axis=1), table_ref[PLANES])
+    return both[:, :256], both[:, 256:]
 
 
 def plus(left, right):
@@ -350,8 +388,8 @@
         near = minus(padded[x + 1], padded[x - 1])
         far = minus(padded[x + 2], padded[x - 2])
         laplace.append(plus(padded[x + 1], padded[x - 1]))
-        near = None if near is None else (8.0 * WIND_FINE[0] / 12.0) * near
-        far = None if far is None else (WIND_FINE[0] / 12.0) * far
+        near = None if near is None else (8.0 * WIND_PARTS[0]) * near
+        far = None if far is None else WIND_PARTS[0] * far
         advect.append(minus(near, far))
     return laplace, advect
 
@@ -363,7 +401,8 @@
 def rate_of(numbers, padded, laplace, advect):
     x_laplace, x_advect = x_parts(padded)
     return [
-        numbers[x] * plus(x_laplace[x], plane(laplace, x)) - plus(x_advect[x], plane(advect, x))
+        numbers[x] * plus(x_laplace[x], plane(laplace, x))
+        - ADVECT_UNIT * plus(x_advect[x], plane(advect, x))
         for x in range(EDGE)
     ]
 
@@ -386,11 +425,11 @@
     return (lax.broadcasted_iota(jnp.int32, (HOSTS, 256), 1) >> 4) & 3
 
 
-def early_kernel(fine_ref, number_ref, table_ref, route_ref, step_ref, back_ref, cells_ref):
+def early_kernel(fields, fine_ref, number_ref, table_ref, after_hbm, step_ref, back_ref):
     numbers = [number_ref[:, pl.ds(x * 256, 256)] for x in range(EDGE)]
     nothing = [None, None]
     back = jnp.zeros((HOSTS, 256), F32)
-    for q in range(4):
+    for q in fields:
         planes = []
         for x in range(EDGE):
             sides = [
@@ -404,9 +443,12 @@
         rate = rate_of(numbers, nothing + half + nothing, *parts)
         done = [0.5 * (planes[x] + half[x] + rate[x]) for x in range(EDGE)]
         for x in range(EDGE):
-            step_ref[pl.ds((q * EDGE + x) * HOSTS, HOSTS)] = done[x]
+            step_ref[pl.ds(((q - fields[0]) * EDGE + x) * HOSTS, HOSTS)] = done[x]
         back = jnp.where(lane_of_q() == q, means(done, table_ref), back)
     back_ref[...] = back
+
+
+def cells_kernel(route_ref, after_hbm, cells_ref):
     lane = lax.broadcasted_iota(jnp.int32, (8, 256), 1)
     row = lax.broadcasted_iota(jnp.int32, (HOSTS, 256), 0)
     by_eight = jnp.zeros((8, 256), jnp.int32)
@@ -439,19 +481,21 @@
             if interp[i, j] != 0.0:
                 total = plus(total, float(interp[i, j]) * coarse[j])
         (inner if 2 <= i < EDGE + 2 else outer).append(total)
-    sides = dot(jnp.concatenate(split(jnp.concatenate(inner, axis=0)), axis=1), table_ref[GHOST])
+    inner = jnp.concatenate(split(jnp.concatenate(inner, axis=0)), axis=1)
     faces = dot(jnp.concatenate(split(jnp.concatenate(outer, axis=0)), axis=1), table_ref[FACE])
-    return sides[:, :256], sides[:, 256:], [plane(faces, i) for i in range(4)]
+    return inner, [plane(faces, i) for i in range(4)]
 
 
 def ghost_part(block_ref, numbers, q, table_ref):
-    laplace, advect, faces = ghosts(block_ref, q, 0, table_ref)
-    half = rate_of(numbers, faces[:2] + [None] * EDGE + faces[2:], laplace, advect)
-    laplace, advect, faces = ghosts(block_ref, q, 1, table_ref)
-    parts = plane_parts(jnp.concatenate(half, axis=0), table_ref)
-    rate = rate_of(
-        numbers, faces[:2] + half + faces[2:], parts[0] + laplace, parts[1] + advect
-    )
+    inner, faces = ghosts(block_ref, q, 0, table_ref)
+    both = dot(inner, table_ref[GHOST])
+    half = rate_of(
+        numbers, faces[:2] + [None] * EDGE + faces[2:], both[:, :256], both[:, 256:]
+    )
+    inner, faces = ghosts(block_ref, q, 1, table_ref)
+    fields = split(jnp.concatenate(half, axis=0)) + (inner,)
+    both = dot(jnp.concatenate(fields, axis=1), table_ref[PLANES_AND_GHOST])
+    rate = rate_of(numbers, faces[:2] + half + faces[2:], both[:, :256], both[:, 256:])
     return [0.5 * (half[x] + rate[x]) for x in range(EDGE)]
 
 
@@ -459,6 +503,7 @@
     got_ref,
     sent_hbm,
     step_hbm,
+    more_hbm,
     old_hbm,
     number_hbm,
     full_ref,
@@ -478,7 +523,8 @@
         for i, (src, dst) in enumerate(
             (
                 (number_hbm, number_ref),
-                (step_hbm, step_ref),
+                (step_hbm, step_ref.at[pl.ds(0, 512)]),
+                (more_hbm, step_ref.at[pl.ds(512, 512)]),
                 (old_hbm, old_ref),
                 (sent_hbm, sent_ref),
             )
@@ -497,8 +543,8 @@
     for q in range(4):
         added = ghost_part(got_ref, numbers, q, table_ref)
         if q == 0:
-            copies[1].wait()
-            copies[2].wait()
+            for copy in copies[1:4]:
+                copy.wait()
         for x in range(EDGE):
             done = step_ref[pl.ds((q * EDGE + x) * HOSTS, HOSTS)] + added[x]
             for side in range(2):
@@ -506,9 +552,9 @@
                 fine_ref[at] = jnp.where(
                     placed, done[:, side * 128 : side * 128 + 128], old_ref[at]
                 )
-    out = pltpu.make_async_copy(fine_ref, fine_hbm, sems.at[4])
+    out = pltpu.make_async_copy(fine_ref, fine_hbm, sems.at[5])
     out.start()
-    copies[3].wait()
+    copies[4].wait()
     numbers = [got(NUMBER_ROW + 2 * x) for x in range(EDGE)]
     back = jnp.zeros((HOSTS, 256), F32)
     for q in range(4):
@@ -542,40 +588,56 @@
     fine_rows = fine_state.reshape(HOSTS, 4, 32, 128).transpose(0, 2, 1, 3).reshape(2048, 128)
     fine_numbers = fine_diffusion.reshape(HOSTS, EDGE**3)
 
-    def exchange(low, high, axis, up_first):
+    def swap(inner, outer, axis):
         count = lax.axis_size(axis)
-        up = [(i, i + 1) for i in range(count - 1)]
-        down = [(i + 1, i) for i in range(count - 1)]
-        if up_first:
-            from_below = lax.ppermute(high, axis, up)
-            return from_below, lax.ppermute(low, axis, down)
-        from_above = lax.ppermute(low, axis, down)
-        return lax.ppermute(high, axis, up), from_above
-
-    fields = jnp.concatenate([coarse_state, diffusion_number[None]], axis=0)
-    first, last = fields[:, :4], fields[:, 4:]
-    own = (first, last) + exchange(first, last, "gx", True)
-    low, high = call(y_kernel, own, [((320, 128), F32)] * 2, name="y_messages")
-    below, above = exchange(low, high, "gy", True)
+        pairs = [[], []]
+        for i in range(count - 1):
+            pairs[i % 2] += [(i, i + 1), (i + 1, i)]
+        return lax.ppermute(inner, axis, pairs[1]), lax.ppermute(outer, axis, pairs[0])
+
+    inner, outer = call(
+        x_kernel,
+        (coarse_state, diffusion_number),
+        [((5, 4, 8, 128), F32)] * 2,
+        hbm=(0, 1),
+        scratch=[pltpu.SemaphoreType.DMA((4,))],
+        name="x_messages",
+    )
+    own = (inner, outer) + swap(inner, outer, "gx")
+
+    def early(fields, after):
+        return call(
+            functools.partial(early_kernel, fields),
+            (fine_rows, fine_numbers, table, after),
+            [((len(fields) * 256, 256), F32), ((HOSTS, 256), F32)],
+            hbm=(3,),
+            flops=10**9,
+            name="fine_early",
+        )
+
+    step, back = early((0, 1), own[2])
+    low, high = call(y_kernel, own + (back,), [((320, 128), F32)] * 2, hbm=(4,), name="y_messages")
+    more_step, more_back = early((2, 3), low)
     everything, low, high = call(
         z_kernel,
-        own + (below, above),
+        own + swap(low, high, "gy") + (more_back,),
         [((1280, 128), F32), ((40, 128), F32), ((40, 128), F32)],
+        hbm=(6,),
         name="z_messages",
     )
-    before, after = exchange(low, high, "gz", False)
-    step, early_means, cells = call(
-        early_kernel,
-        (fine_rows, fine_numbers, table, route_cell.reshape(HOSTS)),
-        [((1024, 256), F32), ((HOSTS, 256), F32), ((32, 256), jnp.int32)],
-        smem=(3,),
-        flops=10**9,
-        name="fine_early",
+    far_low, far_high = swap(low, high, "gz")
+    (cells,) = call(
+        cells_kernel,
+        (route_cell.reshape(HOSTS), everything),
+        [((32, 256), jnp.int32)],
+        smem=(0,),
+        hbm=(1,),
+        name="cells",
     )
     payload = (HOSTS * SLOT_ROWS, 128)
     sent, full = call(
         half_kernel,
-        (everything, before, after, cells, fine_numbers, early_means),
+        (everything, far_low, far_high, cells, fine_numbers, back, more_back),
         [(payload, F32), ((4, 8, 8, 128), F32)],
         hbm_outs=(0,),
         scratch=[
@@ -592,9 +654,9 @@
     ).reshape(payload)
     fine_done, coarse_next = call(
         last_kernel,
-        (got, sent, step, fine_rows, fine_numbers, full, cells, table),
+        (got, sent, step, more_step, fine_rows, fine_numbers, full, cells, table),
         [((2048, 128), F32), ((4, 8, 8, 128), F32)],
-        hbm=(1, 2, 3, 4),
+        hbm=(1, 2, 3, 4, 5),
         hbm_outs=(0,),
         scratch=[
             pltpu.VMEM(payload, F32),
@@ -602,7 +664,7 @@
             pltpu.VMEM((2048, 128), F32),
             pltpu.VMEM((HOSTS, 4096), F32),
             pltpu.VMEM((2048, 128), F32),
-            pltpu.SemaphoreType.DMA((5,)),
+            pltpu.SemaphoreType.DMA((6,)),
         ],
         flops=10**9,
         name="last_step",

time: 81.1 us -> 77.6 us (0.957)
  blocking collectives: 38.3 us -> 34 us
  waiting for transfers between devices: 7.85 us -> 3.83 us
  starting transfers between devices: 16 us -> 19.7 us
  local copies, waits for them, and re-layouts: 1.87 us -> 5.16 us
  Pallas kernels: 14.8 us -> 13.6 us
  other arithmetic: 1.01 us -> 0 us
    all_to_all x1, blocking collectives: 38.3 us -> 34 us  [shards(): lax.all_to_all(sent.reshape(HOSTS, SLOT_ROWS, 1, 128), 'gz', split_axis=0...]
    ppermute x6, waiting for transfers between devices: 7.85 us -> 3.83 us  [the longest x3 2.69 us: swap(): lax.ppermute(inner, axis, pairs[1])]
    ppermute x6, starting transfers between devices: 16 us -> 19.7 us  [the longest x3 15.9 us: swap(): lax.ppermute(outer, axis, pairs[0])]
    unnamed x10 -> x16, local copies, waits for them, and re-layouts: 1.87 us -> 5.16 us
    pallas_call x5 -> x8, Pallas kernels: 14.8 us -> 13.6 us  [call(): pl.pallas_call(kernel, out_shape=tuple((jax.ShapeDtypeStruct(shape, dtype...]
    concatenate x1 -> x0, other arithmetic: 1.01 us -> none  [shards(): fields = jnp.concatenate([coarse_state, diffusion_number[None]], axis=0)]
  transfers between devices with their start and end apart: 6 -> 6, of which waited for: 4 -> 2; matrix products, arithmetic and copies ran while one was open for 0% -> 0% of each run, Pallas kernels for 6% -> 5%
where the time goes in v3:
time: 77.6 us; the launch traced here: 77.2 us
  blocking collectives  34 us (44%)
  starting transfers between devices  19.7 us (25%)
  Pallas kernels  13.6 us (18%)
  local copies, waits for them, and re-layouts  5.16 us (7%)
  waiting for transfers between devices  3.83 us (5%)
  between operations  0.82 us (1%)
    all_to_all x1, blocking collectives, shards(): lax.all_to_all(sent.reshape(HOSTS, SLOT_ROWS, 1, 128), 'gz', split_axis=0...  34 us
    ppermute x3, starting transfers between devices, swap(): lax.ppermute(outer, axis, pairs[0])  15.9 us
    pallas_call x8, Pallas kernels, call(): pl.pallas_call(kernel, out_shape=tuple((jax.ShapeDtypeStruct(shape, dtype...  13.6 us
    unnamed x16, local copies, waits for them, and re-layouts  5.16 us
    ppermute x3, starting transfers between devices, swap(): lax.ppermute(inner, axis, pairs[1])  3.79 us
    ppermute x3, waiting for transfers between devices, swap(): lax.ppermute(inner, axis, pairs[1])  2.69 us
  transfers between devices with their start and end apart: 6, of which 2 were waited for; matrix products, arithmetic and copies ran while one was open for 0% of the time, Pallas kernels for 5%

profile of v3, /device:TPU:16, one launch (start us, length us, event | category | flops | bytes accessed | tf_op | source)
XLA Modules:
  0.0 77.2 jit_solution(12513624245834376530)
XLA Ops:
  0.6 0.0 copy-start.5
  0.6 0.9 %copy-done.5 = f32[4,8,8,128]{3,2,1,0:T(8,128)S(1)} copy-done((f32[4,8,8,128]{3,2,1,0:T(8,128)S(1)}, f32[4,8,8,128]{3,2,1,0:T(8,128)}, u32[]{:S(2)}) %copy-start.5) | copy-done | bytes 131096
  1.5 0.0 copy-start.6
  1.5 0.8 copy-done.6
  2.3 0.1 x_messages.1
  2.4 0.7 collective-permute-start
  3.1 6.1 %collective-permute-start.1 = (f32[5,4,8,128]{3,2,1,0:T(8,128)S(1)}, f32[5,4,8,128]{3,2,1,0:T(8,128)S(1)}, u32[]{:S(2)}, u32[]{:S(2)}) collective-permute-start(f32[5,4,8,128]{3,2,1,0:T(8,128)S(1)} %get-tuple-element.18.outer_ref), channel_id=1, source_target_pairs={{0,128},{128,0},{256,384},{384,256},{1,129},{129,1},{257,385},{385... | collective-permute-start | bytes 245768 | tf_op jit(solution)/shard_map/ppermute | solution.py:596
  9.2 0.0 collective-permute-done.after_hbm.far_inner_ref
  9.2 0.0 copy-start
  9.3 1.3 %copy-done = bf16[1280,512]{1,0:T(8,128)(2,1)S(1)} copy-done((bf16[1280,512]{1,0:T(8,128)(2,1)S(1)}, bf16[1280,512]{1,0:T(8,128)(2,1)}, u32[]{:S(2)}) %copy-start) | copy-done | bytes 1310744
  10.6 0.0 copy-start.2
  10.6 1.2 %copy-done.2 = f32[1,1,1,16,4,4096]{5,4,3,2,1,0:T(4,128)S(1)} copy-done((f32[1,1,1,16,4,4096]{5,4,3,2,1,0:T(4,128)S(1)}, f32[1,1,1,16,4,4096]{5,4,3,2,1,0:T(4,128)}, u32[]{:S(2)}) %copy-start.2) | copy-done | bytes 1048600
  11.8 0.0 copy-start.4
  11.8 0.9 %copy-done.4 = f32[1,1,1,16,4096]{4,3,2,1,0:T(8,128)S(1)} copy-done((f32[1,1,1,16,4096]{4,3,2,1,0:T(8,128)S(1)}, f32[1,1,1,16,4096]{4,3,2,1,0:T(8,128)}, u32[]{:S(2)}) %copy-start.4) | copy-done | bytes 262168
  12.7 0.0 copy-start.3
  12.7 1.4 %fine_early.2 = (f32[512,256]{1,0:T(8,128)S(1)}, f32[16,256]{1,0:T(8,128)S(1)}) custom-call(f32[2048,128]{1,0:T(8,128)S(1)} %bitcast.16, f32[16,4096]{1,0:T(8,128)S(1)} %bitcast.19, bf16[1280,512]{1,0:T(8,128)(2,1)S(1)} %copy-done, f32[5,4,8,128]{3,2,1,0:T(8,128)S(1)} %collective-permute-done.after_hbm.far_inner_ref), custom_call_target="tpu_custom_call" | custom-call | flops 1000000000 | bytes 2703360 | tf_op jit(solution)/shard_map/fine_early/pallas_call | solution.py:572
  14.2 0.0 collective-permute-done.1.far_outer_ref
  14.2 0.1 y_messages.1
  14.3 1.9 %collective-permute-start.3 = (f32[320,128]{1,0:T(8,128)S(1)}, f32[320,128]{1,0:T(8,128)S(1)}, u32[]{:S(2)}, u32[]{:S(2)}) collective-permute-start(f32[320,128]{1,0:T(8,128)S(1)} %get-tuple-element.21), channel_id=1, source_target_pairs={{0,16},{16,0},{32,48},{48,32},{64,80},{80,64},{96,112},{112,96},{1... | collective-permute-start | bytes 491528 | tf_op jit(solution)/shard_map/ppermute | solution.py:596
  16.2 0.0 copy-start.7
  16.2 2.5 %collective-permute-start.2 = (f32[320,128]{1,0:T(8,128)S(1)}, f32[320,128]{1,0:T(8,128)S(1)}, u32[]{:S(2)}, u32[]{:S(2)}) collective-permute-start(f32[320,128]{1,0:T(8,128)S(1)} %get-tuple-element.20.after_hbm), channel_id=1, source_target_pairs={{16,32},{32,16},{48,64},{64,48},{80,96},{96,80},{17,33},{33,17},{4... | collective-permute-start | bytes 491528 | tf_op jit(solution)/shard_map/ppermute | solution.py:596
  18.7 0.0 copy-done.3
  18.7 1.5 %fine_early.3 = (f32[512,256]{1,0:T(8,128)S(1)}, f32[16,256]{1,0:T(8,128)S(1)}) custom-call(f32[2048,128]{1,0:T(8,128)S(1)} %bitcast.17, f32[16,4096]{1,0:T(8,128)S(1)} %bitcast.20, bf16[1280,512]{1,0:T(8,128)(2,1)S(1)} %copy-done, f32[320,128]{1,0:T(8,128)S(1)} %get-tuple-element.20.after_hbm), custom_call_target="tpu_custom_call" | custom-call | flops 1000000000 | bytes 2785280 | tf_op jit(solution)/shard_map/fine_early/pallas_call | solution.py:572
  20.2 0.0 collective-permute-done.3.far_high_ref
  20.2 2.7 %collective-permute-done.2.far_low_ref = f32[320,128]{1,0:T(8,128)S(1)} collective-permute-done((f32[320,128]{1,0:T(8,128)S(1)}, f32[320,128]{1,0:T(8,128)S(1)}, u32[]{:S(2)}, u32[]{:S(2)}) %collective-permute-start.2) | collective-permute-done | bytes 163872 | tf_op jit(solution)/shard_map/ppermute | solution.py:596
  22.9 0.4 z_messages.1
  23.3 0.7 collective-permute-start.4
  23.9 7.9 %collective-permute-start.5 = (f32[40,128]{1,0:T(8,128)S(1)}, f32[40,128]{1,0:T(8,128)S(1)}, u32[]{:S(2)}, u32[]{:S(2)}) collective-permute-start(f32[40,128]{1,0:T(8,128)S(1)} %get-tuple-element.25), channel_id=1, source_target_pairs={{0,1},{1,0},{2,3},{3,2},{4,5},{5,4},{6,7},{7,6},{8,9},{9,8},{10,11... | collective-permute-start | bytes 61448 | tf_op jit(solution)/shard_map/ppermute | solution.py:596
  31.8 0.0 copy-done.7
  31.9 0.0 copy-start.1
  31.9 0.6 cells.1.cells_ref
  32.4 0.0 collective-permute-done.4.far_low_ref
  32.5 1.1 %collective-permute-done.5.far_high_ref = f32[40,128]{1,0:T(8,128)S(1)} collective-permute-done((f32[40,128]{1,0:T(8,128)S(1)}, f32[40,128]{1,0:T(8,128)S(1)}, u32[]{:S(2)}, u32[]{:S(2)}) %collective-permute-start.5) | collective-permute-done | bytes 20512 | tf_op jit(solution)/shard_map/ppermute | solution.py:596
  33.6 2.6 %half_step.1 = (f32[1072,128]{1,0:T(8,128)S(1)}, f32[4,8,8,128]{3,2,1,0:T(8,128)S(1)}) custom-call(f32[1280,128]{1,0:T(8,128)S(1)} %get-tuple-element.23.after_hbm.all_ref, f32[40,128]{1,0:T(8,128)S(1)} %collective-permute-done.4.far_low_ref, f32[40,128]{1,0:T(8,128)S(1)} %collective-permute-done.5.far_high_ref, s32[32,256]{1,0:T(8,128)S(1)} %cells.1.cells_ref, ...), custom_call_target="tpu_custom_call" | custom-call | flops 1000000 | bytes 1024000 | tf_op jit(solution)/shard_map/half_step/pallas_call | solution.py:572
  36.2 34.0 %all_to_all.5 = f32[16,67,1,128]{3,2,1,0:T(1,128)S(1)} all-to-all(f32[16,67,1,128]{3,2,1,0:T(1,128)S(1)} %bitcast.14), channel_id=1, replica_groups=mesh['gx'=4,'gy'=8,'gz'=16] {'gz'}, dimensions={0} | all-to-all | bytes 1097728 | tf_op jit(solution)/shard_map/all_to_all | solution.py:652
  70.2 0.0 copy-done.1
  70.2 6.9 %last_step.1 = (f32[2048,128]{1,0:T(8,128)}, f32[4,8,8,128]{3,2,1,0:T(8,128)}) custom-call(f32[1072,128]{1,0:T(8,128)S(1)} %bitcast.15, f32[1072,128]{1,0:T(8,128)S(1)} %get-tuple-element.26.sent_hbm, f32[512,256]{1,0:T(8,128)S(1)} %get-tuple-element.27.step_hbm, f32[512,256]{1,0:T(8,128)S(1)} %get-tuple-element.28.more_hbm, f32[2048,128]{1,0:T(8,128)S(1)} %bitcast.18, ...), custom_call_target="tpu_custom_call" | custom-call | flops 1000000000 | bytes 4931584 | tf_op jit(solution)/shard_map/last_step/pallas_call | solution.py:572
Async XLA Ops:
  0.6 0.9 %copy-start.5 = (f32[4,8,8,128]{3,2,1,0:T(8,128)S(1)}, f32[4,8,8,128]{3,2,1,0:T(8,128)}, u32[]{:S(2)}) copy-start(f32[4,8,8,128]{3,2,1,0:T(8,128)} %coarse_hbm.1) | copy-start | bytes 393220
  1.5 0.8 copy-start.6
  2.4 6.8 %collective-permute-start = (f32[5,4,8,128]{3,2,1,0:T(8,128)S(1)}, f32[5,4,8,128]{3,2,1,0:T(8,128)S(1)}, u32[]{:S(2)}, u32[]{:S(2)}) collective-permute-start(f32[5,4,8,128]{3,2,1,0:T(8,128)S(1)} %get-tuple-element.17.inner_ref), channel_id=1, source_target_pairs={{128,256},{256,128},{129,257},{257,129},{130,258},{258,130},{131,2... | collective-permute-start | bytes 245768 | tf_op jit(solution)/shard_map/ppermute | solution.py:596
  3.1 11.1 %collective-permute-start.1 = (f32[5,4,8,128]{3,2,1,0:T(8,128)S(1)}, f32[5,4,8,128]{3,2,1,0:T(8,128)S(1)}, u32[]{:S(2)}, u32[]{:S(2)}) collective-permute-start(f32[5,4,8,128]{3,2,1,0:T(8,128)S(1)} %get-tuple-element.18.outer_ref), channel_id=1, source_target_pairs={{0,128},{128,0},{256,384},{384,256},{1,129},{129,1},{257,385},{385... | collective-permute-start | bytes 245768 | tf_op jit(solution)/shard_map/ppermute | solution.py:596
  9.2 1.3 %copy-start = (bf16[1280,512]{1,0:T(8,128)(2,1)S(1)}, bf16[1280,512]{1,0:T(8,128)(2,1)}, u32[]{:S(2)}) copy-start(bf16[1280,512]{1,0:T(8,128)(2,1)} %constant.2.clone.table_ref) | copy-start | bytes 3932164
  10.6 1.2 %copy-start.2 = (f32[1,1,1,16,4,4096]{5,4,3,2,1,0:T(4,128)S(1)}, f32[1,1,1,16,4,4096]{5,4,3,2,1,0:T(4,128)}, u32[]{:S(2)}) copy-start(f32[1,1,1,16,4,4096]{5,4,3,2,1,0:T(4,128)} %param.9) | copy-start | bytes 3145732
  11.8 0.9 %copy-start.4 = (f32[1,1,1,16,4096]{4,3,2,1,0:T(8,128)S(1)}, f32[1,1,1,16,4096]{4,3,2,1,0:T(8,128)}, u32[]{:S(2)}) copy-start(f32[1,1,1,16,4096]{4,3,2,1,0:T(8,128)} %param.10) | copy-start | bytes 786436
  12.7 6.0 %copy-start.3 = (f32[1,1,1,16,4,4096]{5,4,3,2,1,0:T(4,128)S(1)}, f32[1,1,1,16,4,4096]{5,4,3,2,1,0:T(4,128)}, u32[]{:S(2)}) copy-start(f32[1,1,1,16,4,4096]{5,4,3,2,1,0:T(4,128)} %param.9) | copy-start | bytes 3145732
  14.3 5.9 %collective-permute-start.3 = (f32[320,128]{1,0:T(8,128)S(1)}, f32[320,128]{1,0:T(8,128)S(1)}, u32[]{:S(2)}, u32[]{:S(2)}) collective-permute-start(f32[320,128]{1,0:T(8,128)S(1)} %get-tuple-element.21), channel_id=1, source_target_pairs={{0,16},{16,0},{32,48},{48,32},{64,80},{80,64},{96,112},{112,96},{1... | collective-permute-start | bytes 491528 | tf_op jit(solution)/shard_map/ppermute | solution.py:596
  16.2 15.6 %copy-start.7 = (s32[1,1,1,16]{3,2,1,0:T(1,128)S(1)}, s32[1,1,1,16]{3,2,1,0:T(1,128)}, u32[]{:S(2)}) copy-start(s32[1,1,1,16]{3,2,1,0:T(1,128)} %param.8) | copy-start | bytes 196
  16.2 6.6 %collective-permute-start.2 = (f32[320,128]{1,0:T(8,128)S(1)}, f32[320,128]{1,0:T(8,128)S(1)}, u32[]{:S(2)}, u32[]{:S(2)}) collective-permute-start(f32[320,128]{1,0:T(8,128)S(1)} %get-tuple-element.20.after_hbm), channel_id=1, source_target_pairs={{16,32},{32,16},{48,64},{64,48},{80,96},{96,80},{17,33},{33,17},{4... | collective-permute-start | bytes 491528 | tf_op jit(solution)/shard_map/ppermute | solution.py:596
  23.3 9.2 %collective-permute-start.4 = (f32[40,128]{1,0:T(8,128)S(1)}, f32[40,128]{1,0:T(8,128)S(1)}, u32[]{:S(2)}, u32[]{:S(2)}) collective-permute-start(f32[40,128]{1,0:T(8,128)S(1)} %get-tuple-element.24), channel_id=1, source_target_pairs={{1,2},{2,1},{3,4},{4,3},{5,6},{6,5},{7,8},{8,7},{9,10},{10,9},{11,... | collective-permute-start | bytes 61448 | tf_op jit(solution)/shard_map/ppermute | solution.py:596
  23.9 9.6 %collective-permute-start.5 = (f32[40,128]{1,0:T(8,128)S(1)}, f32[40,128]{1,0:T(8,128)S(1)}, u32[]{:S(2)}, u32[]{:S(2)}) collective-permute-start(f32[40,128]{1,0:T(8,128)S(1)} %get-tuple-element.25), channel_id=1, source_target_pairs={{0,1},{1,0},{2,3},{3,2},{4,5},{5,4},{6,7},{7,6},{8,9},{9,8},{10,11... | collective-permute-start | bytes 61448 | tf_op jit(solution)/shard_map/ppermute | solution.py:596
  31.9 38.4 %copy-start.1 = (bf16[1280,512]{1,0:T(8,128)(2,1)S(1)}, bf16[1280,512]{1,0:T(8,128)(2,1)}, u32[]{:S(2)}) copy-start(bf16[1280,512]{1,0:T(8,128)(2,1)} %constant.2.clone.table_ref) | copy-start | bytes 3932164

commit v4 on v3

--- a/solution.py
+++ b/solution.py
@@ -13,6 +13,7 @@
 RATIO = 4
 EDGE = PB * RATIO
 HOSTS = 16
+TOGETHER = 4
 LIMIT = 16
 NUMBER_ROW = 32
 MEAN_ROW = 64
@@ -118,19 +119,13 @@
     return lax.axis_index(axis) % 2 == 0
 
 
-def x_kernel(coarse_hbm, number_hbm, inner_ref, outer_ref, sems):
-    place = jnp.where(is_even("gx"), 4, 0)
-    copies = []
-    for i, ref in enumerate((outer_ref, inner_ref)):
-        at = pl.ds(place if i == 0 else 4 - place, 4)
-        copies.append(
-            pltpu.make_async_copy(coarse_hbm.at[:, at], ref.at[pl.ds(0, 4)], sems.at[2 * i])
-        )
-        copies.append(pltpu.make_async_copy(number_hbm.at[at], ref.at[4], sems.at[2 * i + 1]))
-    for copy in copies:
-        copy.start()
-    for copy in copies:
-        copy.wait()
+def x_kernel(first_ref, last_ref, inner_ref, outer_ref):
+    even = jnp.broadcast_to(is_even("gx"), (8, 128))
+    for q in range(5):
+        for x in range(4):
+            first, last = first_ref[q, x], last_ref[q, x]
+            inner_ref[q, x] = jnp.where(even, first, last)
+            outer_ref[q, x] = jnp.where(even, last, first)
 
 
 def ring_field(inner_ref, outer_ref, far_inner_ref, far_outer_ref, q, x):
@@ -220,7 +215,6 @@
     cells_ref,
     number_ref,
     mean_ref,
-    more_ref,
     sent_ref,
     full_ref,
     now_ref,
@@ -297,9 +291,9 @@
             :, pl.ds(column * 128, 128)
         ]
     for side in range(2):
-        pay_ref[pl.ds(MEAN_ROW + side, HOSTS, stride=SLOT_ROWS)] = (
-            mean_ref[:, pl.ds(side * 128, 128)] + more_ref[:, pl.ds(side * 128, 128)]
-        )
+        pay_ref[pl.ds(MEAN_ROW + side, HOSTS, stride=SLOT_ROWS)] = mean_ref[
+            :, pl.ds(side * 128, 128)
+        ]
     placed = cells_ref[pl.ds(16, HOSTS), pl.ds(0, 128)] >= 0
     pay_ref[pl.ds(FLAG_ROW, HOSTS, stride=SLOT_ROWS)] = jnp.where(placed, 1.0, 0.0)
     copy = pltpu.make_async_copy(pay_ref, sent_ref, sem)
@@ -423,6 +417,14 @@
 
 def lane_of_q():
     return (lax.broadcasted_iota(jnp.int32, (HOSTS, 256), 1) >> 4) & 3
+
+
+def touch_kernel(fine_ref, number_ref, table_ref, after_hbm, out_ref):
+    out_ref[...] = (
+        fine_ref[pl.ds(0, 8)]
+        + number_ref[pl.ds(0, 8), pl.ds(0, 128)]
+        + table_ref[pl.ds(0, 16), pl.ds(0, 128)].astype(F32)[:8]
+    )
 
 
 def early_kernel(fields, fine_ref, number_ref, table_ref, after_hbm, step_ref, back_ref):
@@ -464,7 +466,7 @@
     cells_ref[pl.ds(16, HOSTS)] = by_row
 
 
-def ghosts(block_ref, q, t, table_ref):
+def ghosts(block_ref, q, t):
     interp = interp_table(PB, RATIO)
     first_half = lax.broadcasted_iota(jnp.int32, (HOSTS, 128), 1) < 64
     coarse = []
@@ -482,28 +484,42 @@
                 total = plus(total, float(interp[i, j]) * coarse[j])
         (inner if 2 <= i < EDGE + 2 else outer).append(total)
     inner = jnp.concatenate(split(jnp.concatenate(inner, axis=0)), axis=1)
-    faces = dot(jnp.concatenate(split(jnp.concatenate(outer, axis=0)), axis=1), table_ref[FACE])
-    return inner, [plane(faces, i) for i in range(4)]
-
-
-def ghost_part(block_ref, numbers, q, table_ref):
-    inner, faces = ghosts(block_ref, q, 0, table_ref)
-    both = dot(inner, table_ref[GHOST])
-    half = rate_of(
-        numbers, faces[:2] + [None] * EDGE + faces[2:], both[:, :256], both[:, 256:]
-    )
-    inner, faces = ghosts(block_ref, q, 1, table_ref)
-    fields = split(jnp.concatenate(half, axis=0)) + (inner,)
-    both = dot(jnp.concatenate(fields, axis=1), table_ref[PLANES_AND_GHOST])
-    rate = rate_of(numbers, faces[:2] + half + faces[2:], both[:, :256], both[:, 256:])
-    return [0.5 * (half[x] + rate[x]) for x in range(EDGE)]
+    outer = jnp.concatenate(split(jnp.concatenate(outer, axis=0)), axis=1)
+    return inner, outer
+
+
+def ghost_part(block_ref, numbers, fields, table_ref):
+    def planes_of(t):
+        parts = [ghosts(block_ref, q, t) for q in fields]
+        inner, outer = (jnp.concatenate(part, axis=0) for part in zip(*parts))
+        return inner, dot(outer, table_ref[FACE])
+
+    def rates(values, faces, both):
+        result = []
+        for i in range(len(fields)):
+            low = [plane(faces, i * 4 + j) for j in range(2)]
+            high = [plane(faces, i * 4 + j) for j in range(2, 4)]
+            rows = both[i * 256 : (i + 1) * 256]
+            result.append(
+                rate_of(numbers, low + values[i] + high, rows[:, :256], rows[:, 256:])
+            )
+        return result
+
+    inner, faces = planes_of(0)
+    half = rates([[None] * EDGE for _ in fields], faces, dot(inner, table_ref[GHOST]))
+    inner, faces = planes_of(1)
+    stacked = jnp.concatenate([values for field in half for values in field], axis=0)
+    operand = jnp.concatenate(split(stacked) + (inner,), axis=1)
+    rate = rates(half, faces, dot(operand, table_ref[PLANES_AND_GHOST]))
+    return [
+        [0.5 * (half[i][x] + rate[i][x]) for x in range(EDGE)] for i in range(len(fields))
+    ]
 
 
 def last_kernel(
     got_ref,
     sent_hbm,
     step_hbm,
-    more_hbm,
     old_hbm,
     number_hbm,
     full_ref,
@@ -523,8 +539,7 @@
         for i, (src, dst) in enumerate(
             (
                 (number_hbm, number_ref),
-                (step_hbm, step_ref.at[pl.ds(0, 512)]),
-                (more_hbm, step_ref.at[pl.ds(512, 512)]),
+                (step_hbm, step_ref),
                 (old_hbm, old_ref),
                 (sent_hbm, sent_ref),
             )
@@ -540,26 +555,30 @@
     placed = got_ref[pl.ds(FLAG_ROW, HOSTS, stride=SLOT_ROWS)] > 0.5
     copies[0].wait()
     numbers = [number_ref[:, pl.ds(x * 256, 256)] for x in range(EDGE)]
+    added = []
     for q in range(4):
-        added = ghost_part(got_ref, numbers, q, table_ref)
+        if q % TOGETHER == 0:
+            added += ghost_part(got_ref, numbers, range(q, q + TOGETHER), table_ref)
         if q == 0:
-            for copy in copies[1:4]:
+            for copy in copies[1:3]:
                 copy.wait()
         for x in range(EDGE):
-            done = step_ref[pl.ds((q * EDGE + x) * HOSTS, HOSTS)] + added[x]
+            done = step_ref[pl.ds((q * EDGE + x) * HOSTS, HOSTS)] + added[q][x]
             for side in range(2):
                 at = pl.ds((2 * x + side) * 4 + q, HOSTS, stride=128)
                 fine_ref[at] = jnp.where(
                     placed, done[:, side * 128 : side * 128 + 128], old_ref[at]
                 )
-    out = pltpu.make_async_copy(fine_ref, fine_hbm, sems.at[5])
+    out = pltpu.make_async_copy(fine_ref, fine_hbm, sems.at[4])
     out.start()
-    copies[4].wait()
+    copies[3].wait()
     numbers = [got(NUMBER_ROW + 2 * x) for x in range(EDGE)]
+    added = []
     back = jnp.zeros((HOSTS, 256), F32)
     for q in range(4):
-        added = ghost_part(sent_ref, numbers, q, table_ref)
-        back = jnp.where(lane_of_q() == q, means(added, table_ref), back)
+        if q % TOGETHER == 0:
+            added += ghost_part(sent_ref, numbers, range(q, q + TOGETHER), table_ref)
+        back = jnp.where(lane_of_q() == q, means(added[q], table_ref), back)
     put_means(back + got(MEAN_ROW), full_ref, cells_ref, table_ref, next_ref)
     out.wait()
 
@@ -595,12 +614,11 @@
             pairs[i % 2] += [(i, i + 1), (i + 1, i)]
         return lax.ppermute(inner, axis, pairs[1]), lax.ppermute(outer, axis, pairs[0])
 
+    fields = jnp.concatenate([coarse_state, diffusion_number[None]], axis=0)
     inner, outer = call(
         x_kernel,
-        (coarse_state, diffusion_number),
+        (fields[:, :4], fields[:, 4:]),
         [((5, 4, 8, 128), F32)] * 2,
-        hbm=(0, 1),
-        scratch=[pltpu.SemaphoreType.DMA((4,))],
         name="x_messages",
     )
     own = (inner, outer) + swap(inner, outer, "gx")
@@ -615,16 +633,24 @@
             name="fine_early",
         )
 
-    step, back = early((0, 1), own[2])
-    low, high = call(y_kernel, own + (back,), [((320, 128), F32)] * 2, hbm=(4,), name="y_messages")
-    more_step, more_back = early((2, 3), low)
+    (touched,) = call(
+        touch_kernel,
+        (fine_rows, fine_numbers, table, own[2]),
+        [((8, 128), F32)],
+        hbm=(3,),
+        name="touch",
+    )
+    low, high = call(
+        y_kernel, own + (touched,), [((320, 128), F32)] * 2, hbm=(4,), name="y_messages"
+    )
     everything, low, high = call(
         z_kernel,
-        own + swap(low, high, "gy") + (more_back,),
+        own + swap(low, high, "gy") + (touched,),
         [((1280, 128), F32), ((40, 128), F32), ((40, 128), F32)],
         hbm=(6,),
         name="z_messages",
     )
+    step, back = early((0, 1, 2, 3), everything)
     far_low, far_high = swap(low, high, "gz")
     (cells,) = call(
         cells_kernel,
@@ -637,7 +663,7 @@
     payload = (HOSTS * SLOT_ROWS, 128)
     sent, full = call(
         half_kernel,
-        (everything, far_low, far_high, cells, fine_numbers, back, more_back),
+        (everything, far_low, far_high, cells, fine_numbers, back),
         [(payload, F32), ((4, 8, 8, 128), F32)],
         hbm_outs=(0,),
         scratch=[
@@ -654,9 +680,9 @@
     ).reshape(payload)
     fine_done, coarse_next = call(
         last_kernel,
-        (got, sent, step, more_step, fine_rows, fine_numbers, full, cells, table),
+        (got, sent, step, fine_rows, fine_numbers, full, cells, table),
         [((2048, 128), F32), ((4, 8, 8, 128), F32)],
-        hbm=(1, 2, 3, 4, 5),
+        hbm=(1, 2, 3, 4),
         hbm_outs=(0,),
         scratch=[
             pltpu.VMEM(payload, F32),
@@ -664,7 +690,7 @@
             pltpu.VMEM((2048, 128), F32),
             pltpu.VMEM((HOSTS, 4096), F32),
             pltpu.VMEM((2048, 128), F32),
-            pltpu.SemaphoreType.DMA((6,)),
+            pltpu.SemaphoreType.DMA((5,)),
         ],
         flops=10**9,
         name="last_step",

time: 77.6 us -> 76 us (0.979)
  waiting for transfers between devices: 3.83 us -> 1.13 us
  local copies, waits for them, and re-layouts: 5.16 us -> 3.51 us
  blocking collectives: 34 us -> 35.6 us
  starting transfers between devices: 19.7 us -> 21 us
  Pallas kernels: 13.6 us -> 12.5 us
  other arithmetic: 0 us -> 0.92 us
    ppermute x3, starting transfers between devices: 15.9 us -> 17.6 us  [swap(): lax.ppermute(outer, axis, pairs[0])]
    unnamed x16 -> x14, local copies, waits for them, and re-layouts: 5.16 us -> 3.51 us
    all_to_all x1, blocking collectives: 34 us -> 35.6 us  [shards(): lax.all_to_all(sent.reshape(HOSTS, SLOT_ROWS, 1, 128), 'gz', split_axis=0...]
    ppermute x3, waiting for transfers between devices: 2.69 us -> 1.12 us  [swap(): lax.ppermute(inner, axis, pairs[1])]
    ppermute x3, waiting for transfers between devices: 1.14 us -> 0.01 us  [swap(): lax.ppermute(outer, axis, pairs[0])]
    pallas_call x8, Pallas kernels: 13.6 us -> 12.5 us  [call(): pl.pallas_call(kernel, out_shape=tuple((jax.ShapeDtypeStruct(shape, dtype...]
    concatenate x0 -> x1, other arithmetic: none -> 0.92 us  [shards(): fields = jnp.concatenate([coarse_state, diffusion_number[None]], axis=0)]
  transfers between devices with their start and end apart: 6 -> 6, of which waited for: 2 -> 1; matrix products, arithmetic and copies ran while one was open for 0% -> 0% of each run, Pallas kernels for 5% -> 4%
where the time goes in v4:
time: 76 us; the launch traced here: 75.5 us
  blocking collectives  35.6 us (47%)
  starting transfers between devices  21 us (28%)
  Pallas kernels  12.5 us (16%)
  local copies, waits for them, and re-layouts  3.51 us (5%)
  waiting for transfers between devices  1.13 us (1%)
  other arithmetic  0.92 us (1%)
  between operations  0.82 us (1%)
    all_to_all x1, blocking collectives, shards(): lax.all_to_all(sent.reshape(HOSTS, SLOT_ROWS, 1, 128), 'gz', split_axis=0...  35.6 us
    ppermute x3, starting transfers between devices, swap(): lax.ppermute(outer, axis, pairs[0])  17.6 us
    pallas_call x8, Pallas kernels, call(): pl.pallas_call(kernel, out_shape=tuple((jax.ShapeDtypeStruct(shape, dtype...  12.5 us
    unnamed x14, local copies, waits for them, and re-layouts  3.51 us
    ppermute x3, starting transfers between devices, swap(): lax.ppermute(inner, axis, pairs[1])  3.38 us
  transfers between devices with their start and end apart: 6, of which 1 were waited for; matrix products, arithmetic and copies ran while one was open for 0% of the time, Pallas kernels for 4%

profile of v4, /device:TPU:16, one launch (start us, length us, event | category | flops | bytes accessed | tf_op | source)
XLA Modules:
  0.0 75.5 jit_solution(9090421721529881582)
XLA Ops:
  0.6 0.9 %pad_maximum_fusion = (f32[5,4,8,128]{3,2,1,0:T(8,128)S(1)}, f32[5,4,8,128]{3,2,1,0:T(8,128)S(1)}) fusion(f32[1,8,8,128]{3,2,1,0:T(8,128)} %bitcast.25, f32[4,8,8,128]{3,2,1,0:T(8,128)} %param.6), kind=kLoop, calls=%fused_computation.3 | loop fusion | flops 40960 | bytes 327680 | tf_op jit(solution)/shard_map/concatenate | solution.py:617
  1.6 0.7 collective-permute-start
  2.3 6.1 %collective-permute-start.1 = (f32[5,4,8,128]{3,2,1,0:T(8,128)S(1)}, f32[5,4,8,128]{3,2,1,0:T(8,128)S(1)}, u32[]{:S(2)}, u32[]{:S(2)}) collective-permute-start(f32[5,4,8,128]{3,2,1,0:T(8,128)S(1)} %get-tuple-element.16.outer_ref), channel_id=1, source_target_pairs={{0,128},{128,0},{256,384},{384,256},{1,129},{129,1},{257,385},{385... | collective-permute-start | bytes 245768 | tf_op jit(solution)/shard_map/ppermute | solution.py:615
  8.4 0.0 collective-permute-done.after_hbm.far_inner_ref
  8.4 0.0 copy-start
  8.4 1.3 %copy-done = bf16[1280,512]{1,0:T(8,128)(2,1)S(1)} copy-done((bf16[1280,512]{1,0:T(8,128)(2,1)S(1)}, bf16[1280,512]{1,0:T(8,128)(2,1)}, u32[]{:S(2)}) %copy-start) | copy-done | bytes 1310744
  9.7 0.0 copy-start.2
  9.7 1.2 %copy-done.2 = f32[1,1,1,16,4,4096]{5,4,3,2,1,0:T(4,128)S(1)} copy-done((f32[1,1,1,16,4,4096]{5,4,3,2,1,0:T(4,128)S(1)}, f32[1,1,1,16,4,4096]{5,4,3,2,1,0:T(4,128)}, u32[]{:S(2)}) %copy-start.2) | copy-done | bytes 1048600
  11.0 0.0 copy-start.4
  11.0 0.9 %copy-done.4 = f32[1,1,1,16,4096]{4,3,2,1,0:T(8,128)S(1)} copy-done((f32[1,1,1,16,4096]{4,3,2,1,0:T(8,128)S(1)}, f32[1,1,1,16,4096]{4,3,2,1,0:T(8,128)}, u32[]{:S(2)}) %copy-start.4) | copy-done | bytes 262168
  11.9 0.0 copy-start.1
  11.9 0.0 copy-start.3
  11.9 0.0 collective-permute-done.1.far_outer_ref
  11.9 0.1 y_messages.1
  12.0 2.1 %collective-permute-start.2 = (f32[320,128]{1,0:T(8,128)S(1)}, f32[320,128]{1,0:T(8,128)S(1)}, u32[]{:S(2)}, u32[]{:S(2)}) collective-permute-start(f32[320,128]{1,0:T(8,128)S(1)} %get-tuple-element.17), channel_id=1, source_target_pairs={{16,32},{32,16},{48,64},{64,48},{80,96},{96,80},{17,33},{33,17},{4... | collective-permute-start | bytes 491528 | tf_op jit(solution)/shard_map/ppermute | solution.py:615
  14.1 3.6 %collective-permute-start.3 = (f32[320,128]{1,0:T(8,128)S(1)}, f32[320,128]{1,0:T(8,128)S(1)}, u32[]{:S(2)}, u32[]{:S(2)}) collective-permute-start(f32[320,128]{1,0:T(8,128)S(1)} %get-tuple-element.18), channel_id=1, source_target_pairs={{0,16},{16,0},{32,48},{48,32},{64,80},{80,64},{96,112},{112,96},{1... | collective-permute-start | bytes 491528 | tf_op jit(solution)/shard_map/ppermute | solution.py:615
  17.7 1.1 %collective-permute-done.2.far_low_ref = f32[320,128]{1,0:T(8,128)S(1)} collective-permute-done((f32[320,128]{1,0:T(8,128)S(1)}, f32[320,128]{1,0:T(8,128)S(1)}, u32[]{:S(2)}, u32[]{:S(2)}) %collective-permute-start.2) | collective-permute-done | bytes 163872 | tf_op jit(solution)/shard_map/ppermute | solution.py:615
  18.8 0.0 collective-permute-done.3.far_high_ref
  18.8 0.4 z_messages.1
  19.2 0.7 collective-permute-start.4
  19.9 7.9 %collective-permute-start.5 = (f32[40,128]{1,0:T(8,128)S(1)}, f32[40,128]{1,0:T(8,128)S(1)}, u32[]{:S(2)}, u32[]{:S(2)}) collective-permute-start(f32[40,128]{1,0:T(8,128)S(1)} %get-tuple-element.21), channel_id=1, source_target_pairs={{0,1},{1,0},{2,3},{3,2},{4,5},{5,4},{6,7},{7,6},{8,9},{9,8},{10,11... | collective-permute-start | bytes 61448 | tf_op jit(solution)/shard_map/ppermute | solution.py:615
  27.8 0.0 copy-done.1
  27.8 0.0 copy-done.3
  27.8 0.0 copy-start.6
  27.8 0.0 copy-start.5
  27.8 2.8 %fine_early.1 = (f32[1024,256]{1,0:T(8,128)S(1)}, f32[16,256]{1,0:T(8,128)S(1)}) custom-call(f32[2048,128]{1,0:T(8,128)S(1)} %bitcast.16, f32[16,4096]{1,0:T(8,128)S(1)} %bitcast.19, bf16[1280,512]{1,0:T(8,128)(2,1)S(1)} %copy-done.1, f32[1280,128]{1,0:T(8,128)S(1)} %get-tuple-element.19.after_hbm.all_ref), custom_call_target="tpu_custom_call" | custom-call | flops 1000000000 | bytes 3276800 | tf_op jit(solution)/shard_map/fine_early/pallas_call | solution.py:591
  30.6 0.0 copy-done.6
  30.6 0.6 cells.1.cells_ref
  31.2 0.0 collective-permute-done.4.far_low_ref
  31.2 0.0 collective-permute-done.5.far_high_ref
  31.2 0.0 copy-done.5
  31.2 2.6 %half_step.1 = (f32[1072,128]{1,0:T(8,128)S(1)}, f32[4,8,8,128]{3,2,1,0:T(8,128)S(1)}) custom-call(f32[1280,128]{1,0:T(8,128)S(1)} %get-tuple-element.19.after_hbm.all_ref, f32[40,128]{1,0:T(8,128)S(1)} %collective-permute-done.4.far_low_ref, f32[40,128]{1,0:T(8,128)S(1)} %collective-permute-done.5.far_high_ref, s32[32,256]{1,0:T(8,128)S(1)} %cells.1.cells_ref, ...), custom_call_target="tpu_custom_call" | custom-call | flops 1000000 | bytes 1007616 | tf_op jit(solution)/shard_map/half_step/pallas_call | solution.py:591
  33.9 35.6 %all_to_all.5 = f32[16,67,1,128]{3,2,1,0:T(1,128)S(1)} all-to-all(f32[16,67,1,128]{3,2,1,0:T(1,128)S(1)} %bitcast.22), channel_id=1, replica_groups=mesh['gx'=4,'gy'=8,'gz'=16] {'gz'}, dimensions={0} | all-to-all | bytes 1097728 | tf_op jit(solution)/shard_map/all_to_all | solution.py:678
  69.5 6.0 %last_step.1 = (f32[2048,128]{1,0:T(8,128)}, f32[4,8,8,128]{3,2,1,0:T(8,128)}) custom-call(f32[1072,128]{1,0:T(8,128)S(1)} %bitcast.23, f32[1072,128]{1,0:T(8,128)S(1)} %get-tuple-element.23.sent_hbm, f32[1024,256]{1,0:T(8,128)S(1)} %get-tuple-element.24.step_hbm, f32[2048,128]{1,0:T(8,128)S(1)} %bitcast.17, f32[16,4096]{1,0:T(8,128)S(1)} %bitcast.21, ...), custom_call_target="tpu_custom_call" | custom-call | flops 1000000000 | bytes 4931584 | tf_op jit(solution)/shard_map/last_step/pallas_call | solution.py:591
  (2 shorter events, 0.0 us)
Async XLA Ops:
  1.6 6.8 %collective-permute-start = (f32[5,4,8,128]{3,2,1,0:T(8,128)S(1)}, f32[5,4,8,128]{3,2,1,0:T(8,128)S(1)}, u32[]{:S(2)}, u32[]{:S(2)}) collective-permute-start(f32[5,4,8,128]{3,2,1,0:T(8,128)S(1)} %get-tuple-element.15.inner_ref), channel_id=1, source_target_pairs={{128,256},{256,128},{129,257},{257,129},{130,258},{258,130},{131,2... | collective-permute-start | bytes 245768 | tf_op jit(solution)/shard_map/ppermute | solution.py:615
  2.3 9.7 %collective-permute-start.1 = (f32[5,4,8,128]{3,2,1,0:T(8,128)S(1)}, f32[5,4,8,128]{3,2,1,0:T(8,128)S(1)}, u32[]{:S(2)}, u32[]{:S(2)}) collective-permute-start(f32[5,4,8,128]{3,2,1,0:T(8,128)S(1)} %get-tuple-element.16.outer_ref), channel_id=1, source_target_pairs={{0,128},{128,0},{256,384},{384,256},{1,129},{129,1},{257,385},{385... | collective-permute-start | bytes 245768 | tf_op jit(solution)/shard_map/ppermute | solution.py:615
  8.4 1.3 %copy-start = (bf16[1280,512]{1,0:T(8,128)(2,1)S(1)}, bf16[1280,512]{1,0:T(8,128)(2,1)}, u32[]{:S(2)}) copy-start(bf16[1280,512]{1,0:T(8,128)(2,1)} %constant.2.clone.table_ref) | copy-start | bytes 3932164
  9.7 1.2 %copy-start.2 = (f32[1,1,1,16,4,4096]{5,4,3,2,1,0:T(4,128)S(1)}, f32[1,1,1,16,4,4096]{5,4,3,2,1,0:T(4,128)}, u32[]{:S(2)}) copy-start(f32[1,1,1,16,4,4096]{5,4,3,2,1,0:T(4,128)} %param.9) | copy-start | bytes 3145732
  11.0 0.9 %copy-start.4 = (f32[1,1,1,16,4096]{4,3,2,1,0:T(8,128)S(1)}, f32[1,1,1,16,4096]{4,3,2,1,0:T(8,128)}, u32[]{:S(2)}) copy-start(f32[1,1,1,16,4096]{4,3,2,1,0:T(8,128)} %param.10) | copy-start | bytes 786436
  11.9 15.9 %copy-start.1 = (bf16[1280,512]{1,0:T(8,128)(2,1)S(1)}, bf16[1280,512]{1,0:T(8,128)(2,1)}, u32[]{:S(2)}) copy-start(bf16[1280,512]{1,0:T(8,128)(2,1)} %constant.2.clone.table_ref) | copy-start | bytes 3932164
  11.9 15.9 %copy-start.3 = (f32[1,1,1,16,4,4096]{5,4,3,2,1,0:T(4,128)S(1)}, f32[1,1,1,16,4,4096]{5,4,3,2,1,0:T(4,128)}, u32[]{:S(2)}) copy-start(f32[1,1,1,16,4,4096]{5,4,3,2,1,0:T(4,128)} %param.9) | copy-start | bytes 3145732
  12.0 6.8 %collective-permute-start.2 = (f32[320,128]{1,0:T(8,128)S(1)}, f32[320,128]{1,0:T(8,128)S(1)}, u32[]{:S(2)}, u32[]{:S(2)}) collective-permute-start(f32[320,128]{1,0:T(8,128)S(1)} %get-tuple-element.17), channel_id=1, source_target_pairs={{16,32},{32,16},{48,64},{64,48},{80,96},{96,80},{17,33},{33,17},{4... | collective-permute-start | bytes 491528 | tf_op jit(solution)/shard_map/ppermute | solution.py:615
  14.1 4.7 %collective-permute-start.3 = (f32[320,128]{1,0:T(8,128)S(1)}, f32[320,128]{1,0:T(8,128)S(1)}, u32[]{:S(2)}, u32[]{:S(2)}) collective-permute-start(f32[320,128]{1,0:T(8,128)S(1)} %get-tuple-element.18), channel_id=1, source_target_pairs={{0,16},{16,0},{32,48},{48,32},{64,80},{80,64},{96,112},{112,96},{1... | collective-permute-start | bytes 491528 | tf_op jit(solution)/shard_map/ppermute | solution.py:615
  19.2 12.0 %collective-permute-start.4 = (f32[40,128]{1,0:T(8,128)S(1)}, f32[40,128]{1,0:T(8,128)S(1)}, u32[]{:S(2)}, u32[]{:S(2)}) collective-permute-start(f32[40,128]{1,0:T(8,128)S(1)} %get-tuple-element.20), channel_id=1, source_target_pairs={{1,2},{2,1},{3,4},{4,3},{5,6},{6,5},{7,8},{8,7},{9,10},{10,9},{11,... | collective-permute-start | bytes 61448 | tf_op jit(solution)/shard_map/ppermute | solution.py:615
  19.9 11.4 %collective-permute-start.5 = (f32[40,128]{1,0:T(8,128)S(1)}, f32[40,128]{1,0:T(8,128)S(1)}, u32[]{:S(2)}, u32[]{:S(2)}) collective-permute-start(f32[40,128]{1,0:T(8,128)S(1)} %get-tuple-element.21), channel_id=1, source_target_pairs={{0,1},{1,0},{2,3},{3,2},{4,5},{5,4},{6,7},{7,6},{8,9},{9,8},{10,11... | collective-permute-start | bytes 61448 | tf_op jit(solution)/shard_map/ppermute | solution.py:615
  27.8 2.8 %copy-start.6 = (s32[1,1,1,16]{3,2,1,0:T(1,128)S(1)}, s32[1,1,1,16]{3,2,1,0:T(1,128)}, u32[]{:S(2)}) copy-start(s32[1,1,1,16]{3,2,1,0:T(1,128)} %param.8) | copy-start | bytes 196
  27.8 3.4 %copy-start.5 = (f32[1,1,1,16,4096]{4,3,2,1,0:T(8,128)S(1)}, f32[1,1,1,16,4096]{4,3,2,1,0:T(8,128)}, u32[]{:S(2)}) copy-start(f32[1,1,1,16,4096]{4,3,2,1,0:T(8,128)} %param.10) | copy-start | bytes 786436
